TPU v7x, 32 devices: a whole 2x2x4 slice. The times are simulated.
32 devices in a mesh: seq: 4 (over x, core), chan: 8 (over z, y).
Axes of the slice: x: 2, y: 2, z: 4, core: 2. Of those that a mesh axis runs over, the one named last changes fastest.
Arguments:
- tokens: bfloat16 [512, 8192], P('seq', 'chan'), may hold values from -6 to 6
- in_weight: bfloat16 [8192, 3, 8192], P(None, None, 'chan'), may hold values from -0.0625 to 0.0625
- long_filter: float32 [512, 8192], P('seq', 'chan'), may hold values from -1 to 1
- grad_out: bfloat16 [512, 8192], P('seq', 'chan'), may hold values from -6 to 6
Outputs:
- gated_out: bfloat16 [512, 8192], P('seq', 'chan')
- grad_proj: bfloat16 [512, 3, 8192], P('seq', None, 'chan')
- grad_filter: float32 [512, 8192], P('seq', 'chan')
All inputs are finite; a program needn't handle non-finite values.
Results may differ from a plain program's by a relative error of at most 0.0064.
Values may be sent and summed in bfloat16 or wider, within the bound.
No kernel may reach another device: no remote copies, remote signals or barrier semaphores. Data moves between devices by JAX's collectives and lax.ppermute only.
A program may use at most 192 MiB of HBM per device.

v0:
```python
import math

import jax
import jax.numpy as jnp
from jax import lax
from jax.sharding import PartitionSpec as P


def from_partner(value, axis, stride):
    mask = 2**stride
    pairs = [(source, source ^ mask) for source in range(lax.axis_size(axis))]
    return lax.ppermute(value, axis, pairs)


def bit_reverse(number, bit_count):
    result = number * 0
    for bit_pos in range(bit_count):
        result = result + number // 2**bit_pos % 2 * 2 ** (bit_count - 1 - bit_pos)
    return result


def rotate(state, angle):
    cosine = jnp.cos(angle)
    sine = jnp.sin(angle)
    real_part = state[:, 0]
    imag_part = state[:, 1]
    return jnp.stack(
        [real_part * cosine - imag_part * sine, real_part * sine + imag_part * cosine], axis=1
    )


def pair_swap(state, bit_pos):
    return from_partner(state, "seq", bit_pos)


def across_blocks(state, inverse, seq_index, bit_count):
    if inverse:
        for bit_pos in range(bit_count):
            half_span = 2**bit_pos
            partner = pair_swap(state, bit_pos)
            upper = (seq_index // half_span % 2).astype(jnp.float32)
            lower = 1.0 - upper
            turn_angle = (
                2.0 * math.pi * (seq_index % half_span).astype(jnp.float32) / (2 * half_span)
            )
            first = lower * state + upper * partner
            second = lower * partner + upper * state
            state = 0.5 * (first + (1.0 - 2.0 * upper) * rotate(second, turn_angle))
    else:
        for bit_pos in range(bit_count - 1, -1, -1):
            half_span = 2**bit_pos
            partner = pair_swap(state, bit_pos)
            upper = (seq_index // half_span % 2).astype(jnp.float32)
            turn_angle = (
                -2.0 * math.pi * (seq_index % half_span).astype(jnp.float32) / (2 * half_span)
            )
            state = rotate(partner + (1.0 - 2.0 * upper) * state, upper * turn_angle)
    return state


def per_device(tokens, in_weight, long_filter, grad_out):
    tok_rows, chan_width = long_filter.shape
    groups = lax.axis_size("seq")
    seq_index = lax.axis_index("seq")
    bit_count = groups.bit_length() - 1
    fft_length = 2 * tok_rows * groups
    w_flat = in_weight.reshape(in_weight.shape[0], 3 * chan_width)
    gathered = lax.all_gather(tokens, "chan", axis=1, tiled=True)
    projected = jnp.dot(gathered, w_flat, preferred_element_type=jnp.float32)
    projection = projected.astype(jnp.bfloat16).reshape(tok_rows, 3, chan_width)
    gate_in = projection[:, 0].astype(jnp.float32)
    gate_out = projection[:, 1].astype(jnp.float32)
    values = projection[:, 2].astype(jnp.float32)
    grad_dense = grad_out.astype(jnp.float32)
    signal = jnp.stack([gate_in * values, long_filter, grad_dense * gate_out], axis=1)
    twist_angle = -math.pi * seq_index.astype(jnp.float32) / groups
    real_half = jnp.stack([signal, signal * jnp.cos(twist_angle)], axis=1)
    imag_half = jnp.stack([jnp.zeros_like(signal), signal * jnp.sin(twist_angle)], axis=1)
    twisted = jnp.stack([real_half, imag_half], axis=1)
    mixed = across_blocks(twisted, False, seq_index, bit_count)
    block_freq = 2 * bit_reverse(seq_index, bit_count) + jnp.arange(2, dtype=jnp.int32)
    row_index = jnp.arange(tok_rows, dtype=jnp.int32)
    frequency = block_freq[:, None, None] + 2 * groups * row_index[None, :, None]
    phase = frequency * row_index[None, None, :] % fft_length
    local_angle = -2.0 * math.pi * phase.astype(jnp.float32) / fft_length
    table_re = jnp.cos(local_angle)
    table_im = jnp.sin(local_angle)
    forward_table = jnp.stack(
        [jnp.stack([table_re, -table_im], axis=2), jnp.stack([table_im, table_re], axis=2)], axis=1
    )
    turned_re = jnp.transpose(table_re, (0, 2, 1))
    turned_im = jnp.transpose(table_im, (0, 2, 1))
    inverse_table = jnp.stack(
        [jnp.stack([turned_re, turned_im], axis=2), jnp.stack([-turned_im, turned_re], axis=2)],
        axis=1,
    )
    spectrum = jnp.einsum(
        "eakbn,nbesc->kaesc", forward_table, mixed, precision=lax.Precision.HIGHEST
    )
    spec_re = spectrum[:, 0]
    spec_im = spectrum[:, 1]
    src_re, src_im = (spec_re[:, :, 0], spec_im[:, :, 0])
    filt_re, filt_im = (spec_re[:, :, 1], spec_im[:, :, 1])
    grad_re, grad_im = (spec_re[:, :, 2], spec_im[:, :, 2])
    prod_re = jnp.stack(
        [
            src_re * filt_re - src_im * filt_im,
            filt_re * grad_re + filt_im * grad_im,
            src_re * grad_re + src_im * grad_im,
        ],
        axis=2,
    )
    prod_im = jnp.stack(
        [
            src_re * filt_im + src_im * filt_re,
            filt_re * grad_im - filt_im * grad_re,
            src_re * grad_im - src_im * grad_re,
        ],
        axis=2,
    )
    products = jnp.stack([prod_re, prod_im], axis=1)
    back = (
        jnp.einsum("eanbk,kbesc->naesc", inverse_table, products, precision=lax.Precision.HIGHEST)
        / tok_rows
    )
    returned = across_blocks(back, True, seq_index, bit_count)
    final_angle = math.pi * seq_index.astype(jnp.float32) / groups
    combined = 0.5 * (
        returned[:, 0, 0]
        + returned[:, 0, 1] * jnp.cos(final_angle)
        - returned[:, 1, 1] * jnp.sin(final_angle)
    )
    conv_out = combined[:, 0]
    grad_source = combined[:, 1]
    grad_filter = combined[:, 2]
    gated_out = (gate_out * conv_out).astype(jnp.bfloat16)
    grad_proj = jnp.stack(
        [grad_source * values, grad_dense * conv_out, grad_source * gate_in], axis=1
    ).astype(jnp.bfloat16)
    return (gated_out, grad_proj, grad_filter)


def solution(mesh):
    in_specs = (P("seq", "chan"), P(None, None, "chan"), P("seq", "chan"), P("seq", "chan"))
    out_specs = (P("seq", "chan"), P("seq", None, "chan"), P("seq", "chan"))
    return jax.shard_map(
        per_device, mesh=mesh, in_specs=in_specs, out_specs=out_specs, check_vma=False
    )
```

profile of v0, /device:TPU:0, one launch (start us, length us, event | category | flops | bytes accessed | tf_op | source)
XLA Modules:
  0.0 471.9 jit_solution(11788643299673338047)
XLA Ops:
  7.2 0.7 all-gather.2.cloned.1.call-update
  8.1 63.3 %copy.26 = bf16[8192,3,1024]{0,2,1:T(8,128)(2,1)} copy(bf16[8192,3,1024]{2,0,1:T(8,128)(2,1)} %param.5) | data formatting | bytes 100663296 | tf_op args[1]
  71.4 0.2 copy.29
  71.6 0.2 copy.28
  71.8 22.9 %convolution_convert_fusion = bf16[128,3072]{1,0:T(8,128)(2,1)S(1)} fusion(bf16[128,8192]{1,0:T(8,128)(2,1)} %all-gather.2.cloned.1.call-done, bf16[8192,3072]{0,1:T(8,128)(2,1)} %bitcast.111), kind=kOutput, calls=%fused_computation.24 | convolution fusion | flops 6442844160 | bytes 53215232 | tf_op jit(solution)/shard_map/dot_general | solution.py:69
  94.7 0.4 copy.27
  95.4 0.6 copy-done.5
  96.0 0.2 fusion.16
  96.2 0.5 maximum_bitcast_fusion.2
  96.7 3.3 pad_maximum_fusion
  100.0 0.2 copy-done.3
  100.3 5.9 %collective-permute-start = (f32[128,2,2,3,1024]{0,4,1,3,2:T(8,128)}, f32[128,2,2,3,1024]{0,4,1,3,2:T(8,128)}, u32[]{:S(2)}, u32[]{:S(2)}) collective-permute-start(f32[128,2,2,3,1024]{0,4,1,3,2:T(8,128)} %pad_maximum_fusion), channel_id=1, source_target_pairs={{0,16},{8,24},{16,0},{24,8},{1,17},{9,25},{17,1},{25,9},{2,18},{10... | collective-permute-start | bytes 18874376 | tf_op jit(solution)/shard_map/ppermute | solution.py:12
  106.3 135.7 %collective-permute-done = f32[128,2,2,3,1024]{0,4,1,3,2:T(8,128)} collective-permute-done((f32[128,2,2,3,1024]{0,4,1,3,2:T(8,128)}, f32[128,2,2,3,1024]{0,4,1,3,2:T(8,128)}, u32[]{:S(2)}, u32[]{:S(2)}) %collective-permute-start) | collective-permute-done | bytes 6291488 | tf_op jit(solution)/shard_map/ppermute | solution.py:12
  242.0 4.3 multiply_add_fusion.2
  246.4 0.7 multiply_subtract_fusion.3
  247.1 3.3 pad_maximum_fusion.1
  250.4 0.2 copy-done.4
  250.9 1.1 fusion.40
  252.1 9.1 %collective-permute-done.1 = f32[128,2,2,3,1024]{0,4,1,3,2:T(8,128)} collective-permute-done((f32[128,2,2,3,1024]{0,4,1,3,2:T(8,128)}, f32[128,2,2,3,1024]{0,4,1,3,2:T(8,128)}, u32[]{:S(2)}, u32[]{:S(2)}) %collective-permute-start.1) | collective-permute-done | bytes 6291488 | tf_op jit(solution)/shard_map/ppermute | solution.py:12
  261.1 4.3 multiply_add_fusion.1
  265.5 0.8 multiply_subtract_fusion.2
  266.3 6.5 %fusion.10 = f32[128,2,2,3,1024]{0,4,1,3,2:T(8,128)S(1)} fusion(f32[128,1,2,3,1024]{0,4,1,3,2:T(8,128)S(1)} %get-tuple-element.24, f32[128,1,2,3,1024]{0,4,1,3,2:T(8,128)S(1)} %get-tuple-element.23, f32[2,1,128,2,128]{4,2,3,1,0:T(8,128)S(1)} %get-tuple-element.41, f32[2,1,128,2,128]{4,2,3,1,0:T(8,128)S(1)} %get-tuple-element.40), kind=kOutput, calls=%fused_computation.40 | convolution fusion | flops 4833542144 | bytes 13107200 | tf_op jit(solution)/shard_map/eakbn,nbesc->kaesc/dot_general | solution.py:97
  272.7 0.4 slice_bitcast_fusion.1
  273.2 0.3 multiply_add_fusion.9
  273.5 0.4 multiply_subtract_fusion.6
  273.9 0.2 maximum_bitcast_fusion.3
  274.1 0.2 maximum_bitcast_fusion.4
  274.4 6.2 %fusion.7 = f32[2,3,1024,2,128,1]{4,2,5,1,0,3:T(8,128)S(1)} fusion(f32[2,1,128,2,128]{4,2,3,0,1:T(8,128)S(1)} %get-tuple-element.39, f32[2,1,128,2,128]{4,2,3,0,1:T(8,128)S(1)} %get-tuple-element.38, f32[128,1,2,3,1024]{0,4,3,2,1:T(8,128)S(1)} %maximum_bitcast_fusion.4, f32[128,1,2,3,1024]{0,4,3,2,1:T(8,128)S(1)} %maximum_bitcast_fusion.3), kind=kOutput, calls=%fused_computation.18 | convolution fusion | flops 4833542144 | bytes 13107200 | tf_op jit(solution)/shard_map/eanbk,kbesc->naesc/dot_general | solution.py:123
  280.6 3.7 fusion.6
  284.3 0.9 copy-done
  285.1 0.1 collective-permute-start.2
  285.3 10.4 %collective-permute-done.2 = f32[128,2,2,3,1024]{0,4,3,2,1:T(8,128)} collective-permute-done((f32[128,2,2,3,1024]{0,4,3,2,1:T(8,128)}, f32[128,2,2,3,1024]{0,4,3,2,1:T(8,128)}, u32[]{:S(2)}, u32[]{:S(2)}) %collective-permute-start.2) | collective-permute-done | bytes 6291488 | tf_op jit(solution)/shard_map/ppermute | solution.py:12
  295.6 5.4 %bitcast_add_fusion = f32[128,2,2,3,1024]{0,4,3,2,1:T(8,128)S(1)} fusion(f32[2,3,1024,2,128,1]{4,2,5,1,0,3:T(8,128)} %copy-done, f32[128,2,2,3,1024]{0,4,3,2,1:T(8,128)} %collective-permute-done.2, f32[]{:T(128)S(6)} %mul.440, f32[]{:T(128)S(6)} %sub.63), kind=kLoop, calls=%fused_computation.12 | loop fusion | flops 4718592 | bytes 18874376 | tf_op jit(solution)/shard_map/add | solution.py:47
  301.1 0.6 multiply_subtract_fusion.1
  301.7 2.2 copy-done.1
  303.9 7.1 %broadcast_multiply_fusion = (f32[128,2,2,3,1024]{0,4,3,2,1:T(8,128)}, f32[128,2,2,3,1024]{0,4,3,2,1:T(8,128)}) fusion(f32[128,1,2,3,1024]{0,4,3,2,1:T(8,128)S(1)} %get-tuple-element.14, f32[128,1,2,3,1024]{0,4,3,2,1:T(8,128)S(1)} %get-tuple-element.13, f32[]{:T(128)S(6)} %sub.58, f32[128,2,2,3,1024]{0,4,3,2,1:T(8,128)} %collective-permute-done.2, ...), kind=kLoop, calls=%fused_computation.32 | loop fusion | flops 11010048 | bytes 31457292 | tf_op jit(solution)/shard_map/mul | solution.py:48
  311.0 1.7 collective-permute-start.3
  313.0 135.8 %collective-permute-done.3 = f32[128,2,2,3,1024]{0,4,3,2,1:T(8,128)} collective-permute-done((f32[128,2,2,3,1024]{0,4,3,2,1:T(8,128)}, f32[128,2,2,3,1024]{0,4,3,2,1:T(8,128)}, u32[]{:S(2)}, u32[]{:S(2)}) %collective-permute-start.3) | collective-permute-done | bytes 6291488 | tf_op jit(solution)/shard_map/ppermute | solution.py:12
  448.9 5.4 %multiply_add_fusion = f32[128,2,2,3,1024]{0,4,3,2,1:T(8,128)S(1)} fusion(f32[128,2,2,3,1024]{0,4,3,2,1:T(8,128)} %get-tuple-element.10, f32[128,2,2,3,1024]{0,4,3,2,1:T(8,128)} %collective-permute-done.3, f32[]{:T(128)S(6)} %mul.456, f32[]{:T(128)S(6)} %sub.65), kind=kLoop, calls=%fused_computation.21 | loop fusion | flops 4718592 | bytes 18874376 | tf_op jit(solution)/shard_map/add | solution.py:47
  454.3 0.8 multiply_subtract_fusion
  455.1 2.0 copy-done.2
  457.1 3.5 fusion.5
  460.6 0.3 fusion.13
  460.8 0.9 copy-done.6
  461.7 0.1 fusion.18
  462.0 1.2 copy.42
  463.2 1.0 copy.43
  464.2 0.8 copy.41
  (24 shorter events, 0.7 us)
Async XLA Ops:
  7.2 64.6 %all-gather.2.cloned.1.call-start = ((), (), s32[]{:S(2)}) async-start(), calls=%async_computation | async-start | bytes 2359296 | tf_op jit(solution)/shard_map/all_gather | solution.py:68
  8.1 63.3 %copy-start.8 = (bf16[128,1024]{1,0:T(8,128)(2,1)S(1)}, bf16[128,1024]{1,0:T(8,128)(2,1)}, u32[]{:S(2)}) copy-start(bf16[128,1024]{1,0:T(8,128)(2,1)} %param.7) | copy-start | bytes 786436
  8.1 63.5 %copy-start.7 = (f32[128,1024]{1,0:T(8,128)S(1)}, f32[128,1024]{1,0:T(8,128)}, u32[]{:S(2)}) copy-start(f32[128,1024]{1,0:T(8,128)} %param.6) | copy-start | bytes 1572868
  95.1 0.9 copy-start.5
  96.7 3.6 copy-start.3
  100.3 141.8 %collective-permute-start = (f32[128,2,2,3,1024]{0,4,1,3,2:T(8,128)}, f32[128,2,2,3,1024]{0,4,1,3,2:T(8,128)}, u32[]{:S(2)}, u32[]{:S(2)}) collective-permute-start(f32[128,2,2,3,1024]{0,4,1,3,2:T(8,128)} %pad_maximum_fusion), channel_id=1, source_target_pairs={{0,16},{8,24},{16,0},{24,8},{1,17},{9,25},{17,1},{25,9},{2,18},{10... | collective-permute-start | bytes 18874376 | tf_op jit(solution)/shard_map/ppermute | solution.py:12
  247.0 3.6 copy-start.4
  250.6 10.5 %collective-permute-start.1 = (f32[128,2,2,3,1024]{0,4,1,3,2:T(8,128)}, f32[128,2,2,3,1024]{0,4,1,3,2:T(8,128)}, u32[]{:S(2)}, u32[]{:S(2)}) collective-permute-start(f32[128,2,2,3,1024]{0,4,1,3,2:T(8,128)} %pad_maximum_fusion.1), channel_id=1, source_target_pairs={{0,8},{8,0},{16,24},{24,16},{1,9},{9,1},{17,25},{25,17},{2,10},{10... | collective-permute-start | bytes 18874376 | tf_op jit(solution)/shard_map/ppermute | solution.py:12
  280.6 4.5 copy-start
  285.1 10.5 %collective-permute-start.2 = (f32[128,2,2,3,1024]{0,4,3,2,1:T(8,128)}, f32[128,2,2,3,1024]{0,4,3,2,1:T(8,128)}, u32[]{:S(2)}, u32[]{:S(2)}) collective-permute-start(f32[128,2,2,3,1024]{0,4,3,2,1:T(8,128)} %fusion.6), channel_id=1, source_target_pairs={{0,8},{8,0},{16,24},{24,16},{1,9},{9,1},{17,25},{25,17},{2,10},{10... | collective-permute-start | bytes 18874376 | tf_op jit(solution)/shard_map/ppermute | solution.py:12
  301.1 2.8 copy-start.1
  311.0 137.9 %collective-permute-start.3 = (f32[128,2,2,3,1024]{0,4,3,2,1:T(8,128)}, f32[128,2,2,3,1024]{0,4,3,2,1:T(8,128)}, u32[]{:S(2)}, u32[]{:S(2)}) collective-permute-start(f32[128,2,2,3,1024]{0,4,3,2,1:T(8,128)} %get-tuple-element.9), channel_id=1, source_target_pairs={{0,16},{8,24},{16,0},{24,8},{1,17},{9,25},{17,1},{25,9},{2,18},{10... | collective-permute-start | bytes 18874376 | tf_op jit(solution)/shard_map/ppermute | solution.py:12
  454.3 2.8 copy-start.2
  460.6 1.1 copy-start.6
Sparse Core Ops, SparseCore 0:
  10.2 51.9 all-gather.1
where the time goes:
time: 474 us; the launch traced here: 472 us
  waiting for transfers between devices  292 us (62%)
  local copies, waits for them, and re-layouts  74.5 us (16%)
  other arithmetic  47.3 us (10%)
  matrix products  35.5 us (7%)
  between operations  15.2 us (3%)
  starting transfers between devices  7.82 us (2%)
    ppermute x4, waiting for transfers between devices, from_partner(): return lax.ppermute(value, axis, pairs)  291 us
    unnamed x24, local copies, waits for them, and re-layouts  73.7 us
    dot_general x1, matrix products, per_device(): projected = jnp.dot(gathered, w_flat, preferred_element_type=jnp.float32)  22.9 us
    add x2, other arithmetic, across_blocks(): second = lower * partner + upper * state  10.9 us
    mul x2, other arithmetic, across_blocks(): state = 0.5 * (first + (1.0 - 2.0 * upper) * rotate(second, turn_angle))  10.6 us
  transfers between devices with their start and end apart: 5, of which 4 were waited for; matrix products, arithmetic and copies ran while one was open for 14% of the time, Pallas kernels for 0%

commit v1 on v0

v1 whole, which is shorter than its diff:
```python
import functools

import jax
import jax.numpy as jnp
import numpy as np
from jax import lax
from jax.experimental import pallas as pl
from jax.experimental.pallas import tpu as pltpu
from jax.sharding import PartitionSpec as P

BF16 = jnp.bfloat16
F32 = jnp.float32


def dot(a, b):
    return jnp.dot(a, b, preferred_element_type=F32)


def divisor(size, most):
    tile = min(size, most)
    while size % tile:
        tile //= 2
    return tile


def params(mebibytes):
    return pltpu.CompilerParams(vmem_limit_bytes=mebibytes * 1024 * 1024)


def mebibytes_for(size):
    return max(8, -(-size // 2**20) + 4)


def ring_order(size):
    evens = list(range(0, size, 2))
    return evens + [index + 1 for index in reversed(evens)]


def ring_pairs(size):
    order = ring_order(size)
    return [(order[i], order[(i + 1) % size]) for i in range(size)]


def ring_owners(size):
    order = ring_order(size)
    table = np.zeros((size, size), np.int32)
    for place, index in enumerate(order):
        steps = [0] + [sign * step for step in range(1, size // 2) for sign in (-1, 1)] + [size // 2]
        table[index] = [order[(place + step) % size] for step in steps]
    return table


def sequence_owners(size):
    table = np.zeros((size, size), np.int32)
    for index in range(size):
        chips = [(index + size - 2 * distance) % size for distance in range(1, size // 2)]
        table[index] = [index, index ^ 1] + chips + [chip ^ 1 for chip in chips]
    return table


def in_vmem(array):
    return pltpu.with_memory_space_constraint(array, pltpu.VMEM)


VMEM = pl.BlockSpec(memory_space=pltpu.VMEM)
SMEM = pl.BlockSpec(memory_space=pltpu.SMEM)
ANY = pl.BlockSpec(memory_space=pl.ANY)


def blocks_kernel(owners, first, fresh, place_ref, *refs):
    first_refs, refs = (refs[:2], refs[2:]) if first else ((), refs)
    total_ref, refs = (None, refs) if fresh else (refs[0], refs[1:])
    x_ref, source, out_ref, next_ref, held, sems = refs
    depth = x_ref.shape[1]
    copies = []
    for slot, target in enumerate((held, next_ref)):
        start = pl.multiple_of(place_ref[owners[slot]] * depth, depth)
        copies.append([])
        for j in range(3):
            copy = pltpu.make_async_copy(
                source.at[j, pl.ds(start, depth)], target.at[j], sems.at[slot, j]
            )
            copy.start()
            copies[slot].append(copy)
    values = [None if fresh else total_ref[j] for j in range(3)]
    if first:
        for j in range(3):
            part = dot(first_refs[0][...], first_refs[1][j])
            values[j] = part if fresh else values[j] + part
            out_ref[j] = values[j]
    for j in range(3):
        copies[0][j].wait()
        part = dot(x_ref[...], held[j])
        out_ref[j] = out_ref[j] + part if first else (part if fresh else values[j] + part)
    for copy in copies[1]:
        copy.wait()


def add_blocks(places, owners, total, first, x, weight):
    rows, depth = x.shape
    width = weight.shape[2]
    operands = [places, *(first or ())]
    aliases = {}
    if total is not None:
        aliases = {len(operands): 0}
        operands.append(total)
    operands += [x, weight]
    block = (3, depth, width)
    size = 2 * int(np.prod(block)) + 16 * rows * width + 8 * rows * depth
    return pl.pallas_call(
        functools.partial(blocks_kernel, owners, first is not None, total is None),
        in_specs=[SMEM] + [VMEM] * (len(operands) - 2) + [ANY],
        out_specs=[VMEM] * 2,
        out_shape=[jax.ShapeDtypeStruct((3, rows, width), F32), pltpu.VMEM(block, BF16)],
        scratch_shapes=[pltpu.VMEM(block, BF16), pltpu.SemaphoreType.DMA((2, 3))],
        input_output_aliases=aliases,
        compiler_params=params(mebibytes_for(size)),
        cost_estimate=pl.CostEstimate(
            flops=12 * rows * depth * width, bytes_accessed=12 * depth * width, transcendentals=0
        ),
        name="add_blocks",
    )(*operands)


def last_kernel(chunks, total_ref, grad_ref, x_ref, weight_ref, proj_ref, whole_ref, *chunk_refs):
    width = grad_ref.shape[1] // chunks
    for chunk in range(chunks):
        columns = slice(chunk * width, (chunk + 1) * width)
        streams = []
        for j in range(3):
            value = total_ref[j, :, columns] + dot(x_ref[...], weight_ref[j, :, columns])
            value = value.astype(BF16)
            proj_ref[j, :, columns] = value
            streams.append(value.astype(F32))
        source = (streams[0] * streams[2]).astype(BF16)
        grad = (grad_ref[:, columns].astype(F32) * streams[1]).astype(BF16)
        for ref, place in ((whole_ref, columns), (chunk_refs[chunk], slice(None))):
            ref[0, :, place] = source
            ref[1, :, place] = grad


def last_block(total, grad_out, x, weights, chunks):
    rows, width = grad_out.shape
    depth = x.shape[1]
    size = 40 * rows * width + 4 * rows * depth
    return pl.pallas_call(
        functools.partial(last_kernel, chunks),
        in_specs=[VMEM] * 4,
        out_specs=[VMEM] * (2 + chunks),
        out_shape=[pltpu.VMEM((3, rows, width), BF16), pltpu.VMEM((2, rows, width), BF16)]
        + [pltpu.VMEM((2, rows, width // chunks), BF16)] * chunks,
        compiler_params=params(mebibytes_for(size)),
        cost_estimate=pl.CostEstimate(
            flops=6 * rows * depth * width, bytes_accessed=2**20, transcendentals=0
        ),
        name="last_block",
    )(total, grad_out, x, in_vmem(weights))


def transform_table(length):
    steps = np.arange(length)
    turns = np.outer(2 * steps + 1, steps) % (4 * length)
    angle = turns * (np.pi / (2 * length))
    table = np.concatenate([np.cos(angle), -np.sin(angle)], axis=0).astype(np.float32)
    return jnp.asarray(table.astype(jnp.bfloat16))


def conv_kernel(chunk, final, near, far, first, where_ref, table_ref, back_ref, grad_ref, proj_ref, *refs):
    count = near + far
    tap_refs, pair_refs, refs = refs[:count], refs[count : 2 * count], refs[2 * count :]
    before_refs, refs = (refs[:3], refs[3:]) if chunk else ((), refs)
    held, sems = refs[-2:]
    result_refs, refs = refs[-5:-2], refs[:-5]
    out_refs = refs[-3:]
    gated, gproj, gfilt = result_refs
    rows, width = gated.shape
    columns = slice(chunk * width, (chunk + 1) * width)
    bins = table_ref.shape[0] // 2

    def write(refs, number, slot):
        place = pl.ds(number * width, width)
        copies = [
            pltpu.make_async_copy(refs[0], out_refs[0].at[:, place], sems.at[slot, 0]),
            pltpu.make_async_copy(refs[1], out_refs[1].at[:, :, place], sems.at[slot, 1]),
            pltpu.make_async_copy(refs[2], out_refs[2].at[:, place], sems.at[slot, 2]),
        ]
        return copies

    copies = write(before_refs, chunk - 1, 0) if chunk else []
    for copy in copies:
        copy.start()
    for block in range(count):
        place = pl.ds(pl.multiple_of(where_ref[first + block] * rows, 128), rows)
        taken = columns if block < near else slice(None)
        held[place, :width] = pair_refs[block][0, :, taken]
        held[place, width : 2 * width] = pair_refs[block][1, :, taken]
        held[place, 2 * width :] = tap_refs[block][:, columns].astype(BF16)

    def spectrum(signal):
        both = dot(table_ref[...], held[:, signal * width : (signal + 1) * width])
        return both[:bins], both[bins:]

    def back(real, imag):
        return dot(back_ref[...], jnp.concatenate([real.astype(BF16), imag.astype(BF16)], axis=0))

    src_re, src_im = spectrum(0)
    grad_re, grad_im = spectrum(1)
    filt_re, filt_im = spectrum(2)
    gfilt[...] = back(src_re * grad_re + src_im * grad_im, src_re * grad_im - src_im * grad_re)
    conv_out = back(src_re * filt_re - src_im * filt_im, src_re * filt_im + src_im * filt_re)
    grad_source = back(filt_re * grad_re + filt_im * grad_im, filt_re * grad_im - filt_im * grad_re)
    gated[...] = (proj_ref[1, :, columns].astype(F32) * conv_out).astype(BF16)
    gproj[0] = (grad_source * proj_ref[2, :, columns].astype(F32)).astype(BF16)
    gproj[1] = (grad_ref[:, columns].astype(F32) * conv_out).astype(BF16)
    gproj[2] = (grad_source * proj_ref[0, :, columns].astype(F32)).astype(BF16)
    if final:
        mine = write(result_refs, chunk, 1)
        for copy in mine:
            copy.start()
        copies = copies + mine
    for copy in copies:
        copy.wait()


def convolve(places, first, table, back, grad_out, proj, taps, near, far, before, outs, chunk, final):
    rows, width = grad_out.shape
    length = table.shape[1]
    chunk_width = far[0].shape[2]
    operands = [places, table, back, grad_out, proj, *taps, *near, *far, *before]
    in_specs = [SMEM] + [VMEM] * (len(operands) - 1)
    out_specs, out_shape, aliases = [], [], {}
    if chunk or final:
        out_specs = [ANY] * 3
        out_shape = [
            jax.ShapeDtypeStruct((rows, width), BF16),
            jax.ShapeDtypeStruct((3, rows, width), BF16),
            jax.ShapeDtypeStruct((rows, width), F32),
        ]
    if outs:
        aliases = {len(operands) + i: i for i in range(3)}
        in_specs += [ANY] * 3
        operands += outs
    results = [((rows, chunk_width), BF16), ((3, rows, chunk_width), BF16), ((rows, chunk_width), F32)]
    scratch = [pltpu.VMEM(*result) for result in results] if final else []
    if not final:
        out_specs += [VMEM] * 3
        out_shape += [pltpu.VMEM(*result) for result in results]
    size = 60 * length * chunk_width + 2**22
    out = pl.pallas_call(
        functools.partial(conv_kernel, chunk, final, len(near), len(far), first),
        in_specs=in_specs,
        out_specs=out_specs,
        out_shape=out_shape,
        scratch_shapes=scratch
        + [
            pltpu.VMEM((length, 3 * chunk_width), BF16),
            pltpu.SemaphoreType.DMA((2, 3)),
        ],
        input_output_aliases=aliases,
        compiler_params=params(mebibytes_for(size)),
        cost_estimate=pl.CostEstimate(
            flops=6 * (table.size + 2 * rows * length) * chunk_width,
            bytes_accessed=2**20,
            transcendentals=0,
        ),
        name="convolve",
    )(*operands)
    out = list(out)
    outs = [out.pop(0) for _ in range(3)] if chunk or final else []
    return outs, out


def to_other_core(value, groups):
    return lax.ppermute(value, "seq", [(i, i ^ 1) for i in range(groups)])


def from_other_chips(value, groups):
    return [
        lax.ppermute(value, "seq", [(i, (i + 2 * d) % groups) for i in range(groups)])
        for d in range(1, groups // 2)
    ]


def per_device(tokens, in_weight, long_filter, grad_out):
    rows, width = long_filter.shape
    depth = tokens.shape[1]
    groups = lax.axis_size("seq")
    chans = lax.axis_size("chan")
    seq_index = lax.axis_index("seq")
    chan_index = lax.axis_index("chan")
    length = rows * groups
    weight = jnp.transpose(in_weight, (1, 0, 2))

    owners = np.concatenate(
        [
            np.repeat(sequence_owners(groups), chans, axis=0),
            np.tile(ring_owners(chans), (groups, 1)),
        ],
        axis=1,
    )
    places = lax.dynamic_index_in_dim(
        jnp.asarray(owners), seq_index * chans + chan_index, 0, keepdims=False
    )
    forward = ring_pairs(chans)
    reverse = [(b, a) for a, b in forward]
    steps = chans // 2

    up, down = tokens, tokens
    total, first, x = None, None, tokens
    for step in range(1, steps + 1):
        next_up = lax.ppermute(up, "chan", forward)
        if step < steps:
            next_down = lax.ppermute(down, "chan", reverse)
        if step == 1:
            taps = [long_filter] + from_other_chips(long_filter, groups)
            taps += [to_other_core(block, groups) for block in taps]
        now = 0 if step == 1 else 2 * step - 2
        total, weights = add_blocks(
            places, (groups + now, groups + 2 * step - 1), total, first, x, weight
        )
        if step < steps:
            up, down, total = lax.optimization_barrier((next_up, next_down, total))
            first, x = (up, in_vmem(weights)), down

    table = transform_table(length)
    back = lax.dynamic_slice(table, (0, seq_index * rows), (2 * length, rows))
    back = jnp.transpose(back) * jnp.asarray(1.0 / length, BF16)
    taps = [taps[0], taps[groups // 2]] + taps[1 : groups // 2] + taps[groups // 2 + 1 :]

    chunks = width // divisor(width, 256)
    proj, pair, *pieces = last_block(total, grad_out, next_up, weights, chunks)
    near = [pair, to_other_core(pair, groups)]
    fars = [from_other_chips(piece, groups) for piece in pieces]
    outs, before = [], []
    for chunk in range(chunks):
        far = fars[chunk]
        if chunk >= 2:
            *far, before[0] = lax.optimization_barrier((*far, before[0]))
        fars[chunk] = far + [to_other_core(block, groups) for block in far]
        if chunk:
            outs, before = convolve(
                places, 0, table, back, grad_out, proj, taps, near, fars[chunk - 1], before, outs, chunk - 1, False
            )
    outs, _ = convolve(
        places, 0, table, back, grad_out, proj, taps, near, fars[-1], before, outs, chunks - 1, True
    )
    gated_out, grad_proj, grad_filter = outs
    return gated_out, jnp.transpose(grad_proj, (1, 0, 2)), grad_filter


def solution(mesh):
    in_specs = (P("seq", "chan"), P(None, None, "chan"), P("seq", "chan"), P("seq", "chan"))
    out_specs = (P("seq", "chan"), P("seq", None, "chan"), P("seq", "chan"))
    return jax.shard_map(
        per_device, mesh=mesh, in_specs=in_specs, out_specs=out_specs, check_vma=False
    )
```

time: 474 us -> 65.5 us (0.14)
  waiting for transfers between devices: 292 us -> 7.47 us
  local copies, waits for them, and re-layouts: 74.5 us -> 2.61 us
  other arithmetic: 47.3 us -> 1 us
  Pallas kernels: 0 us -> 37.8 us
  matrix products: 35.5 us -> 0 us
  between operations: 15.2 us -> 0.97 us
  starting transfers between devices: 7.82 us -> 15.3 us
    ppermute x4 -> x19, waiting for transfers between devices: 291 us -> 7.47 us  [the longest x5 5.74 us: from_other_chips(): lax.ppermute(value, 'seq', [(i, (i + 2 * d) % groups) for i in range(grou...]
    unnamed x24 -> x14, local copies, waits for them, and re-layouts: 73.7 us -> 1.92 us
    pallas_call x0 -> x9, Pallas kernels: none -> 37.8 us  [the longest x4 21 us: add_blocks(): pl.pallas_call(functools.partial(blocks_kernel, owners, first is not None...]
    dot_general x3 -> x0, matrix products: 35.5 us -> none  [the longest x1 22.9 us: per_device(): projected = jnp.dot(gathered, w_flat, preferred_element_type=jnp.float32)]
    add x7 -> x0, other arithmetic: 19.9 us -> none  [the longest x2 10.9 us: across_blocks(): second = lower * partner + upper * state]
    mul x6 -> x1, other arithmetic: 11.1 us -> 1 us  [per_device(): back = jnp.transpose(back) * jnp.asarray(1.0 / length, BF16)]
    another operation x12 -> x0, other arithmetic: 8.19 us -> none  [the longest x2 3.86 us: per_device(): twisted = jnp.stack([real_half, imag_half], axis=1)]
    ppermute x4 -> x19, starting transfers between devices: 7.78 us -> 15.3 us  [the longest x4 7.86 us: per_device(): next_up = lax.ppermute(up, 'chan', forward)]
  transfers between devices with their start and end apart: 5 -> 19, of which waited for: 4 -> 4; matrix products, arithmetic and copies ran while one was open for 14% -> 3% of each run, Pallas kernels for 0% -> 52%
where the time goes in v1:
time: 65.5 us; the launch traced here: 65.2 us
  Pallas kernels  37.8 us (58%)
  starting transfers between devices  15.3 us (23%)
  waiting for transfers between devices  7.47 us (11%)
  local copies, waits for them, and re-layouts  2.61 us (4%)
  other arithmetic  1 us (2%)
  between operations  0.97 us (1%)
    pallas_call x4, Pallas kernels, add_blocks(): pl.pallas_call(functools.partial(blocks_kernel, owners, first is not None...  21 us
    pallas_call x4, Pallas kernels, convolve(): pl.pallas_call(functools.partial(conv_kernel, chunk, final, len(near), le...  14.7 us
    ppermute x4, starting transfers between devices, per_device(): next_up = lax.ppermute(up, 'chan', forward)  7.86 us
    ppermute x5, waiting for transfers between devices, from_other_chips(): lax.ppermute(value, 'seq', [(i, (i + 2 * d) % groups) for i in range(grou...  5.74 us
    ppermute x5, starting transfers between devices, from_other_chips(): lax.ppermute(value, 'seq', [(i, (i + 2 * d) % groups) for i in range(grou...  5.39 us
    pallas_call x1, Pallas kernels, last_block(): pl.pallas_call(functools.partial(last_kernel, chunks), in_specs=[VMEM] *...  2.06 us
    unnamed x14, local copies, waits for them, and re-layouts  1.92 us
    ppermute x3, waiting for transfers between devices, per_device(): next_down = lax.ppermute(down, 'chan', reverse)  1.7 us
  transfers between devices with their start and end apart: 19, of which 4 were waited for; matrix products, arithmetic and copies ran while one was open for 3% of the time, Pallas kernels for 52%

profile of v1, /device:TPU:0, one launch (start us, length us, event | category | flops | bytes accessed | tf_op | source)
XLA Modules:
  0.0 65.2 jit_solution(3863918544917463023)
XLA Ops:
  0.6 3.1 %collective-permute-start = (bf16[128,1024]{1,0:T(8,128)(2,1)}, bf16[128,1024]{1,0:T(8,128)(2,1)S(1)}, u32[]{:S(2)}, u32[]{:S(2)}) collective-permute-start(bf16[128,1024]{1,0:T(8,128)(2,1)} %refs_0_.5), channel_id=1, source_target_pairs={{0,2},{2,4},{4,6},{6,7},{7,5},{5,3},{3,1},{1,0},{8,10},{10,12},{12... | collective-permute-start | bytes 786440 | tf_op jit(solution)/shard_map/ppermute | solution.py:311
  3.7 0.0 collective-permute-start.1
  3.7 0.7 %dynamic-slice_bitcast_fusion.place_ref.where_ref = s32[12]{0:T(128)S(1)} fusion(s32[32,12]{1,0:T(8,128)} %constant.27.clone, s32[]{:T(128)S(6)} %select_n.7), kind=kLoop, calls=%fused_computation.1 | loop fusion | bytes 100 | tf_op jit(solution)/shard_map/jit(dynamic_index_in_dim)/squeeze | solution.py:301
  4.4 0.9 %copy-done.4 = bf16[128,1024]{1,0:T(8,128)(2,1)S(1)} copy-done((bf16[128,1024]{1,0:T(8,128)(2,1)S(1)}, bf16[128,1024]{1,0:T(8,128)(2,1)}, u32[]{:S(2)}) %copy-start.4) | copy-done | bytes 262168
  5.4 5.3 %add_blocks.4 = (f32[3,128,1024]{2,1,0:T(8,128)S(1)}, bf16[3,1024,1024]{2,1,0:T(8,128)(2,1)S(1)}) custom-call(s32[12]{0:T(128)S(1)} %dynamic-slice_bitcast_fusion.place_ref.where_ref, bf16[128,1024]{1,0:T(8,128)(2,1)S(1)} %copy-done.4, bf16[3,8192,1024]{2,1,0:T(8,128)(2,1)} %bitcast.6), custom_call_target="tpu_custom_call" | custom-call | flops 1610612736 | bytes 12582912 | tf_op jit(solution)/shard_map/add_blocks/pallas_call | solution.py:110
  10.6 0.0 collective-permute-done.refs_0_
  10.6 1.0 %collective-permute-done.1.refs_3_ = bf16[128,1024]{1,0:T(8,128)(2,1)S(1)} collective-permute-done((bf16[128,1024]{1,0:T(8,128)(2,1)}, bf16[128,1024]{1,0:T(8,128)(2,1)S(1)}, u32[]{:S(2)}, u32[]{:S(2)}) %collective-permute-start.1) | collective-permute-done | bytes 262176 | tf_op jit(solution)/shard_map/ppermute | solution.py:313
  11.7 1.6 %collective-permute-start.2 = (bf16[128,1024]{1,0:T(8,128)(2,1)S(1)}, bf16[128,1024]{1,0:T(8,128)(2,1)S(1)}, u32[]{:S(2)}, u32[]{:S(2)}) collective-permute-start(bf16[128,1024]{1,0:T(8,128)(2,1)S(1)} %collective-permute-done.refs_0_), channel_id=1, source_target_pairs={{0,2},{2,4},{4,6},{6,7},{7,5},{5,3},{3,1},{1,0},{8,10},{10,12},{12... | collective-permute-start | bytes 786440 | tf_op jit(solution)/shard_map/ppermute | solution.py:311
  13.3 0.4 collective-permute-start.3
  13.7 1.5 %collective-permute-start.8 = (f32[128,1024]{1,0:T(8,128)S(1)}, f32[128,1024]{1,0:T(8,128)S(1)}, u32[]{:S(2)}, u32[]{:S(2)}) collective-permute-start(f32[128,1024]{1,0:T(8,128)S(1)} %copy-done.1), channel_id=1, source_target_pairs={{0,16},{8,24},{16,0},{24,8},{1,17},{9,25},{17,1},{25,9},{2,18},{10... | collective-permute-start | bytes 1572872 | tf_op jit(solution)/shard_map/ppermute | solution.py:279
  15.2 5.3 %add_blocks.5 = (f32[3,128,1024]{2,1,0:T(8,128)S(1)}, bf16[3,1024,1024]{2,1,0:T(8,128)(2,1)S(1)}) custom-call(s32[12]{0:T(128)S(1)} %dynamic-slice_bitcast_fusion.place_ref.where_ref, bf16[128,1024]{1,0:T(8,128)(2,1)S(1)} %collective-permute-done.refs_0_, bf16[3,1024,1024]{2,1,0:T(8,128)(2,1)S(1)} %get-tuple-element.51.refs_1_, ...), custom_call_target="tpu_custom_call", output_to_operand_aliasing={{0}: (3, {})} | custom-call | flops 1610612736 | bytes 12582912 | tf_op jit(solution)/shard_map/add_blocks/pallas_call | solution.py:110
  20.5 0.0 collective-permute-done.2.refs_0_
  20.5 0.0 collective-permute-done.3.refs_3_
  20.5 1.6 %collective-permute-start.4 = (bf16[128,1024]{1,0:T(8,128)(2,1)S(1)}, bf16[128,1024]{1,0:T(8,128)(2,1)S(1)}, u32[]{:S(2)}, u32[]{:S(2)}) collective-permute-start(bf16[128,1024]{1,0:T(8,128)(2,1)S(1)} %collective-permute-done.2.refs_0_), channel_id=1, source_target_pairs={{0,2},{2,4},{4,6},{6,7},{7,5},{5,3},{3,1},{1,0},{8,10},{10,12},{12... | collective-permute-start | bytes 786440 | tf_op jit(solution)/shard_map/ppermute | solution.py:311
  22.1 0.4 collective-permute-start.5
  22.6 5.3 %add_blocks.6 = (f32[3,128,1024]{2,1,0:T(8,128)S(1)}, bf16[3,1024,1024]{2,1,0:T(8,128)(2,1)S(1)}) custom-call(s32[12]{0:T(128)S(1)} %dynamic-slice_bitcast_fusion.place_ref.where_ref, bf16[128,1024]{1,0:T(8,128)(2,1)S(1)} %collective-permute-done.2.refs_0_, bf16[3,1024,1024]{2,1,0:T(8,128)(2,1)S(1)} %get-tuple-element.56.refs_1_, ...), custom_call_target="tpu_custom_call", output_to_operand_aliasing={{0}: (3, {})} | custom-call | flops 1610612736 | bytes 12582912 | tf_op jit(solution)/shard_map/add_blocks/pallas_call | solution.py:110
  27.8 0.0 collective-permute-done.4.refs_0_
  27.8 0.6 collective-permute-done.5.refs_3_
  28.5 1.6 %collective-permute-start.6 = (bf16[128,1024]{1,0:T(8,128)(2,1)S(1)}, bf16[128,1024]{1,0:T(8,128)(2,1)S(1)}, u32[]{:S(2)}, u32[]{:S(2)}) collective-permute-start(bf16[128,1024]{1,0:T(8,128)(2,1)S(1)} %collective-permute-done.4.refs_0_), channel_id=1, source_target_pairs={{0,2},{2,4},{4,6},{6,7},{7,5},{5,3},{3,1},{1,0},{8,10},{10,12},{12... | collective-permute-start | bytes 786440 | tf_op jit(solution)/shard_map/ppermute | solution.py:311
  30.1 0.0 collective-permute-start.7
  30.1 0.0 collective-permute-done.8.refs_2_
  30.1 0.5 collective-permute-start.9
  30.6 5.3 %add_blocks.7 = (f32[3,128,1024]{2,1,0:T(8,128)S(1)}, bf16[3,1024,1024]{2,1,0:T(8,128)(2,1)S(1)}) custom-call(s32[12]{0:T(128)S(1)} %dynamic-slice_bitcast_fusion.place_ref.where_ref, bf16[128,1024]{1,0:T(8,128)(2,1)S(1)} %collective-permute-done.4.refs_0_, bf16[3,1024,1024]{2,1,0:T(8,128)(2,1)S(1)} %get-tuple-element.60.refs_1_, ...), custom_call_target="tpu_custom_call", output_to_operand_aliasing={{0}: (3, {})} | custom-call | flops 1610612736 | bytes 12582912 | tf_op jit(solution)/shard_map/add_blocks/pallas_call | solution.py:110
  35.8 0.0 copy-start
  35.9 2.1 %last_block.1 = (bf16[3,128,1024]{2,1,0:T(8,128)(2,1)S(1)}, bf16[2,128,1024]{2,1,0:T(8,128)(2,1)}, bf16[2,128,256]{2,1,0:T(8,128)(2,1)S(1)}, bf16[2,128,256]{2,1...) custom-call(f32[3,128,1024]{2,1,0:T(8,128)S(1)} %get-tuple-element.63.total_ref, ...), custom_call_target="tpu_custom_call" | custom-call | flops 805306368 | bytes 1048576 | tf_op jit(solution)/shard_map/last_block/pallas_call | solution.py:146
  37.9 0.0 collective-permute-start.10
  38.0 0.9 %collective-permute-start.15 = (bf16[2,128,256]{2,1,0:T(8,128)(2,1)S(1)}, bf16[2,128,256]{2,1,0:T(8,128)(2,1)}, u32[]{:S(2)}, u32[]{:S(2)}) collective-permute-start(bf16[2,128,256]{2,1,0:T(8,128)(2,1)S(1)} %get-tuple-element.70), channel_id=1, source_target_pairs={{0,16},{8,24},{16,0},{24,8},{1,17},{9,25},{17,1},{25,9},{2,18},{10... | collective-permute-start | bytes 393224 | tf_op jit(solution)/shard_map/ppermute | solution.py:279
  38.9 1.2 %collective-permute-start.12 = (bf16[2,128,256]{2,1,0:T(8,128)(2,1)}, bf16[2,128,256]{2,1,0:T(8,128)(2,1)S(1)}, u32[]{:S(2)}, u32[]{:S(2)}) collective-permute-start(bf16[2,128,256]{2,1,0:T(8,128)(2,1)} %get-tuple-element.68), channel_id=1, source_target_pairs={{0,16},{8,24},{16,0},{24,8},{1,17},{9,25},{17,1},{25,9},{2,18},{10... | collective-permute-start | bytes 393224 | tf_op jit(solution)/shard_map/ppermute | solution.py:279
  40.1 4.4 %collective-permute-done.15.refs_6_ = bf16[2,128,256]{2,1,0:T(8,128)(2,1)} collective-permute-done((bf16[2,128,256]{2,1,0:T(8,128)(2,1)S(1)}, bf16[2,128,256]{2,1,0:T(8,128)(2,1)}, u32[]{:S(2)}, u32[]{:S(2)}) %collective-permute-start.15) | collective-permute-done | bytes 131104 | tf_op jit(solution)/shard_map/ppermute | solution.py:279
  44.4 0.0 collective-permute-start.16
  44.4 0.0 collective-permute-done.7.refs_1_
  44.4 0.9 %collective-permute-start.14 = (bf16[2,128,256]{2,1,0:T(8,128)(2,1)}, bf16[2,128,256]{2,1,0:T(8,128)(2,1)S(1)}, u32[]{:S(2)}, u32[]{:S(2)}) collective-permute-start(bf16[2,128,256]{2,1,0:T(8,128)(2,1)} %copy-done.6), channel_id=1, source_target_pairs={{0,16},{8,24},{16,0},{24,8},{1,17},{9,25},{17,1},{25,9},{2,18},{10... | collective-permute-start | bytes 393224 | tf_op jit(solution)/shard_map/ppermute | solution.py:279
  45.3 1.4 %collective-permute-done.12.refs_6_ = bf16[2,128,256]{2,1,0:T(8,128)(2,1)S(1)} collective-permute-done((bf16[2,128,256]{2,1,0:T(8,128)(2,1)}, bf16[2,128,256]{2,1,0:T(8,128)(2,1)S(1)}, u32[]{:S(2)}, u32[]{:S(2)}) %collective-permute-start.12) | collective-permute-done | bytes 131104 | tf_op jit(solution)/shard_map/ppermute | solution.py:279
  46.7 1.0 %multiply_bitcast_fusion.back_ref = bf16[128,1024]{1,0:T(8,128)(2,1)S(1)} fusion(bf16[1024,512]{0,1:T(8,128)(2,1)} %constant.28.clone, s32[]{:T(128)S(6)} %select_n.8), kind=kLoop, calls=%fused_computation | loop fusion | flops 524288 | bytes 524292 | tf_op jit(solution)/shard_map/mul | solution.py:327
  47.7 0.0 collective-permute-done.9.refs_3_
  47.7 0.9 %collective-permute-start.11 = (bf16[2,128,256]{2,1,0:T(8,128)(2,1)}, bf16[2,128,256]{2,1,0:T(8,128)(2,1)S(1)}, u32[]{:S(2)}, u32[]{:S(2)}) collective-permute-start(bf16[2,128,256]{2,1,0:T(8,128)(2,1)} %copy-done.5), channel_id=1, source_target_pairs={{0,16},{8,24},{16,0},{24,8},{1,17},{9,25},{17,1},{25,9},{2,18},{10... | collective-permute-start | bytes 393224 | tf_op jit(solution)/shard_map/ppermute | solution.py:279
  48.6 0.0 copy-start.3
  48.7 0.9 %copy-done.3 = bf16[128,1024]{1,0:T(8,128)(2,1)S(1)} copy-done((bf16[128,1024]{1,0:T(8,128)(2,1)S(1)}, bf16[128,1024]{1,0:T(8,128)(2,1)}, u32[]{:S(2)}) %copy-start.3) | copy-done | bytes 262168
  49.6 3.3 %convolve.4 = (bf16[128,256]{1,0:T(8,128)(2,1)S(1)}, bf16[3,128,256]{2,1,0:T(8,128)(2,1)S(1)}, f32[128,256]{1,0:T(8,128)S(1)}) custom-call(s32[12]{0:T(128)S(1)} %dynamic-slice_bitcast_fusion.place_ref.where_ref, bf16[1024,512]{1,0:T(8,128)(2,1)S(1)} %copy-done, bf16[128,1024]{1,0:T(8,128)(2,1)S(1)} %multiply_bitcast_fusion.back_ref, ...), custom_call_target="tpu_custom_call" | custom-call | flops 1006632960 | bytes 1048576 | tf_op jit(solution)/shard_map/convolve/pallas_call | solution.py:249
  52.9 0.3 collective-permute-start.18
  53.2 0.0 collective-permute-done.13.refs_7_
  53.2 3.8 %convolve.5 = (bf16[128,1024]{1,0:T(8,128)(2,1)}, bf16[3,128,1024]{2,1,0:T(8,128)(2,1)}, f32[128,1024]{1,0:T(8,128)}, bf16[128,256]{1,0:T(8,128)(2,1)S(1)}, bf16...) custom-call(s32[12]{0:T(128)S(1)} %dynamic-slice_bitcast_fusion.place_ref.where_ref, bf16[1024,512]{1,0:T(8,128)(2,1)S(1)} %copy-done, ...), custom_call_target="tpu_custom_call" | custom-call | flops 1006632960 | bytes 1048576 | tf_op jit(solution)/shard_map/convolve/pallas_call | solution.py:249
  56.9 0.0 collective-permute-done.11.refs_6_
  56.9 0.3 collective-permute-start.17
  57.3 0.0 collective-permute-done.18.refs_7_
  57.3 3.8 %convolve.6 = (bf16[128,1024]{1,0:T(8,128)(2,1)}, bf16[3,128,1024]{2,1,0:T(8,128)(2,1)}, f32[128,1024]{1,0:T(8,128)}, bf16[128,256]{1,0:T(8,128)(2,1)S(1)}, bf16...) custom-call(s32[12]{0:T(128)S(1)} %dynamic-slice_bitcast_fusion.plac, ...), custom_call_target="tpu_custom_call", output_to_operand_aliasing={{0}: (16, {}), {1}: (17, {}), {2}: (18, {})} | custom-call | flops 1006632960 | bytes 1048576 | tf_op jit(solution)/shard_map/convolve/pallas_call | solution.py:249
  61.1 0.0 collective-permute-done.17.refs_7_
  61.1 3.9 %convolve.7 = (bf16[128,1024]{1,0:T(8,128)(2,1)}, bf16[3,128,1024]{2,1,0:T(8,128)(2,1)}, f32[128,1024]{1,0:T(8,128)}) custom-call(s32[12]{0:T(128)S(1)} %dynamic-slice_bitcast_fusion.place_ref.where_ref, bf16[1024,512]{1,0:T(8,128)(2,1)S(1)} %copy-done, ...), custom_call_target="tpu_custom_call", output_to_operand_aliasing={{0}: (16, {}), {1}: (17, {}), {2}: (18, {})} | custom-call | flops 1006632960 | bytes 1048576 | tf_op jit(solution)/shard_map/convolve/pallas_call | solution.py:249
  (15 shorter events, 0.0 us)
Async XLA Ops:
  0.6 10.0 %collective-permute-start = (bf16[128,1024]{1,0:T(8,128)(2,1)}, bf16[128,1024]{1,0:T(8,128)(2,1)S(1)}, u32[]{:S(2)}, u32[]{:S(2)}) collective-permute-start(bf16[128,1024]{1,0:T(8,128)(2,1)} %refs_0_.5), channel_id=1, source_target_pairs={{0,2},{2,4},{4,6},{6,7},{7,5},{5,3},{3,1},{1,0},{8,10},{10,12},{12... | collective-permute-start | bytes 786440 | tf_op jit(solution)/shard_map/ppermute | solution.py:311
  3.7 8.0 %collective-permute-start.1 = (bf16[128,1024]{1,0:T(8,128)(2,1)}, bf16[128,1024]{1,0:T(8,128)(2,1)S(1)}, u32[]{:S(2)}, u32[]{:S(2)}) collective-permute-start(bf16[128,1024]{1,0:T(8,128)(2,1)} %refs_0_.5), channel_id=1, source_target_pairs={{2,0},{4,2},{6,4},{7,6},{5,7},{3,5},{1,3},{0,1},{10,8},{12,10},{14... | collective-permute-start | bytes 786440 | tf_op jit(solution)/shard_map/ppermute | solution.py:313
  4.4 0.9 %copy-start.4 = (bf16[128,1024]{1,0:T(8,128)(2,1)S(1)}, bf16[128,1024]{1,0:T(8,128)(2,1)}, u32[]{:S(2)}) copy-start(bf16[128,1024]{1,0:T(8,128)(2,1)} %refs_0_.5) | copy-start | bytes 786436
  5.4 8.4 %copy-start.1 = (f32[128,1024]{1,0:T(8,128)S(1)}, f32[128,1024]{1,0:T(8,128)}, u32[]{:S(2)}) copy-start(f32[128,1024]{1,0:T(8,128)} %refs_0_.9) | copy-start | bytes 1572868
  11.7 8.8 %collective-permute-start.2 = (bf16[128,1024]{1,0:T(8,128)(2,1)S(1)}, bf16[128,1024]{1,0:T(8,128)(2,1)S(1)}, u32[]{:S(2)}, u32[]{:S(2)}) collective-permute-start(bf16[128,1024]{1,0:T(8,128)(2,1)S(1)} %collective-permute-done.refs_0_), channel_id=1, source_target_pairs={{0,2},{2,4},{4,6},{6,7},{7,5},{5,3},{3,1},{1,0},{8,10},{10,12},{12... | collective-permute-start | bytes 786440 | tf_op jit(solution)/shard_map/ppermute | solution.py:311
  13.3 7.2 %collective-permute-start.3 = (bf16[128,1024]{1,0:T(8,128)(2,1)S(1)}, bf16[128,1024]{1,0:T(8,128)(2,1)S(1)}, u32[]{:S(2)}, u32[]{:S(2)}) collective-permute-start(bf16[128,1024]{1,0:T(8,128)(2,1)S(1)} %collective-permute-done.1.refs_3_), channel_id=1, source_target_pairs={{2,0},{4,2},{6,4},{7,6},{5,7},{3,5},{1,3},{0,1},{10,8},{12,10},{14... | collective-permute-start | bytes 786440 | tf_op jit(solution)/shard_map/ppermute | solution.py:313
  13.7 16.4 %collective-permute-start.8 = (f32[128,1024]{1,0:T(8,128)S(1)}, f32[128,1024]{1,0:T(8,128)S(1)}, u32[]{:S(2)}, u32[]{:S(2)}) collective-permute-start(f32[128,1024]{1,0:T(8,128)S(1)} %copy-done.1), channel_id=1, source_target_pairs={{0,16},{8,24},{16,0},{24,8},{1,17},{9,25},{17,1},{25,9},{2,18},{10... | collective-permute-start | bytes 1572872 | tf_op jit(solution)/shard_map/ppermute | solution.py:279
  20.5 7.3 %collective-permute-start.4 = (bf16[128,1024]{1,0:T(8,128)(2,1)S(1)}, bf16[128,1024]{1,0:T(8,128)(2,1)S(1)}, u32[]{:S(2)}, u32[]{:S(2)}) collective-permute-start(bf16[128,1024]{1,0:T(8,128)(2,1)S(1)} %collective-permute-done.2.refs_0_), channel_id=1, source_target_pairs={{0,2},{2,4},{4,6},{6,7},{7,5},{5,3},{3,1},{1,0},{8,10},{10,12},{12... | collective-permute-start | bytes 786440 | tf_op jit(solution)/shard_map/ppermute | solution.py:311
  22.1 6.4 %collective-permute-start.5 = (bf16[128,1024]{1,0:T(8,128)(2,1)S(1)}, bf16[128,1024]{1,0:T(8,128)(2,1)S(1)}, u32[]{:S(2)}, u32[]{:S(2)}) collective-permute-start(bf16[128,1024]{1,0:T(8,128)(2,1)S(1)} %collective-permute-done.3.refs_3_), channel_id=1, source_target_pairs={{2,0},{4,2},{6,4},{7,6},{5,7},{3,5},{1,3},{0,1},{10,8},{12,10},{14... | collective-permute-start | bytes 786440 | tf_op jit(solution)/shard_map/ppermute | solution.py:313
  28.5 7.4 %collective-permute-start.6 = (bf16[128,1024]{1,0:T(8,128)(2,1)S(1)}, bf16[128,1024]{1,0:T(8,128)(2,1)S(1)}, u32[]{:S(2)}, u32[]{:S(2)}) collective-permute-start(bf16[128,1024]{1,0:T(8,128)(2,1)S(1)} %collective-permute-done.4.refs_0_), channel_id=1, source_target_pairs={{0,2},{2,4},{4,6},{6,7},{7,5},{5,3},{3,1},{1,0},{8,10},{10,12},{12... | collective-permute-start | bytes 786440 | tf_op jit(solution)/shard_map/ppermute | solution.py:311
  30.1 14.4 %collective-permute-start.7 = (f32[128,1024]{1,0:T(8,128)S(1)}, f32[128,1024]{1,0:T(8,128)S(1)}, u32[]{:S(2)}, u32[]{:S(2)}) collective-permute-start(f32[128,1024]{1,0:T(8,128)S(1)} %copy-done.1), channel_id=1, source_target_pairs={{0,8},{8,0},{16,24},{24,16},{1,9},{9,1},{17,25},{25,17},{2,10},{10... | collective-permute-start | bytes 1572872 | tf_op jit(solution)/shard_map/ppermute | solution.py:274
  30.1 17.6 %collective-permute-start.9 = (f32[128,1024]{1,0:T(8,128)S(1)}, f32[128,1024]{1,0:T(8,128)}, u32[]{:S(2)}, u32[]{:S(2)}) collective-permute-start(f32[128,1024]{1,0:T(8,128)S(1)} %collective-permute-done.8.refs_2_), channel_id=1, source_target_pairs={{0,8},{8,0},{16,24},{24,16},{1,9},{9,1},{17,25},{25,17},{2,10},{10... | collective-permute-start | bytes 1572872 | tf_op jit(solution)/shard_map/ppermute | solution.py:274
  30.6 5.3 %copy-start.2 = (bf16[128,1024]{1,0:T(8,128)(2,1)S(1)}, bf16[128,1024]{1,0:T(8,128)(2,1)}, u32[]{:S(2)}) copy-start(bf16[128,1024]{1,0:T(8,128)(2,1)} %grad_ref.9) | copy-start | bytes 786436
  35.8 12.8 %copy-start = (bf16[1024,512]{1,0:T(8,128)(2,1)S(1)}, bf16[1024,512]{1,0:T(8,128)(2,1)}, u32[]{:S(2)}) copy-start(bf16[1024,512]{1,0:T(8,128)(2,1)} %constant.29.table_ref) | copy-start | bytes 3145732
  37.9 1.0 %copy-start.5 = (bf16[2,128,256]{2,1,0:T(8,128)(2,1)}, bf16[2,128,256]{2,1,0:T(8,128)(2,1)S(1)}, u32[]{:S(2)}) copy-start(bf16[2,128,256]{2,1,0:T(8,128)(2,1)S(1)} %get-tuple-element.67) | copy-start | bytes 393220
  37.9 1.0 %copy-start.6 = (bf16[2,128,256]{2,1,0:T(8,128)(2,1)}, bf16[2,128,256]{2,1,0:T(8,128)(2,1)S(1)}, u32[]{:S(2)}) copy-start(bf16[2,128,256]{2,1,0:T(8,128)(2,1)S(1)} %get-tuple-element.69) | copy-start | bytes 393220
  37.9 10.7 %collective-permute-start.10 = (bf16[2,128,1024]{2,1,0:T(8,128)(2,1)}, bf16[2,128,1024]{2,1,0:T(8,128)(2,1)}, u32[]{:S(2)}, u32[]{:S(2)}) collective-permute-start(bf16[2,128,1024]{2,1,0:T(8,128)(2,1)} %get-tuple-element.66.refs_4_), channel_id=1, source_target_pairs={{0,8},{8,0},{16,24},{24,16},{1,9},{9,1},{17,25},{25,17},{2,10},{10... | collective-permute-start | bytes 1572872 | tf_op jit(solution)/shard_map/ppermute | solution.py:274
  38.0 6.5 %collective-permute-start.15 = (bf16[2,128,256]{2,1,0:T(8,128)(2,1)S(1)}, bf16[2,128,256]{2,1,0:T(8,128)(2,1)}, u32[]{:S(2)}, u32[]{:S(2)}) collective-permute-start(bf16[2,128,256]{2,1,0:T(8,128)(2,1)S(1)} %get-tuple-element.70), channel_id=1, source_target_pairs={{0,16},{8,24},{16,0},{24,8},{1,17},{9,25},{17,1},{25,9},{2,18},{10... | collective-permute-start | bytes 393224 | tf_op jit(solution)/shard_map/ppermute | solution.py:279
  38.9 7.8 %collective-permute-start.12 = (bf16[2,128,256]{2,1,0:T(8,128)(2,1)}, bf16[2,128,256]{2,1,0:T(8,128)(2,1)S(1)}, u32[]{:S(2)}, u32[]{:S(2)}) collective-permute-start(bf16[2,128,256]{2,1,0:T(8,128)(2,1)} %get-tuple-element.68), channel_id=1, source_target_pairs={{0,16},{8,24},{16,0},{24,8},{1,17},{9,25},{17,1},{25,9},{2,18},{10... | collective-permute-start | bytes 393224 | tf_op jit(solution)/shard_map/ppermute | solution.py:279
  44.4 4.2 %collective-permute-start.16 = (bf16[2,128,256]{2,1,0:T(8,128)(2,1)}, bf16[2,128,256]{2,1,0:T(8,128)(2,1)}, u32[]{:S(2)}, u32[]{:S(2)}) collective-permute-start(bf16[2,128,256]{2,1,0:T(8,128)(2,1)} %collective-permute-done.15.refs_6_), channel_id=1, source_target_pairs={{0,8},{8,0},{16,24},{24,16},{1,9},{9,1},{17,25},{25,17},{2,10},{10... | collective-permute-start | bytes 393224 | tf_op jit(solution)/shard_map/ppermute | solution.py:274
  44.4 8.4 %collective-permute-start.14 = (bf16[2,128,256]{2,1,0:T(8,128)(2,1)}, bf16[2,128,256]{2,1,0:T(8,128)(2,1)S(1)}, u32[]{:S(2)}, u32[]{:S(2)}) collective-permute-start(bf16[2,128,256]{2,1,0:T(8,128)(2,1)} %copy-done.6), channel_id=1, source_target_pairs={{0,16},{8,24},{16,0},{24,8},{1,17},{9,25},{17,1},{25,9},{2,18},{10... | collective-permute-start | bytes 393224 | tf_op jit(solution)/shard_map/ppermute | solution.py:279
  46.7 6.5 %collective-permute-start.13 = (bf16[2,128,256]{2,1,0:T(8,128)(2,1)S(1)}, bf16[2,128,256]{2,1,0:T(8,128)(2,1)S(1)}, u32[]{:S(2)}, u32[]{:S(2)}) collective-permute-start(bf16[2,128,256]{2,1,0:T(8,128)(2,1)S(1)} %collective-permute-done.12.refs_6_), channel_id=1, source_target_pairs={{0,8},{8,0},{16,24},{24,16},{1,9},{9,1},{17,25},{25,17},{2,10},{10... | collective-permute-start | bytes 393224 | tf_op jit(solution)/shard_map/ppermute | solution.py:274
  47.7 9.2 %collective-permute-start.11 = (bf16[2,128,256]{2,1,0:T(8,128)(2,1)}, bf16[2,128,256]{2,1,0:T(8,128)(2,1)S(1)}, u32[]{:S(2)}, u32[]{:S(2)}) collective-permute-start(bf16[2,128,256]{2,1,0:T(8,128)(2,1)} %copy-done.5), channel_id=1, source_target_pairs={{0,16},{8,24},{16,0},{24,8},{1,17},{9,25},{17,1},{25,9},{2,18},{10... | collective-permute-start | bytes 393224 | tf_op jit(solution)/shard_map/ppermute | solution.py:279
  48.6 1.0 %copy-start.3 = (bf16[128,1024]{1,0:T(8,128)(2,1)S(1)}, bf16[128,1024]{1,0:T(8,128)(2,1)}, u32[]{:S(2)}) copy-start(bf16[128,1024]{1,0:T(8,128)(2,1)} %grad_ref.9) | copy-start | bytes 786436
  52.9 4.4 %collective-permute-start.18 = (bf16[2,128,256]{2,1,0:T(8,128)(2,1)S(1)}, bf16[2,128,256]{2,1,0:T(8,128)(2,1)S(1)}, u32[]{:S(2)}, u32[]{:S(2)}) collective-permute-start(bf16[2,128,256]{2,1,0:T(8,128)(2,1)S(1)} %collective-permute-done.14.refs_6_), channel_id=1, source_target_pairs={{0,8},{8,0},{16,24},{24,16},{1,9},{9,1},{17,25},{25,17},{2,10},{10... | collective-permute-start | bytes 393224 | tf_op jit(solution)/shard_map/ppermute | solution.py:274
  56.9 4.1 %collective-permute-start.17 = (bf16[2,128,256]{2,1,0:T(8,128)(2,1)S(1)}, bf16[2,128,256]{2,1,0:T(8,128)(2,1)S(1)}, u32[]{:S(2)}, u32[]{:S(2)}) collective-permute-start(bf16[2,128,256]{2,1,0:T(8,128)(2,1)S(1)} %collective-permute-done.11.refs_6_), channel_id=1, source_target_pairs={{0,8},{8,0},{16,24},{24,16},{1,9},{9,1},{17,25},{25,17},{2,10},{10... | collective-permute-start | bytes 393224 | tf_op jit(solution)/shard_map/ppermute | solution.py:274

commit v2 on v1

v2 whole, which is shorter than its diff:
```python
import functools

import jax
import jax.numpy as jnp
import numpy as np
from jax import lax
from jax.experimental import pallas as pl
from jax.experimental.pallas import tpu as pltpu
from jax.sharding import PartitionSpec as P

BF16 = jnp.bfloat16
F32 = jnp.float32


def dot(a, b):
    return jnp.dot(a, b, preferred_element_type=F32)


def divisor(size, most):
    tile = min(size, most)
    while size % tile:
        tile //= 2
    return tile


def params(mebibytes):
    return pltpu.CompilerParams(vmem_limit_bytes=mebibytes * 1024 * 1024)


def mebibytes_for(size):
    return max(8, -(-size // 2**20) + 4)


def ring_order(size):
    evens = list(range(0, size, 2))
    return evens + [index + 1 for index in reversed(evens)]


def ring_pairs(size):
    order = ring_order(size)
    return [(order[i], order[(i + 1) % size]) for i in range(size)]


def ring_owner(device, chans, offset):
    index = lax.rem(device, chans)
    half = lax.div(index, 2)
    position = jnp.where(lax.rem(index, 2) == 0, half, chans - 1 - half)
    position = lax.rem(position + (offset + chans), chans)
    return jnp.where(position < chans // 2, 2 * position, 2 * (chans - 1 - position) + 1)


def sequence_owner(device, chans, groups, distance):
    return lax.rem(lax.div(device, chans) + (groups - 2 * distance), groups)


def in_vmem(array):
    return pltpu.with_memory_space_constraint(array, pltpu.VMEM)


VMEM = pl.BlockSpec(memory_space=pltpu.VMEM)
SMEM = pl.BlockSpec(memory_space=pltpu.SMEM)
ANY = pl.BlockSpec(memory_space=pl.ANY)
HBM = pl.BlockSpec(memory_space=pltpu.HBM)


def blocks_kernel(chans, offsets, first, fresh, own, device_ref, *refs):
    first_refs, refs = (refs[:2], refs[2:]) if first else ((), refs)
    total_ref, refs = (None, refs) if fresh else (refs[0], refs[1:])
    x_ref, source, out_ref, next_ref, held, sems, *own_refs = refs
    depth = x_ref.shape[1]
    if own:
        own_x, own_sem = own_refs
        own_copy = pltpu.make_async_copy(x_ref, own_x, own_sem)
        own_copy.start()
        x_ref = own_x
    copies = []
    for slot, target in enumerate((held, next_ref)):
        start = pl.multiple_of(ring_owner(device_ref[0], chans, offsets[slot]) * depth, depth)
        copies.append(
            pltpu.make_async_copy(source.at[:, pl.ds(start, depth)], target, sems.at[slot])
        )
        copies[slot].start()
    values = [None if fresh else total_ref[j] for j in range(3)]
    if first:
        for j in range(3):
            part = dot(first_refs[0][...], first_refs[1][j])
            values[j] = part if fresh else values[j] + part
            out_ref[j] = values[j]
    if own:
        own_copy.wait()
    copies[0].wait()
    for j in range(3):
        part = dot(x_ref[...], held[j])
        out_ref[j] = out_ref[j] + part if first else (part if fresh else values[j] + part)
    copies[1].wait()


def add_blocks(device, chans, offsets, total, first, x, weight):
    rows, depth = x.shape
    width = weight.shape[2]
    own = first is None
    operands = [device, *(first or ())]
    aliases = {}
    if total is not None:
        aliases = {len(operands): 0}
        operands.append(total)
    operands += [x, weight]
    block = (3, depth, width)
    size = 2 * int(np.prod(block)) + 16 * rows * width + 8 * rows * depth
    scratch = [pltpu.VMEM(block, BF16), pltpu.SemaphoreType.DMA((2,))]
    if own:
        scratch += [pltpu.VMEM((rows, depth), BF16), pltpu.SemaphoreType.DMA]
    return pl.pallas_call(
        functools.partial(blocks_kernel, chans, offsets, not own, total is None, own),
        in_specs=[SMEM] + [VMEM] * (len(operands) - 3) + [ANY if own else VMEM, ANY],
        out_specs=[VMEM] * 2,
        out_shape=[jax.ShapeDtypeStruct((3, rows, width), F32), pltpu.VMEM(block, BF16)],
        scratch_shapes=scratch,
        input_output_aliases=aliases,
        compiler_params=params(mebibytes_for(size)),
        cost_estimate=pl.CostEstimate(
            flops=12 * rows * depth * width, bytes_accessed=12 * depth * width, transcendentals=0
        ),
        name="add_blocks",
    )(*operands)


def last_kernel(cuts, total_ref, grad_ref, x_ref, weight_ref, proj_ref, whole_ref, *chunk_refs):
    for chunk_ref, columns in zip(chunk_refs, cuts):
        streams = []
        for j in range(3):
            value = total_ref[j, :, columns] + dot(x_ref[...], weight_ref[j, :, columns])
            value = value.astype(BF16)
            proj_ref[j, :, columns] = value
            streams.append(value.astype(F32))
        source = (streams[0] * streams[2]).astype(BF16)
        grad = (grad_ref[:, columns].astype(F32) * streams[1]).astype(BF16)
        for ref, place in ((whole_ref, columns), (chunk_ref, slice(None))):
            ref[0, :, place] = source
            ref[1, :, place] = grad


def last_block(total, grad_out, x, weights, cuts):
    rows, width = grad_out.shape
    depth = x.shape[1]
    size = 40 * rows * width + 4 * rows * depth
    return pl.pallas_call(
        functools.partial(last_kernel, cuts),
        in_specs=[VMEM] * 4,
        out_specs=[VMEM] * (2 + len(cuts)),
        out_shape=[pltpu.VMEM((3, rows, width), BF16), pltpu.VMEM((2, rows, width), BF16)]
        + [pltpu.VMEM((2, rows, cut.stop - cut.start), BF16) for cut in cuts],
        compiler_params=params(mebibytes_for(size)),
        cost_estimate=pl.CostEstimate(
            flops=6 * rows * depth * width, bytes_accessed=2**20, transcendentals=0
        ),
        name="last_block",
    )(total, grad_out, x, in_vmem(weights))


def transform_table(length):
    steps = np.arange(length)
    turns = np.outer(2 * steps + 1, steps) % (4 * length)
    angle = turns * (np.pi / (2 * length))
    table = np.concatenate([np.cos(angle), -np.sin(angle)], axis=0).astype(np.float32)
    return jnp.asarray(table.astype(jnp.bfloat16))


def chip_rows(owner, ref, other_ref, columns):
    first = lax.rem(owner, 2) == 0
    signals = []
    for signal in range(2):
        mine, others = ref[signal, :, columns], other_ref[signal, :, columns]
        signals.append(
            jnp.concatenate([jnp.where(first, mine, others), jnp.where(first, others, mine)], axis=0)
        )
    return jnp.concatenate(signals, axis=1)


def chip_table(table_ref, owner, rows):
    return table_ref[:, pl.ds(pl.multiple_of(owner // 2 * 2 * rows, 256), 2 * rows)]


def spectra_kernel(chans, groups, device_ref, table_ref, *refs):
    tap_refs, (own_ref, other_ref, filt_ref, near_ref, back_ref, taps) = refs[:groups], refs[groups:]
    rows, width = tap_refs[0].shape
    tile = divisor(width, 256)
    chips = groups // 2
    for number, ref in enumerate(tap_refs):
        owner = sequence_owner(device_ref[0], chans, groups, number % chips)
        if number >= chips:
            owner = owner + 1 - 2 * lax.rem(owner, 2)
        taps[pl.ds(pl.multiple_of(owner * rows, 128), rows)] = ref[...]
    for start in range(0, width, tile):
        columns = slice(start, start + tile)
        filt_ref[:, columns] = dot(table_ref[...], taps[:, columns])
    owner = sequence_owner(device_ref[0], chans, groups, 0)
    length = table_ref.shape[1]
    mine = table_ref[:, pl.ds(pl.multiple_of(owner * rows, 128), rows)]
    back_ref[...] = (mine.astype(F32).T * (1.0 / length)).astype(BF16)
    table = chip_table(table_ref, owner, rows)
    for start in range(0, width, tile):
        held = chip_rows(owner, own_ref, other_ref, slice(start, start + tile))
        near_ref[:, 2 * start : 2 * start + 2 * tile] = dot(table, held)


def spectra(device, chans, table, taps, pair, other_pair):
    rows, width = taps[0].shape
    bins, length = table.shape
    size = 2 * table.size + 4 * length * width + 40 * rows * width + 2**21
    return pl.pallas_call(
        functools.partial(spectra_kernel, chans, len(taps)),
        in_specs=[SMEM] + [VMEM] * (3 + len(taps)),
        out_specs=[VMEM] * 3,
        out_shape=[
            pltpu.VMEM((bins, width), F32),
            pltpu.VMEM((bins, 2 * width), F32),
            pltpu.VMEM((rows, bins), BF16),
        ],
        scratch_shapes=[pltpu.VMEM((length, width), BF16)],
        compiler_params=params(mebibytes_for(size)),
        cost_estimate=pl.CostEstimate(flops=2**20, bytes_accessed=2**16, transcendentals=0),
        name="spectra",
    )(device, table, *taps, pair, other_pair)


def conv_kernel(chans, groups, pieces, first, tile, aliased, device_ref, *refs):
    chips = groups // 2 - 1
    table_ref, back_ref, grad_ref, proj_ref, filt_ref, near_ref, *refs = refs
    count = 2 * chips * pieces
    far_refs, refs = refs[:count], refs[count + 3 * aliased :]
    gated_out, gproj_out, gfilt_out, gated, gproj, gfilt, sems = refs
    rows, width = gated.shape
    bins = table_ref.shape[0] // 2
    owners = [sequence_owner(device_ref[0], chans, groups, chip + 1) for chip in range(chips)]
    piece_width = width // pieces
    copies = []
    for start in range(0, width, tile):
        here = slice(start, start + tile)
        there = slice(first + start, first + start + tile)
        pairs = slice(2 * (first + start), 2 * (first + start) + 2 * tile)
        both = near_ref[:, pairs]
        piece, offset = divmod(start, piece_width)
        for chip, owner in enumerate(owners):
            held = chip_rows(
                owner,
                far_refs[chip * pieces + piece],
                far_refs[(chips + chip) * pieces + piece],
                slice(offset, offset + tile),
            )
            both = both + dot(chip_table(table_ref, owner, rows), held)
        src_re, src_im = both[:bins, :tile], both[bins:, :tile]
        grad_re, grad_im = both[:bins, tile:], both[bins:, tile:]
        filt_re, filt_im = filt_ref[:bins, there], filt_ref[bins:, there]
        real = [
            src_re * filt_re - src_im * filt_im,
            filt_re * grad_re + filt_im * grad_im,
            src_re * grad_re + src_im * grad_im,
        ]
        imag = [
            src_re * filt_im + src_im * filt_re,
            filt_re * grad_im - filt_im * grad_re,
            src_re * grad_im - src_im * grad_re,
        ]
        products = jnp.concatenate(
            [
                jnp.concatenate([re.astype(BF16), im.astype(BF16)], axis=0)
                for re, im in zip(real, imag)
            ],
            axis=1,
        )
        result = dot(back_ref[...], products)
        conv_out, grad_source = result[:, :tile], result[:, tile : 2 * tile]
        gfilt[:, here] = result[:, 2 * tile :]
        gated[:, here] = (proj_ref[1, :, there].astype(F32) * conv_out).astype(BF16)
        gproj[0, :, here] = (grad_source * proj_ref[2, :, there].astype(F32)).astype(BF16)
        gproj[1, :, here] = (grad_ref[:, there].astype(F32) * conv_out).astype(BF16)
        gproj[2, :, here] = (grad_source * proj_ref[0, :, there].astype(F32)).astype(BF16)
        number = start // tile
        copies += [
            pltpu.make_async_copy(gated.at[:, here], gated_out.at[:, there], sems.at[number, 0]),
            pltpu.make_async_copy(gproj.at[:, :, here], gproj_out.at[:, :, there], sems.at[number, 1]),
            pltpu.make_async_copy(gfilt.at[:, here], gfilt_out.at[:, there], sems.at[number, 2]),
        ]
        for copy in copies[-3:]:
            copy.start()
    for copy in copies:
        copy.wait()


def convolve(device, chans, groups, table, back, grad_out, proj, filt, near, far, pieces, outs, cut):
    rows, width = grad_out.shape
    bins, length = table.shape
    chunk_width = cut.stop - cut.start
    chips = groups // 2 - 1
    tile = divisor(chunk_width, 256)
    operands = [device, table, back, grad_out, proj, filt, near, *far]
    in_specs = [SMEM] + [VMEM] * (len(operands) - 1)
    aliases = {}
    if outs:
        aliases = {len(operands) + i: i for i in range(3)}
        in_specs += [ANY] * 3
        operands += outs
    size = 48 * length * tile + 20 * chips * rows * chunk_width + 2 * table.size + 2**22
    return pl.pallas_call(
        functools.partial(conv_kernel, chans, groups, pieces, cut.start, tile, bool(outs)),
        in_specs=in_specs,
        out_specs=[ANY] * 3,
        out_shape=[
            jax.ShapeDtypeStruct((rows, width), BF16),
            jax.ShapeDtypeStruct((3, rows, width), BF16),
            jax.ShapeDtypeStruct((rows, width), F32),
        ],
        scratch_shapes=[
            pltpu.VMEM((rows, chunk_width), BF16),
            pltpu.VMEM((3, rows, chunk_width), BF16),
            pltpu.VMEM((rows, chunk_width), F32),
            pltpu.SemaphoreType.DMA((chunk_width // tile, 3)),
        ],
        input_output_aliases=aliases,
        compiler_params=params(mebibytes_for(size)),
        cost_estimate=pl.CostEstimate(flops=2**20, bytes_accessed=2**16, transcendentals=0),
        name="convolve",
    )(*operands)


def to_other_core(value, groups):
    return lax.ppermute(value, "seq", [(i, i ^ 1) for i in range(groups)])


def from_other_chips(value, groups):
    return [
        lax.ppermute(value, "seq", [(i, (i + 2 * d) % groups) for i in range(groups)])
        for d in range(1, groups // 2)
    ]


def per_device(tokens, in_weight, long_filter, grad_out):
    rows, width = long_filter.shape
    depth = tokens.shape[1]
    groups = lax.axis_size("seq")
    chans = lax.axis_size("chan")
    seq_index = lax.axis_index("seq")
    chan_index = lax.axis_index("chan")
    length = rows * groups
    weight = jnp.transpose(in_weight, (1, 0, 2))

    device = (seq_index * chans + chan_index)[None]
    forward = ring_pairs(chans)
    reverse = [(b, a) for a, b in forward]
    steps = chans // 2

    up, down = tokens, tokens
    total, first, x = None, None, pltpu.with_memory_space_constraint(tokens, pltpu.HBM)
    for step in range(1, steps + 1):
        next_up = lax.ppermute(up, "chan", forward)
        if step < steps:
            next_down = lax.ppermute(down, "chan", reverse)
        if step == 1:
            filt = long_filter.astype(BF16)
        if step == steps:
            taps = [filt] + from_other_chips(filt, groups)
        total, weights = add_blocks(
            device, chans, (step - 1, -step), total, first, x, weight
        )
        if step < steps:
            up, down, total, filt = lax.optimization_barrier((next_up, next_down, total, filt))
            first, x = (up, in_vmem(weights)), down
        else:
            last, total, *taps = lax.optimization_barrier((next_up, total, *taps))

    table = transform_table(length)
    edge = width // 2
    cuts = [slice(0, edge), slice(edge, width)] if edge % 256 == 0 else [slice(0, width)]
    pieces = [slice(0, edge // 2), slice(edge // 2, edge)] + cuts[1:] if len(cuts) > 1 else cuts
    proj, pair, *parts = last_block(total, grad_out, last, weights, pieces)
    fars = [from_other_chips(part, groups) for part in parts]
    filt, near, back = spectra(
        device,
        chans,
        table,
        taps + [to_other_core(block, groups) for block in taps],
        pair,
        to_other_core(pair, groups),
    )
    outs = None
    for cut in cuts:
        far = [fars.pop(0) for piece in pieces if cut.start <= piece.start < cut.stop]
        count = len(far)
        far = [block for blocks in zip(*far) for block in blocks]
        if outs:
            *far, outs[2] = lax.optimization_barrier((*far, outs[2]))
        else:
            *far, near = lax.optimization_barrier((*far, near))
        far = far + [to_other_core(block, groups) for block in far]
        outs = list(
            convolve(
                device, chans, groups, table, back, grad_out, proj, filt, near, far, count, outs, cut
            )
        )
    gated_out, grad_proj, grad_filter = outs
    return gated_out, jnp.transpose(grad_proj, (1, 0, 2)), grad_filter


def solution(mesh):
    in_specs = (P("seq", "chan"), P(None, None, "chan"), P("seq", "chan"), P("seq", "chan"))
    out_specs = (P("seq", "chan"), P("seq", None, "chan"), P("seq", "chan"))
    return jax.shard_map(
        per_device, mesh=mesh, in_specs=in_specs, out_specs=out_specs, check_vma=False
    )
```

time: 65.5 us -> 57.3 us (0.87)
  Pallas kernels: 37.8 us -> 30.6 us
  waiting for transfers between devices: 7.47 us -> 10.2 us
  local copies, waits for them, and re-layouts: 2.61 us -> 0.01 us
  starting transfers between devices: 15.3 us -> 14.3 us
    pallas_call x9 -> x8, Pallas kernels: 37.8 us -> 30.6 us  [the longest x4 20.9 us: add_blocks(): pl.pallas_call(functools.partial(blocks_kernel, chans, offsets, not own,...]
    ppermute x7 -> x6, waiting for transfers between devices: 0.02 us -> 2.56 us  [to_other_core(): return lax.ppermute(value, 'seq', [(i, i ^ 1) for i in range(groups)])]
    unnamed x14 -> x4, local copies, waits for them, and re-layouts: 1.92 us -> 0.01 us
    ppermute x5 -> x4, waiting for transfers between devices: 5.74 us -> 4.28 us  [from_other_chips(): lax.ppermute(value, 'seq', [(i, (i + 2 * d) % groups) for i in range(grou...]
    convert_element_type x0 -> x1, other arithmetic: none -> 1.07 us  [per_device(): filt = long_filter.astype(BF16)]
    ppermute x3, waiting for transfers between devices: 1.7 us -> 2.73 us  [per_device(): next_down = lax.ppermute(down, 'chan', reverse)]
    mul x1 -> x0, other arithmetic: 1 us -> none  [per_device(): back = jnp.transpose(back) * jnp.asarray(1.0 / length, BF16)]
    ppermute x5 -> x4, starting transfers between devices: 5.39 us -> 4.44 us  [from_other_chips(): lax.ppermute(value, 'seq', [(i, (i + 2 * d) % groups) for i in range(grou...]
  transfers between devices with their start and end apart: 19 -> 17, of which waited for: 4 -> 10; matrix products, arithmetic and copies ran while one was open for 3% -> 2% of each run, Pallas kernels for 52% -> 46%
where the time goes in v2:
time: 57.3 us; the launch traced here: 57.1 us
  Pallas kernels  30.6 us (53%)
  starting transfers between devices  14.3 us (25%)
  waiting for transfers between devices  10.2 us (18%)
  other arithmetic  1.07 us (2%)
  between operations  0.93 us (2%)
    pallas_call x4, Pallas kernels, add_blocks(): pl.pallas_call(functools.partial(blocks_kernel, chans, offsets, not own,...  20.9 us
    ppermute x4, starting transfers between devices, per_device(): next_up = lax.ppermute(up, 'chan', forward)  7.75 us
    pallas_call x2, Pallas kernels, convolve(): pl.pallas_call(functools.partial(conv_kernel, chans, groups, pieces, cut....  6.12 us
    ppermute x4, starting transfers between devices, from_other_chips(): lax.ppermute(value, 'seq', [(i, (i + 2 * d) % groups) for i in range(grou...  4.44 us
    ppermute x4, waiting for transfers between devices, from_other_chips(): lax.ppermute(value, 'seq', [(i, (i + 2 * d) % groups) for i in range(grou...  4.28 us
    ppermute x3, waiting for transfers between devices, per_device(): next_down = lax.ppermute(down, 'chan', reverse)  2.73 us
    ppermute x6, waiting for transfers between devices, to_other_core(): return lax.ppermute(value, 'seq', [(i, i ^ 1) for i in range(groups)])  2.56 us
    pallas_call x1, Pallas kernels, spectra(): pl.pallas_call(functools.partial(spectra_kernel, chans, len(taps)), in_sp...  2.43 us
  transfers between devices with their start and end apart: 17, of which 10 were waited for; matrix products, arithmetic and copies ran while one was open for 2% of the time, Pallas kernels for 46%

profile of v2, /device:TPU:0, one launch (start us, length us, event | category | flops | bytes accessed | tf_op | source)
XLA Modules:
  0.0 57.1 jit_solution(13792237341929775097)
XLA Ops:
  0.6 3.1 %collective-permute-start = (bf16[128,1024]{1,0:T(8,128)(2,1)}, bf16[128,1024]{1,0:T(8,128)(2,1)S(1)}, u32[]{:S(2)}, u32[]{:S(2)}) collective-permute-start(bf16[128,1024]{1,0:T(8,128)(2,1)} %refs_0_.3), channel_id=1, source_target_pairs={{0,2},{2,4},{4,6},{6,7},{7,5},{5,3},{3,1},{1,0},{8,10},{10,12},{12... | collective-permute-start | bytes 786440 | tf_op jit(solution)/shard_map/ppermute | solution.py:356
  3.7 0.0 collective-permute-start.1
  3.7 1.1 %convert_element_type.3.refs_0_ = bf16[128,1024]{1,0:T(8,128)(2,1)S(1)} convert(f32[128,1024]{1,0:T(8,128)} %param.7) | non-fusion elementwise | flops 131072 | bytes 786432 | tf_op jit(solution)/shard_map/convert_element_type | solution.py:360
  4.8 4.7 %add_blocks.4 = (f32[3,128,1024]{2,1,0:T(8,128)S(1)}, bf16[3,1024,1024]{2,1,0:T(8,128)(2,1)S(1)}) custom-call(s32[1]{0:T(128)} %bitcast.device_ref, bf16[128,1024]{1,0:T(8,128)(2,1)} %refs_0_.3, bf16[3,8192,1024]{2,1,0:T(8,128)(2,1)} %bitcast.3), custom_call_target="tpu_custom_call" | custom-call | flops 1610612736 | bytes 12582912 | tf_op jit(solution)/shard_map/add_blocks/pallas_call | solution.py:113
  9.5 0.6 %collective-permute-done.refs_0_ = bf16[128,1024]{1,0:T(8,128)(2,1)S(1)} collective-permute-done((bf16[128,1024]{1,0:T(8,128)(2,1)}, bf16[128,1024]{1,0:T(8,128)(2,1)S(1)}, u32[]{:S(2)}, u32[]{:S(2)}) %collective-permute-start) | collective-permute-done | bytes 262176 | tf_op jit(solution)/shard_map/ppermute | solution.py:356
  10.2 1.5 %collective-permute-done.1.refs_3_ = bf16[128,1024]{1,0:T(8,128)(2,1)S(1)} collective-permute-done((bf16[128,1024]{1,0:T(8,128)(2,1)}, bf16[128,1024]{1,0:T(8,128)(2,1)S(1)}, u32[]{:S(2)}, u32[]{:S(2)}) %collective-permute-start.1) | collective-permute-done | bytes 262176 | tf_op jit(solution)/shard_map/ppermute | solution.py:358
  11.7 1.6 %collective-permute-start.2 = (bf16[128,1024]{1,0:T(8,128)(2,1)S(1)}, bf16[128,1024]{1,0:T(8,128)(2,1)S(1)}, u32[]{:S(2)}, u32[]{:S(2)}) collective-permute-start(bf16[128,1024]{1,0:T(8,128)(2,1)S(1)} %collective-permute-done.refs_0_), channel_id=1, source_target_pairs={{0,2},{2,4},{4,6},{6,7},{7,5},{5,3},{3,1},{1,0},{8,10},{10,12},{12... | collective-permute-start | bytes 786440 | tf_op jit(solution)/shard_map/ppermute | solution.py:356
  13.3 0.4 collective-permute-start.3
  13.7 5.4 %add_blocks.5 = (f32[3,128,1024]{2,1,0:T(8,128)S(1)}, bf16[3,1024,1024]{2,1,0:T(8,128)(2,1)S(1)}) custom-call(s32[1]{0:T(128)} %bitcast.device_ref, bf16[128,1024]{1,0:T(8,128)(2,1)S(1)} %collective-permute-done.refs_0_, bf16[3,1024,1024]{2,1,0:T(8,128)(2,1)S(1)} %get-tuple-element.49.refs_1_, ...), custom_call_target="tpu_custom_call", output_to_operand_aliasing={{0}: (3, {})} | custom-call | flops 1610612736 | bytes 12582912 | tf_op jit(solution)/shard_map/add_blocks/pallas_call | solution.py:113
  19.1 0.0 collective-permute-done.2.refs_0_
  19.1 0.7 %collective-permute-done.3.refs_3_ = bf16[128,1024]{1,0:T(8,128)(2,1)S(1)} collective-permute-done((bf16[128,1024]{1,0:T(8,128)(2,1)S(1)}, bf16[128,1024]{1,0:T(8,128)(2,1)S(1)}, u32[]{:S(2)}, u32[]{:S(2)}) %collective-permute-start.3) | collective-permute-done | bytes 262176 | tf_op jit(solution)/shard_map/ppermute | solution.py:358
  19.8 1.6 %collective-permute-start.4 = (bf16[128,1024]{1,0:T(8,128)(2,1)S(1)}, bf16[128,1024]{1,0:T(8,128)(2,1)S(1)}, u32[]{:S(2)}, u32[]{:S(2)}) collective-permute-start(bf16[128,1024]{1,0:T(8,128)(2,1)S(1)} %collective-permute-done.2.refs_0_), channel_id=1, source_target_pairs={{0,2},{2,4},{4,6},{6,7},{7,5},{5,3},{3,1},{1,0},{8,10},{10,12},{12... | collective-permute-start | bytes 786440 | tf_op jit(solution)/shard_map/ppermute | solution.py:356
  21.4 0.4 collective-permute-start.5
  21.9 5.4 %add_blocks.6 = (f32[3,128,1024]{2,1,0:T(8,128)S(1)}, bf16[3,1024,1024]{2,1,0:T(8,128)(2,1)S(1)}) custom-call(s32[1]{0:T(128)} %bitcast.device_ref, bf16[128,1024]{1,0:T(8,128)(2,1)S(1)} %collective-permute-done.2.refs_0_, bf16[3,1024,1024]{2,1,0:T(8,128)(2,1)S(1)} %get-tuple-element.55.refs_1_, ...), custom_call_target="tpu_custom_call", output_to_operand_aliasing={{0}: (3, {})} | custom-call | flops 1610612736 | bytes 12582912 | tf_op jit(solution)/shard_map/add_blocks/pallas_call | solution.py:113
  27.2 0.0 collective-permute-done.4.refs_0_
  27.3 0.5 collective-permute-done.5.refs_3_
  27.8 1.5 %collective-permute-start.6 = (bf16[128,1024]{1,0:T(8,128)(2,1)S(1)}, bf16[128,1024]{1,0:T(8,128)(2,1)S(1)}, u32[]{:S(2)}, u32[]{:S(2)}) collective-permute-start(bf16[128,1024]{1,0:T(8,128)(2,1)S(1)} %collective-permute-done.4.refs_0_), channel_id=1, source_target_pairs={{0,2},{2,4},{4,6},{6,7},{7,5},{5,3},{3,1},{1,0},{8,10},{10,12},{12... | collective-permute-start | bytes 786440 | tf_op jit(solution)/shard_map/ppermute | solution.py:356
  29.3 1.5 %collective-permute-start.7 = (bf16[128,1024]{1,0:T(8,128)(2,1)S(1)}, bf16[128,1024]{1,0:T(8,128)(2,1)S(1)}, u32[]{:S(2)}, u32[]{:S(2)}) collective-permute-start(bf16[128,1024]{1,0:T(8,128)(2,1)S(1)} %convert_element_type.3.refs_0_), channel_id=1, source_target_pairs={{0,16},{8,24},{16,0},{24,8},{1,17},{9,25},{17,1},{25,9},{2,18},{10... | collective-permute-start | bytes 786440 | tf_op jit(solution)/shard_map/ppermute | solution.py:333
  30.8 0.0 copy-start.1
  30.8 5.4 %add_blocks.7 = (f32[3,128,1024]{2,1,0:T(8,128)S(1)}, bf16[3,1024,1024]{2,1,0:T(8,128)(2,1)S(1)}) custom-call(s32[1]{0:T(128)} %bitcast.device_ref, bf16[128,1024]{1,0:T(8,128)(2,1)S(1)} %collective-permute-done.4.refs_0_, bf16[3,1024,1024]{2,1,0:T(8,128)(2,1)S(1)} %get-tuple-element.60.refs_1_, ...), custom_call_target="tpu_custom_call", output_to_operand_aliasing={{0}: (3, {})} | custom-call | flops 1610612736 | bytes 12582912 | tf_op jit(solution)/shard_map/add_blocks/pallas_call | solution.py:113
  36.2 0.0 copy-start
  36.2 0.0 collective-permute-done.6.x_ref
  36.2 0.0 collective-permute-done.7.refs_1_
  36.2 0.0 copy-done.1
  36.3 1.2 %last_block.1 = (bf16[3,128,1024]{2,1,0:T(8,128)(2,1)S(1)}, bf16[2,128,1024]{2,1,0:T(8,128)(2,1)S(1)}, bf16[2,128,256]{2,1,0:T(8,128)(2,1)S(1)}, bf16[2,128,256]...) custom-call(f32[3,128,1024]{2,1,0:T(8,128)S(1)} %get-tuple-element.67.total_ref, bf16[128,1024]{1,0:T(8,128)(2,1)S(1)} %copy-done.1, ...), custom_call_target="tpu_custom_call" | custom-call | flops 805306368 | bytes 1048576 | tf_op jit(solution)/shard_map/last_block/pallas_call | solution.py:147
  37.4 0.1 collective-permute-start.10
  37.5 0.5 collective-permute-start.8
  38.0 0.1 collective-permute-start.9
  38.1 0.9 %collective-permute-start.11 = (bf16[2,128,256]{2,1,0:T(8,128)(2,1)S(1)}, bf16[2,128,256]{2,1,0:T(8,128)(2,1)S(1)}, u32[]{:S(2)}, u32[]{:S(2)}) collective-permute-start(bf16[2,128,256]{2,1,0:T(8,128)(2,1)S(1)} %get-tuple-element.74), channel_id=1, source_target_pairs={{0,16},{8,24},{16,0},{24,8},{1,17},{9,25},{17,1},{25,9},{2,18},{10... | collective-permute-start | bytes 393224 | tf_op jit(solution)/shard_map/ppermute | solution.py:333
  39.0 1.1 %collective-permute-start.12 = (bf16[2,128,256]{2,1,0:T(8,128)(2,1)S(1)}, bf16[2,128,256]{2,1,0:T(8,128)(2,1)S(1)}, u32[]{:S(2)}, u32[]{:S(2)}) collective-permute-start(bf16[2,128,256]{2,1,0:T(8,128)(2,1)S(1)} %get-tuple-element.75), channel_id=1, source_target_pairs={{0,16},{8,24},{16,0},{24,8},{1,17},{9,25},{17,1},{25,9},{2,18},{10... | collective-permute-start | bytes 393224 | tf_op jit(solution)/shard_map/ppermute | solution.py:333
  40.1 0.0 collective-permute-done.8.refs_2_
  40.1 0.9 %collective-permute-start.13 = (bf16[2,128,512]{2,1,0:T(8,128)(2,1)S(1)}, bf16[2,128,512]{2,1,0:T(8,128)(2,1)S(1)}, u32[]{:S(2)}, u32[]{:S(2)}) collective-permute-start(bf16[2,128,512]{2,1,0:T(8,128)(2,1)S(1)} %get-tuple-element.78), channel_id=1, source_target_pairs={{0,16},{8,24},{16,0},{24,8},{1,17},{9,25},{17,1},{25,9},{2,18},{10... | collective-permute-start | bytes 786440 | tf_op jit(solution)/shard_map/ppermute | solution.py:333
  41.0 0.0 collective-permute-done.9.refs_3_
  41.1 0.0 collective-permute-done.10.refs_5_
  41.1 0.0 copy-done
  41.1 2.4 %spectra.1 = (f32[1024,1024]{1,0:T(8,128)S(1)}, f32[1024,2048]{1,0:T(8,128)S(1)}, bf16[128,1024]{1,0:T(8,128)(2,1)S(1)}) custom-call(s32[1]{0:T(128)} %bitcast.device_ref, bf16[1024,512]{1,0:T(8,128)(2,1)S(1)} %copy-done, bf16[128,1024]{1,0:T(8,128)(2,1)S(1)} %convert_element_type.3.refs_0_, bf16[128,1024]{1,0:T(8,128)(2,1)S(1)} %collective-permute-done.7.refs_1_, ...), custom_call_target="tpu_custom_call" | custom-call | flops 1048576 | bytes 65536 | tf_op jit(solution)/shard_map/spectra/pallas_call | solution.py:211
  43.5 0.9 %collective-permute-done.11.refs_6_ = bf16[2,128,256]{2,1,0:T(8,128)(2,1)S(1)} collective-permute-done((bf16[2,128,256]{2,1,0:T(8,128)(2,1)S(1)}, bf16[2,128,256]{2,1,0:T(8,128)(2,1)S(1)}, u32[]{:S(2)}, u32[]{:S(2)}) %collective-permute-start.11) | collective-permute-done | bytes 131104 | tf_op jit(solution)/shard_map/ppermute | solution.py:333
  44.4 2.8 %collective-permute-done.12.refs_7_ = bf16[2,128,256]{2,1,0:T(8,128)(2,1)S(1)} collective-permute-done((bf16[2,128,256]{2,1,0:T(8,128)(2,1)S(1)}, bf16[2,128,256]{2,1,0:T(8,128)(2,1)S(1)}, u32[]{:S(2)}, u32[]{:S(2)}) %collective-permute-start.12) | collective-permute-done | bytes 131104 | tf_op jit(solution)/shard_map/ppermute | solution.py:333
  47.2 0.0 collective-permute-start.14
  47.2 0.5 collective-permute-start.15
  47.7 0.8 %collective-permute-done.14.refs_8_ = bf16[2,128,256]{2,1,0:T(8,128)(2,1)S(1)} collective-permute-done((bf16[2,128,256]{2,1,0:T(8,128)(2,1)S(1)}, bf16[2,128,256]{2,1,0:T(8,128)(2,1)S(1)}, u32[]{:S(2)}, u32[]{:S(2)}) %collective-permute-start.14) | collective-permute-done | bytes 131104 | tf_op jit(solution)/shard_map/ppermute | solution.py:328
  48.6 0.2 collective-permute-done.15.refs_9_
  48.7 3.1 %convolve.2 = (bf16[128,1024]{1,0:T(8,128)(2,1)}, bf16[3,128,1024]{2,1,0:T(8,128)(2,1)}, f32[128,1024]{1,0:T(8,128)}) custom-call(s32[1]{0:T(128)} %bitcast.device_ref, bf16[1024,512]{1,0:T(8,128)(2,1)S(1)} %copy-done, bf16[128,1024]{1,0:T(8,128)(2,1)S(1)} %get-tuple-element.71.refs_1_, bf16[128,1024]{1,0:T(8,128)(2,1)S(1)} %copy-done.1, ...), custom_call_target="tpu_custom_call" | custom-call | flops 1048576 | bytes 65536 | tf_op jit(solution)/shard_map/convolve/pallas_call | solution.py:305
  51.8 0.6 collective-permute-done.13.refs_6_
  52.4 0.0 collective-permute-start.16
  52.4 1.5 %collective-permute-done.16.refs_7_ = bf16[2,128,512]{2,1,0:T(8,128)(2,1)S(1)} collective-permute-done((bf16[2,128,512]{2,1,0:T(8,128)(2,1)S(1)}, bf16[2,128,512]{2,1,0:T(8,128)(2,1)S(1)}, u32[]{:S(2)}, u32[]{:S(2)}) %collective-permute-start.16) | collective-permute-done | bytes 262176 | tf_op jit(solution)/shard_map/ppermute | solution.py:328
  53.9 3.1 %convolve.3 = (bf16[128,1024]{1,0:T(8,128)(2,1)}, bf16[3,128,1024]{2,1,0:T(8,128)(2,1)}, f32[128,1024]{1,0:T(8,128)}) custom-call(s32[1]{0:T(128)} %bitcast.device_ref, bf16[1024,512]{1,0:T(8,128)(2,1)S(1)} %copy-done, bf16[128,1024]{1,0:T(8,128)(2,1)S(1)} %get-tuple-element.71.refs_1_, ...), custom_call_target="tpu_custom_call", output_to_operand_aliasing={{0}: (9, {}), {1}: (10, {}), {2}: (11, {})} | custom-call | flops 1048576 | bytes 65536 | tf_op jit(solution)/shard_map/convolve/pallas_call | solution.py:305
Async XLA Ops:
  0.6 9.5 %collective-permute-start = (bf16[128,1024]{1,0:T(8,128)(2,1)}, bf16[128,1024]{1,0:T(8,128)(2,1)S(1)}, u32[]{:S(2)}, u32[]{:S(2)}) collective-permute-start(bf16[128,1024]{1,0:T(8,128)(2,1)} %refs_0_.3), channel_id=1, source_target_pairs={{0,2},{2,4},{4,6},{6,7},{7,5},{5,3},{3,1},{1,0},{8,10},{10,12},{12... | collective-permute-start | bytes 786440 | tf_op jit(solution)/shard_map/ppermute | solution.py:356
  3.7 8.0 %collective-permute-start.1 = (bf16[128,1024]{1,0:T(8,128)(2,1)}, bf16[128,1024]{1,0:T(8,128)(2,1)S(1)}, u32[]{:S(2)}, u32[]{:S(2)}) collective-permute-start(bf16[128,1024]{1,0:T(8,128)(2,1)} %refs_0_.3), channel_id=1, source_target_pairs={{2,0},{4,2},{6,4},{7,6},{5,7},{3,5},{1,3},{0,1},{10,8},{12,10},{14... | collective-permute-start | bytes 786440 | tf_op jit(solution)/shard_map/ppermute | solution.py:358
  11.7 7.5 %collective-permute-start.2 = (bf16[128,1024]{1,0:T(8,128)(2,1)S(1)}, bf16[128,1024]{1,0:T(8,128)(2,1)S(1)}, u32[]{:S(2)}, u32[]{:S(2)}) collective-permute-start(bf16[128,1024]{1,0:T(8,128)(2,1)S(1)} %collective-permute-done.refs_0_), channel_id=1, source_target_pairs={{0,2},{2,4},{4,6},{6,7},{7,5},{5,3},{3,1},{1,0},{8,10},{10,12},{12... | collective-permute-start | bytes 786440 | tf_op jit(solution)/shard_map/ppermute | solution.py:356
  13.3 6.6 %collective-permute-start.3 = (bf16[128,1024]{1,0:T(8,128)(2,1)S(1)}, bf16[128,1024]{1,0:T(8,128)(2,1)S(1)}, u32[]{:S(2)}, u32[]{:S(2)}) collective-permute-start(bf16[128,1024]{1,0:T(8,128)(2,1)S(1)} %collective-permute-done.1.refs_3_), channel_id=1, source_target_pairs={{2,0},{4,2},{6,4},{7,6},{5,7},{3,5},{1,3},{0,1},{10,8},{12,10},{14... | collective-permute-start | bytes 786440 | tf_op jit(solution)/shard_map/ppermute | solution.py:358
  19.8 7.4 %collective-permute-start.4 = (bf16[128,1024]{1,0:T(8,128)(2,1)S(1)}, bf16[128,1024]{1,0:T(8,128)(2,1)S(1)}, u32[]{:S(2)}, u32[]{:S(2)}) collective-permute-start(bf16[128,1024]{1,0:T(8,128)(2,1)S(1)} %collective-permute-done.2.refs_0_), channel_id=1, source_target_pairs={{0,2},{2,4},{4,6},{6,7},{7,5},{5,3},{3,1},{1,0},{8,10},{10,12},{12... | collective-permute-start | bytes 786440 | tf_op jit(solution)/shard_map/ppermute | solution.py:356
  21.4 6.4 %collective-permute-start.5 = (bf16[128,1024]{1,0:T(8,128)(2,1)S(1)}, bf16[128,1024]{1,0:T(8,128)(2,1)S(1)}, u32[]{:S(2)}, u32[]{:S(2)}) collective-permute-start(bf16[128,1024]{1,0:T(8,128)(2,1)S(1)} %collective-permute-done.3.refs_3_), channel_id=1, source_target_pairs={{2,0},{4,2},{6,4},{7,6},{5,7},{3,5},{1,3},{0,1},{10,8},{12,10},{14... | collective-permute-start | bytes 786440 | tf_op jit(solution)/shard_map/ppermute | solution.py:358
  27.8 8.4 %collective-permute-start.6 = (bf16[128,1024]{1,0:T(8,128)(2,1)S(1)}, bf16[128,1024]{1,0:T(8,128)(2,1)S(1)}, u32[]{:S(2)}, u32[]{:S(2)}) collective-permute-start(bf16[128,1024]{1,0:T(8,128)(2,1)S(1)} %collective-permute-done.4.refs_0_), channel_id=1, source_target_pairs={{0,2},{2,4},{4,6},{6,7},{7,5},{5,3},{3,1},{1,0},{8,10},{10,12},{12... | collective-permute-start | bytes 786440 | tf_op jit(solution)/shard_map/ppermute | solution.py:356
  29.3 6.9 %collective-permute-start.7 = (bf16[128,1024]{1,0:T(8,128)(2,1)S(1)}, bf16[128,1024]{1,0:T(8,128)(2,1)S(1)}, u32[]{:S(2)}, u32[]{:S(2)}) collective-permute-start(bf16[128,1024]{1,0:T(8,128)(2,1)S(1)} %convert_element_type.3.refs_0_), channel_id=1, source_target_pairs={{0,16},{8,24},{16,0},{24,8},{1,17},{9,25},{17,1},{25,9},{2,18},{10... | collective-permute-start | bytes 786440 | tf_op jit(solution)/shard_map/ppermute | solution.py:333
  30.8 5.4 %copy-start.1 = (bf16[128,1024]{1,0:T(8,128)(2,1)S(1)}, bf16[128,1024]{1,0:T(8,128)(2,1)}, u32[]{:S(2)}) copy-start(bf16[128,1024]{1,0:T(8,128)(2,1)} %refs_2_.3) | copy-start | bytes 786436
  36.2 4.8 %copy-start = (bf16[1024,512]{1,0:T(8,128)(2,1)S(1)}, bf16[1024,512]{1,0:T(8,128)(2,1)}, u32[]{:S(2)}) copy-start(bf16[1024,512]{1,0:T(8,128)(2,1)} %constant.12.clone.table_ref.refs_0_) | copy-start | bytes 3145732
  37.4 3.6 %collective-permute-start.10 = (bf16[2,128,1024]{2,1,0:T(8,128)(2,1)S(1)}, bf16[2,128,1024]{2,1,0:T(8,128)(2,1)S(1)}, u32[]{:S(2)}, u32[]{:S(2)}) collective-permute-start(bf16[2,128,1024]{2,1,0:T(8,128)(2,1)S(1)} %get-tuple-element.70.refs_4_), channel_id=1, source_target_pairs={{0,8},{8,0},{16,24},{24,16},{1,9},{9,1},{17,25},{25,17},{2,10},{10... | collective-permute-start | bytes 1572872 | tf_op jit(solution)/shard_map/ppermute | solution.py:328
  37.5 2.6 %collective-permute-start.8 = (bf16[128,1024]{1,0:T(8,128)(2,1)S(1)}, bf16[128,1024]{1,0:T(8,128)(2,1)S(1)}, u32[]{:S(2)}, u32[]{:S(2)}) collective-permute-start(bf16[128,1024]{1,0:T(8,128)(2,1)S(1)} %convert_element_type.3.refs_0_), channel_id=1, source_target_pairs={{0,8},{8,0},{16,24},{24,16},{1,9},{9,1},{17,25},{25,17},{2,10},{10... | collective-permute-start | bytes 786440 | tf_op jit(solution)/shard_map/ppermute | solution.py:328
  38.0 3.0 %collective-permute-start.9 = (bf16[128,1024]{1,0:T(8,128)(2,1)S(1)}, bf16[128,1024]{1,0:T(8,128)(2,1)S(1)}, u32[]{:S(2)}, u32[]{:S(2)}) collective-permute-start(bf16[128,1024]{1,0:T(8,128)(2,1)S(1)} %collective-permute-done.7.refs_1_), channel_id=1, source_target_pairs={{0,8},{8,0},{16,24},{24,16},{1,9},{9,1},{17,25},{25,17},{2,10},{10... | collective-permute-start | bytes 786440 | tf_op jit(solution)/shard_map/ppermute | solution.py:328
  38.1 6.3 %collective-permute-start.11 = (bf16[2,128,256]{2,1,0:T(8,128)(2,1)S(1)}, bf16[2,128,256]{2,1,0:T(8,128)(2,1)S(1)}, u32[]{:S(2)}, u32[]{:S(2)}) collective-permute-start(bf16[2,128,256]{2,1,0:T(8,128)(2,1)S(1)} %get-tuple-element.74), channel_id=1, source_target_pairs={{0,16},{8,24},{16,0},{24,8},{1,17},{9,25},{17,1},{25,9},{2,18},{10... | collective-permute-start | bytes 393224 | tf_op jit(solution)/shard_map/ppermute | solution.py:333
  39.0 8.2 %collective-permute-start.12 = (bf16[2,128,256]{2,1,0:T(8,128)(2,1)S(1)}, bf16[2,128,256]{2,1,0:T(8,128)(2,1)S(1)}, u32[]{:S(2)}, u32[]{:S(2)}) collective-permute-start(bf16[2,128,256]{2,1,0:T(8,128)(2,1)S(1)} %get-tuple-element.75), channel_id=1, source_target_pairs={{0,16},{8,24},{16,0},{24,8},{1,17},{9,25},{17,1},{25,9},{2,18},{10... | collective-permute-start | bytes 393224 | tf_op jit(solution)/shard_map/ppermute | solution.py:333
  40.1 12.2 %collective-permute-start.13 = (bf16[2,128,512]{2,1,0:T(8,128)(2,1)S(1)}, bf16[2,128,512]{2,1,0:T(8,128)(2,1)S(1)}, u32[]{:S(2)}, u32[]{:S(2)}) collective-permute-start(bf16[2,128,512]{2,1,0:T(8,128)(2,1)S(1)} %get-tuple-element.78), channel_id=1, source_target_pairs={{0,16},{8,24},{16,0},{24,8},{1,17},{9,25},{17,1},{25,9},{2,18},{10... | collective-permute-start | bytes 786440 | tf_op jit(solution)/shard_map/ppermute | solution.py:333
  47.2 1.3 %collective-permute-start.14 = (bf16[2,128,256]{2,1,0:T(8,128)(2,1)S(1)}, bf16[2,128,256]{2,1,0:T(8,128)(2,1)S(1)}, u32[]{:S(2)}, u32[]{:S(2)}) collective-permute-start(bf16[2,128,256]{2,1,0:T(8,128)(2,1)S(1)} %collective-permute-done.11.refs_6_), channel_id=1, source_target_pairs={{0,8},{8,0},{16,24},{24,16},{1,9},{9,1},{17,25},{25,17},{2,10},{10... | collective-permute-start | bytes 393224 | tf_op jit(solution)/shard_map/ppermute | solution.py:328
  47.2 1.5 %collective-permute-start.15 = (bf16[2,128,256]{2,1,0:T(8,128)(2,1)S(1)}, bf16[2,128,256]{2,1,0:T(8,128)(2,1)S(1)}, u32[]{:S(2)}, u32[]{:S(2)}) collective-permute-start(bf16[2,128,256]{2,1,0:T(8,128)(2,1)S(1)} %collective-permute-done.12.refs_7_), channel_id=1, source_target_pairs={{0,8},{8,0},{16,24},{24,16},{1,9},{9,1},{17,25},{25,17},{2,10},{10... | collective-permute-start | bytes 393224 | tf_op jit(solution)/shard_map/ppermute | solution.py:328
  52.4 1.5 %collective-permute-start.16 = (bf16[2,128,512]{2,1,0:T(8,128)(2,1)S(1)}, bf16[2,128,512]{2,1,0:T(8,128)(2,1)S(1)}, u32[]{:S(2)}, u32[]{:S(2)}) collective-permute-start(bf16[2,128,512]{2,1,0:T(8,128)(2,1)S(1)} %collective-permute-done.13.refs_6_), channel_id=1, source_target_pairs={{0,8},{8,0},{16,24},{24,16},{1,9},{9,1},{17,25},{25,17},{2,10},{10... | collective-permute-start | bytes 786440 | tf_op jit(solution)/shard_map/ppermute | solution.py:328

commit v3 on v2

--- a/solution.py
+++ b/solution.py
@@ -125,8 +125,8 @@
     )(*operands)
 
 
-def last_kernel(cuts, total_ref, grad_ref, x_ref, weight_ref, proj_ref, whole_ref, *chunk_refs):
-    for chunk_ref, columns in zip(chunk_refs, cuts):
+def last_kernel(cuts, total_ref, grad_ref, x_ref, weight_ref, proj_ref, whole_ref, *piece_refs):
+    for piece_ref, columns in zip(piece_refs, cuts):
         streams = []
         for j in range(3):
             value = total_ref[j, :, columns] + dot(x_ref[...], weight_ref[j, :, columns])
@@ -135,7 +135,7 @@
             streams.append(value.astype(F32))
         source = (streams[0] * streams[2]).astype(BF16)
         grad = (grad_ref[:, columns].astype(F32) * streams[1]).astype(BF16)
-        for ref, place in ((whole_ref, columns), (chunk_ref, slice(None))):
+        for ref, place in ((whole_ref, columns), (piece_ref, slice(None))):
             ref[0, :, place] = source
             ref[1, :, place] = grad
 
@@ -166,11 +166,11 @@
     return jnp.asarray(table.astype(jnp.bfloat16))
 
 
-def chip_rows(owner, ref, other_ref, columns):
+def chip_rows(owner, ref, other_ref):
     first = lax.rem(owner, 2) == 0
     signals = []
     for signal in range(2):
-        mine, others = ref[signal, :, columns], other_ref[signal, :, columns]
+        mine, others = ref[signal], other_ref[signal]
         signals.append(
             jnp.concatenate([jnp.where(first, mine, others), jnp.where(first, others, mine)], axis=0)
         )
@@ -182,7 +182,8 @@
 
 
 def spectra_kernel(chans, groups, device_ref, table_ref, *refs):
-    tap_refs, (own_ref, other_ref, filt_ref, near_ref, back_ref, taps) = refs[:groups], refs[groups:]
+    tap_refs, (own_ref, *other_refs) = refs[:groups], refs[groups:-4]
+    filt_ref, near_ref, back_ref, taps = refs[-4:]
     rows, width = tap_refs[0].shape
     tile = divisor(width, 256)
     chips = groups // 2
@@ -200,17 +201,22 @@
     back_ref[...] = (mine.astype(F32).T * (1.0 / length)).astype(BF16)
     table = chip_table(table_ref, owner, rows)
     for start in range(0, width, tile):
-        held = chip_rows(owner, own_ref, other_ref, slice(start, start + tile))
+        piece, offset = divmod(start, other_refs[0].shape[2])
+        held = chip_rows(
+            owner,
+            own_ref.at[:, :, start : start + tile],
+            other_refs[piece].at[:, :, offset : offset + tile],
+        )
         near_ref[:, 2 * start : 2 * start + 2 * tile] = dot(table, held)
 
 
-def spectra(device, chans, table, taps, pair, other_pair):
+def spectra(device, chans, table, taps, pair, other_pieces):
     rows, width = taps[0].shape
     bins, length = table.shape
     size = 2 * table.size + 4 * length * width + 40 * rows * width + 2**21
     return pl.pallas_call(
         functools.partial(spectra_kernel, chans, len(taps)),
-        in_specs=[SMEM] + [VMEM] * (3 + len(taps)),
+        in_specs=[SMEM] + [VMEM] * (2 + len(taps) + len(other_pieces)),
         out_specs=[VMEM] * 3,
         out_shape=[
             pltpu.VMEM((bins, width), F32),
@@ -221,7 +227,7 @@
         compiler_params=params(mebibytes_for(size)),
         cost_estimate=pl.CostEstimate(flops=2**20, bytes_accessed=2**16, transcendentals=0),
         name="spectra",
-    )(device, table, *taps, pair, other_pair)
+    )(device, table, *taps, pair, *other_pieces)
 
 
 def conv_kernel(chans, groups, pieces, first, tile, aliased, device_ref, *refs):
@@ -244,9 +250,8 @@
         for chip, owner in enumerate(owners):
             held = chip_rows(
                 owner,
-                far_refs[chip * pieces + piece],
-                far_refs[(chips + chip) * pieces + piece],
-                slice(offset, offset + tile),
+                far_refs[chip * pieces + piece].at[:, :, offset : offset + tile],
+                far_refs[(chips + chip) * pieces + piece].at[:, :, offset : offset + tile],
             )
             both = both + dot(chip_table(table_ref, owner, rows), held)
         src_re, src_im = both[:bins, :tile], both[bins:, :tile]
@@ -371,33 +376,17 @@
 
     table = transform_table(length)
     edge = width // 2
-    cuts = [slice(0, edge), slice(edge, width)] if edge % 256 == 0 else [slice(0, width)]
-    pieces = [slice(0, edge // 2), slice(edge // 2, edge)] + cuts[1:] if len(cuts) > 1 else cuts
+    pieces = [slice(0, edge), slice(edge, width)] if edge % 256 == 0 else [slice(0, width)]
     proj, pair, *parts = last_block(total, grad_out, last, weights, pieces)
-    fars = [from_other_chips(part, groups) for part in parts]
-    filt, near, back = spectra(
-        device,
-        chans,
-        table,
-        taps + [to_other_core(block, groups) for block in taps],
-        pair,
-        to_other_core(pair, groups),
+    far = from_other_chips(pair, groups)
+    taps = taps + [to_other_core(block, groups) for block in taps]
+    others = [to_other_core(part, groups) for part in parts]
+    filt, near, back = spectra(device, chans, table, taps, pair, others)
+    *far, near = lax.optimization_barrier((*far, near))
+    far = far + [to_other_core(block, groups) for block in far]
+    outs = convolve(
+        device, chans, groups, table, back, grad_out, proj, filt, near, far, 1, None, slice(0, width)
     )
-    outs = None
-    for cut in cuts:
-        far = [fars.pop(0) for piece in pieces if cut.start <= piece.start < cut.stop]
-        count = len(far)
-        far = [block for blocks in zip(*far) for block in blocks]
-        if outs:
-            *far, outs[2] = lax.optimization_barrier((*far, outs[2]))
-        else:
-            *far, near = lax.optimization_barrier((*far, near))
-        far = far + [to_other_core(block, groups) for block in far]
-        outs = list(
-            convolve(
-                device, chans, groups, table, back, grad_out, proj, filt, near, far, count, outs, cut
-            )
-        )
     gated_out, grad_proj, grad_filter = outs
     return gated_out, jnp.transpose(grad_proj, (1, 0, 2)), grad_filter
 

time: 57.3 us -> 55.2 us (0.963)
  starting transfers between devices: 14.3 us -> 12.4 us
  Pallas kernels: 30.6 us -> 29.9 us
    ppermute x4 -> x2, starting transfers between devices: 4.44 us -> 2.71 us  [from_other_chips(): lax.ppermute(value, 'seq', [(i, (i + 2 * d) % groups) for i in range(grou...]
    ppermute x6 -> x5, waiting for transfers between devices: 2.56 us -> 3.54 us  [to_other_core(): return lax.ppermute(value, 'seq', [(i, i ^ 1) for i in range(groups)])]
    pallas_call x2 -> x1, Pallas kernels: 6.12 us -> 5.38 us  [convolve(): pl.pallas_call(functools.partial(conv_kernel, chans, groups, pieces, cut....]
    ppermute x4 -> x2, waiting for transfers between devices: 4.28 us -> 3.78 us  [from_other_chips(): lax.ppermute(value, 'seq', [(i, (i + 2 * d) % groups) for i in range(grou...]
    ppermute x6 -> x5, starting transfers between devices: 1.16 us -> 1.02 us  [to_other_core(): return lax.ppermute(value, 'seq', [(i, i ^ 1) for i in range(groups)])]
  transfers between devices with their start and end apart: 17 -> 14, of which waited for: 10 -> 10; matrix products, arithmetic and copies ran while one was open for 2% -> 2% of each run, Pallas kernels for 46% -> 43%
where the time goes in v3:
time: 55.2 us; the launch traced here: 55 us
  Pallas kernels  29.9 us (54%)
  starting transfers between devices  12.4 us (22%)
  waiting for transfers between devices  10.7 us (19%)
  other arithmetic  1.07 us (2%)
  between operations  0.91 us (2%)
    pallas_call x4, Pallas kernels, add_blocks(): pl.pallas_call(functools.partial(blocks_kernel, chans, offsets, not own,...  21 us
    ppermute x4, starting transfers between devices, per_device(): next_up = lax.ppermute(up, 'chan', forward)  7.75 us
    pallas_call x1, Pallas kernels, convolve(): pl.pallas_call(functools.partial(conv_kernel, chans, groups, pieces, cut....  5.38 us
    ppermute x2, waiting for transfers between devices, from_other_chips(): lax.ppermute(value, 'seq', [(i, (i + 2 * d) % groups) for i in range(grou...  3.78 us
    ppermute x5, waiting for transfers between devices, to_other_core(): return lax.ppermute(value, 'seq', [(i, i ^ 1) for i in range(groups)])  3.54 us
    ppermute x2, starting transfers between devices, from_other_chips(): lax.ppermute(value, 'seq', [(i, (i + 2 * d) % groups) for i in range(grou...  2.71 us
    ppermute x3, waiting for transfers between devices, per_device(): next_down = lax.ppermute(down, 'chan', reverse)  2.69 us
    pallas_call x1, Pallas kernels, spectra(): pl.pallas_call(functools.partial(spectra_kernel, chans, len(taps)), in_sp...  2.43 us
  transfers between devices with their start and end apart: 14, of which 10 were waited for; matrix products, arithmetic and copies ran while one was open for 2% of the time, Pallas kernels for 43%

profile of v3, /device:TPU:0, one launch (start us, length us, event | category | flops | bytes accessed | tf_op | source)
XLA Modules:
  0.0 55.0 jit_solution(10518518834189837764)
XLA Ops:
  0.6 3.1 %collective-permute-start = (bf16[128,1024]{1,0:T(8,128)(2,1)}, bf16[128,1024]{1,0:T(8,128)(2,1)S(1)}, u32[]{:S(2)}, u32[]{:S(2)}) collective-permute-start(bf16[128,1024]{1,0:T(8,128)(2,1)} %refs_0_.2), channel_id=1, source_target_pairs={{0,2},{2,4},{4,6},{6,7},{7,5},{5,3},{3,1},{1,0},{8,10},{10,12},{12... | collective-permute-start | bytes 786440 | tf_op jit(solution)/shard_map/ppermute | solution.py:361
  3.7 0.0 collective-permute-start.1
  3.7 1.1 %convert_element_type.3.refs_0_ = bf16[128,1024]{1,0:T(8,128)(2,1)S(1)} convert(f32[128,1024]{1,0:T(8,128)} %param.7) | non-fusion elementwise | flops 131072 | bytes 786432 | tf_op jit(solution)/shard_map/convert_element_type | solution.py:365
  4.8 4.7 %add_blocks.4 = (f32[3,128,1024]{2,1,0:T(8,128)S(1)}, bf16[3,1024,1024]{2,1,0:T(8,128)(2,1)S(1)}) custom-call(s32[1]{0:T(128)} %bitcast.device_ref, bf16[128,1024]{1,0:T(8,128)(2,1)} %refs_0_.2, bf16[3,8192,1024]{2,1,0:T(8,128)(2,1)} %bitcast.3), custom_call_target="tpu_custom_call" | custom-call | flops 1610612736 | bytes 12582912 | tf_op jit(solution)/shard_map/add_blocks/pallas_call | solution.py:113
  9.5 0.6 %collective-permute-done.refs_0_ = bf16[128,1024]{1,0:T(8,128)(2,1)S(1)} collective-permute-done((bf16[128,1024]{1,0:T(8,128)(2,1)}, bf16[128,1024]{1,0:T(8,128)(2,1)S(1)}, u32[]{:S(2)}, u32[]{:S(2)}) %collective-permute-start) | collective-permute-done | bytes 262176 | tf_op jit(solution)/shard_map/ppermute | solution.py:361
  10.2 1.5 %collective-permute-done.1.refs_3_ = bf16[128,1024]{1,0:T(8,128)(2,1)S(1)} collective-permute-done((bf16[128,1024]{1,0:T(8,128)(2,1)}, bf16[128,1024]{1,0:T(8,128)(2,1)S(1)}, u32[]{:S(2)}, u32[]{:S(2)}) %collective-permute-start.1) | collective-permute-done | bytes 262176 | tf_op jit(solution)/shard_map/ppermute | solution.py:363
  11.7 1.6 %collective-permute-start.2 = (bf16[128,1024]{1,0:T(8,128)(2,1)S(1)}, bf16[128,1024]{1,0:T(8,128)(2,1)S(1)}, u32[]{:S(2)}, u32[]{:S(2)}) collective-permute-start(bf16[128,1024]{1,0:T(8,128)(2,1)S(1)} %collective-permute-done.refs_0_), channel_id=1, source_target_pairs={{0,2},{2,4},{4,6},{6,7},{7,5},{5,3},{3,1},{1,0},{8,10},{10,12},{12... | collective-permute-start | bytes 786440 | tf_op jit(solution)/shard_map/ppermute | solution.py:361
  13.3 0.4 collective-permute-start.3
  13.7 5.4 %add_blocks.5 = (f32[3,128,1024]{2,1,0:T(8,128)S(1)}, bf16[3,1024,1024]{2,1,0:T(8,128)(2,1)S(1)}) custom-call(s32[1]{0:T(128)} %bitcast.device_ref, bf16[128,1024]{1,0:T(8,128)(2,1)S(1)} %collective-permute-done.refs_0_, bf16[3,1024,1024]{2,1,0:T(8,128)(2,1)S(1)} %get-tuple-element.42.refs_1_, ...), custom_call_target="tpu_custom_call", output_to_operand_aliasing={{0}: (3, {})} | custom-call | flops 1610612736 | bytes 12582912 | tf_op jit(solution)/shard_map/add_blocks/pallas_call | solution.py:113
  19.1 0.0 collective-permute-done.2.refs_0_
  19.1 0.7 %collective-permute-done.3.refs_3_ = bf16[128,1024]{1,0:T(8,128)(2,1)S(1)} collective-permute-done((bf16[128,1024]{1,0:T(8,128)(2,1)S(1)}, bf16[128,1024]{1,0:T(8,128)(2,1)S(1)}, u32[]{:S(2)}, u32[]{:S(2)}) %collective-permute-start.3) | collective-permute-done | bytes 262176 | tf_op jit(solution)/shard_map/ppermute | solution.py:363
  19.8 1.6 %collective-permute-start.4 = (bf16[128,1024]{1,0:T(8,128)(2,1)S(1)}, bf16[128,1024]{1,0:T(8,128)(2,1)S(1)}, u32[]{:S(2)}, u32[]{:S(2)}) collective-permute-start(bf16[128,1024]{1,0:T(8,128)(2,1)S(1)} %collective-permute-done.2.refs_0_), channel_id=1, source_target_pairs={{0,2},{2,4},{4,6},{6,7},{7,5},{5,3},{3,1},{1,0},{8,10},{10,12},{12... | collective-permute-start | bytes 786440 | tf_op jit(solution)/shard_map/ppermute | solution.py:361
  21.4 0.4 collective-permute-start.5
  21.9 5.4 %add_blocks.6 = (f32[3,128,1024]{2,1,0:T(8,128)S(1)}, bf16[3,1024,1024]{2,1,0:T(8,128)(2,1)S(1)}) custom-call(s32[1]{0:T(128)} %bitcast.device_ref, bf16[128,1024]{1,0:T(8,128)(2,1)S(1)} %collective-permute-done.2.refs_0_, bf16[3,1024,1024]{2,1,0:T(8,128)(2,1)S(1)} %get-tuple-element.48.refs_1_, ...), custom_call_target="tpu_custom_call", output_to_operand_aliasing={{0}: (3, {})} | custom-call | flops 1610612736 | bytes 12582912 | tf_op jit(solution)/shard_map/add_blocks/pallas_call | solution.py:113
  27.3 0.0 collective-permute-done.4.refs_0_
  27.3 0.5 collective-permute-done.5.refs_3_
  27.8 1.5 %collective-permute-start.6 = (bf16[128,1024]{1,0:T(8,128)(2,1)S(1)}, bf16[128,1024]{1,0:T(8,128)(2,1)S(1)}, u32[]{:S(2)}, u32[]{:S(2)}) collective-permute-start(bf16[128,1024]{1,0:T(8,128)(2,1)S(1)} %collective-permute-done.4.refs_0_), channel_id=1, source_target_pairs={{0,2},{2,4},{4,6},{6,7},{7,5},{5,3},{3,1},{1,0},{8,10},{10,12},{12... | collective-permute-start | bytes 786440 | tf_op jit(solution)/shard_map/ppermute | solution.py:361
  29.3 1.5 %collective-permute-start.7 = (bf16[128,1024]{1,0:T(8,128)(2,1)S(1)}, bf16[128,1024]{1,0:T(8,128)(2,1)S(1)}, u32[]{:S(2)}, u32[]{:S(2)}) collective-permute-start(bf16[128,1024]{1,0:T(8,128)(2,1)S(1)} %convert_element_type.3.refs_0_), channel_id=1, source_target_pairs={{0,16},{8,24},{16,0},{24,8},{1,17},{9,25},{17,1},{25,9},{2,18},{10... | collective-permute-start | bytes 786440 | tf_op jit(solution)/shard_map/ppermute | solution.py:338
  30.8 0.0 copy-start.1
  30.8 5.4 %add_blocks.7 = (f32[3,128,1024]{2,1,0:T(8,128)S(1)}, bf16[3,1024,1024]{2,1,0:T(8,128)(2,1)S(1)}) custom-call(s32[1]{0:T(128)} %bitcast.device_ref, bf16[128,1024]{1,0:T(8,128)(2,1)S(1)} %collective-permute-done.4.refs_0_, bf16[3,1024,1024]{2,1,0:T(8,128)(2,1)S(1)} %get-tuple-element.53.refs_1_, ...), custom_call_target="tpu_custom_call", output_to_operand_aliasing={{0}: (3, {})} | custom-call | flops 1610612736 | bytes 12582912 | tf_op jit(solution)/shard_map/add_blocks/pallas_call | solution.py:113
  36.2 0.0 copy-start
  36.2 0.0 collective-permute-done.6.x_ref
  36.3 0.0 collective-permute-done.7.refs_1_
  36.3 0.0 copy-done.1
  36.3 1.2 %last_block.1 = (bf16[3,128,1024]{2,1,0:T(8,128)(2,1)S(1)}, bf16[2,128,1024]{2,1,0:T(8,128)(2,1)S(1)}, bf16[2,128,512]{2,1,0:T(8,128)(2,1)S(1)}, bf16[2,128,512]{2,1,0:T(8,128)(2,1)S(1)}) custom-call(f32[3,128,1024]{2,1,0:T(8,128)S(1)} %get-tuple-element.60.total_ref, bf16[128,1024]{1,0:T(8,128)(2,1)S(1)} %copy-done.1, ...), custom_call_target="tpu_custom_call" | custom-call | flops 805306368 | bytes 1048576 | tf_op jit(solution)/shard_map/last_block/pallas_call | solution.py:147
  37.5 1.2 %collective-permute-start.12 = (bf16[2,128,1024]{2,1,0:T(8,128)(2,1)S(1)}, bf16[2,128,1024]{2,1,0:T(8,128)(2,1)S(1)}, u32[]{:S(2)}, u32[]{:S(2)}) collective-permute-start(bf16[2,128,1024]{2,1,0:T(8,128)(2,1)S(1)} %get-tuple-element.63.refs_4_), channel_id=1, source_target_pairs={{0,16},{8,24},{16,0},{24,8},{1,17},{9,25},{17,1},{25,9},{2,18},{10... | collective-permute-start | bytes 1572872 | tf_op jit(solution)/shard_map/ppermute | solution.py:338
  38.7 0.0 collective-permute-start.10
  38.7 0.5 collective-permute-start.11
  39.2 0.0 collective-permute-start.8
  39.2 0.5 collective-permute-start.9
  39.7 0.5 collective-permute-done.10.refs_5_
  40.2 0.4 collective-permute-done.11.refs_6_
  40.6 0.4 collective-permute-done.8.refs_2_
  41.0 0.4 collective-permute-done.9.refs_3_
  41.3 0.0 copy-done
  41.3 2.4 %spectra.1 = (f32[1024,1024]{1,0:T(8,128)S(1)}, f32[1024,2048]{1,0:T(8,128)S(1)}, bf16[128,1024]{1,0:T(8,128)(2,1)S(1)}) custom-call(s32[1]{0:T(128)} %bitcast.device_ref, bf16[1024,512]{1,0:T(8,128)(2,1)S(1)} %copy-done, bf16[128,1024]{1,0:T(8,128)(2,1)S(1)} %convert_element_type.3.refs_0_, bf16[128,1024]{1,0:T(8,128)(2,1)S(1)} %collective-permute-done.7.refs_1_, ...), custom_call_target="tpu_custom_call" | custom-call | flops 1048576 | bytes 65536 | tf_op jit(solution)/shard_map/spectra/pallas_call | solution.py:217
  43.8 3.8 %collective-permute-done.12.refs_6_ = bf16[2,128,1024]{2,1,0:T(8,128)(2,1)S(1)} collective-permute-done((bf16[2,128,1024]{2,1,0:T(8,128)(2,1)S(1)}, bf16[2,128,1024]{2,1,0:T(8,128)(2,1)S(1)}, u32[]{:S(2)}, u32[]{:S(2)}) %collective-permute-start.12) | collective-permute-done | bytes 524320 | tf_op jit(solution)/shard_map/ppermute | solution.py:338
  47.5 0.0 collective-permute-start.13
  47.5 1.9 %collective-permute-done.13.refs_7_ = bf16[2,128,1024]{2,1,0:T(8,128)(2,1)S(1)} collective-permute-done((bf16[2,128,1024]{2,1,0:T(8,128)(2,1)S(1)}, bf16[2,128,1024]{2,1,0:T(8,128)(2,1)S(1)}, u32[]{:S(2)}, u32[]{:S(2)}) %collective-permute-start.13) | collective-permute-done | bytes 524320 | tf_op jit(solution)/shard_map/ppermute | solution.py:333
  49.5 5.4 %convolve.1 = (bf16[128,1024]{1,0:T(8,128)(2,1)}, bf16[3,128,1024]{2,1,0:T(8,128)(2,1)}, f32[128,1024]{1,0:T(8,128)}) custom-call(s32[1]{0:T(128)} %bitcast.device_ref, bf16[1024,512]{1,0:T(8,128)(2,1)S(1)} %copy-done, bf16[128,1024]{1,0:T(8,128)(2,1)S(1)} %get-tuple-element.66.refs_1_, bf16[128,1024]{1,0:T(8,128)(2,1)S(1)} %copy-done.1, ...), custom_call_target="tpu_custom_call" | custom-call | flops 1048576 | bytes 65536 | tf_op jit(solution)/shard_map/convolve/pallas_call | solution.py:310
Async XLA Ops:
  0.6 9.5 %collective-permute-start = (bf16[128,1024]{1,0:T(8,128)(2,1)}, bf16[128,1024]{1,0:T(8,128)(2,1)S(1)}, u32[]{:S(2)}, u32[]{:S(2)}) collective-permute-start(bf16[128,1024]{1,0:T(8,128)(2,1)} %refs_0_.2), channel_id=1, source_target_pairs={{0,2},{2,4},{4,6},{6,7},{7,5},{5,3},{3,1},{1,0},{8,10},{10,12},{12... | collective-permute-start | bytes 786440 | tf_op jit(solution)/shard_map/ppermute | solution.py:361
  3.7 8.0 %collective-permute-start.1 = (bf16[128,1024]{1,0:T(8,128)(2,1)}, bf16[128,1024]{1,0:T(8,128)(2,1)S(1)}, u32[]{:S(2)}, u32[]{:S(2)}) collective-permute-start(bf16[128,1024]{1,0:T(8,128)(2,1)} %refs_0_.2), channel_id=1, source_target_pairs={{2,0},{4,2},{6,4},{7,6},{5,7},{3,5},{1,3},{0,1},{10,8},{12,10},{14... | collective-permute-start | bytes 786440 | tf_op jit(solution)/shard_map/ppermute | solution.py:363
  11.7 7.5 %collective-permute-start.2 = (bf16[128,1024]{1,0:T(8,128)(2,1)S(1)}, bf16[128,1024]{1,0:T(8,128)(2,1)S(1)}, u32[]{:S(2)}, u32[]{:S(2)}) collective-permute-start(bf16[128,1024]{1,0:T(8,128)(2,1)S(1)} %collective-permute-done.refs_0_), channel_id=1, source_target_pairs={{0,2},{2,4},{4,6},{6,7},{7,5},{5,3},{3,1},{1,0},{8,10},{10,12},{12... | collective-permute-start | bytes 786440 | tf_op jit(solution)/shard_map/ppermute | solution.py:361
  13.3 6.6 %collective-permute-start.3 = (bf16[128,1024]{1,0:T(8,128)(2,1)S(1)}, bf16[128,1024]{1,0:T(8,128)(2,1)S(1)}, u32[]{:S(2)}, u32[]{:S(2)}) collective-permute-start(bf16[128,1024]{1,0:T(8,128)(2,1)S(1)} %collective-permute-done.1.refs_3_), channel_id=1, source_target_pairs={{2,0},{4,2},{6,4},{7,6},{5,7},{3,5},{1,3},{0,1},{10,8},{12,10},{14... | collective-permute-start | bytes 786440 | tf_op jit(solution)/shard_map/ppermute | solution.py:363
  19.8 7.5 %collective-permute-start.4 = (bf16[128,1024]{1,0:T(8,128)(2,1)S(1)}, bf16[128,1024]{1,0:T(8,128)(2,1)S(1)}, u32[]{:S(2)}, u32[]{:S(2)}) collective-permute-start(bf16[128,1024]{1,0:T(8,128)(2,1)S(1)} %collective-permute-done.2.refs_0_), channel_id=1, source_target_pairs={{0,2},{2,4},{4,6},{6,7},{7,5},{5,3},{3,1},{1,0},{8,10},{10,12},{12... | collective-permute-start | bytes 786440 | tf_op jit(solution)/shard_map/ppermute | solution.py:361
  21.4 6.4 %collective-permute-start.5 = (bf16[128,1024]{1,0:T(8,128)(2,1)S(1)}, bf16[128,1024]{1,0:T(8,128)(2,1)S(1)}, u32[]{:S(2)}, u32[]{:S(2)}) collective-permute-start(bf16[128,1024]{1,0:T(8,128)(2,1)S(1)} %collective-permute-done.3.refs_3_), channel_id=1, source_target_pairs={{2,0},{4,2},{6,4},{7,6},{5,7},{3,5},{1,3},{0,1},{10,8},{12,10},{14... | collective-permute-start | bytes 786440 | tf_op jit(solution)/shard_map/ppermute | solution.py:363
  27.8 8.5 %collective-permute-start.6 = (bf16[128,1024]{1,0:T(8,128)(2,1)S(1)}, bf16[128,1024]{1,0:T(8,128)(2,1)S(1)}, u32[]{:S(2)}, u32[]{:S(2)}) collective-permute-start(bf16[128,1024]{1,0:T(8,128)(2,1)S(1)} %collective-permute-done.4.refs_0_), channel_id=1, source_target_pairs={{0,2},{2,4},{4,6},{6,7},{7,5},{5,3},{3,1},{1,0},{8,10},{10,12},{12... | collective-permute-start | bytes 786440 | tf_op jit(solution)/shard_map/ppermute | solution.py:361
  29.3 7.0 %collective-permute-start.7 = (bf16[128,1024]{1,0:T(8,128)(2,1)S(1)}, bf16[128,1024]{1,0:T(8,128)(2,1)S(1)}, u32[]{:S(2)}, u32[]{:S(2)}) collective-permute-start(bf16[128,1024]{1,0:T(8,128)(2,1)S(1)} %convert_element_type.3.refs_0_), channel_id=1, source_target_pairs={{0,16},{8,24},{16,0},{24,8},{1,17},{9,25},{17,1},{25,9},{2,18},{10... | collective-permute-start | bytes 786440 | tf_op jit(solution)/shard_map/ppermute | solution.py:338
  30.8 5.5 %copy-start.1 = (bf16[128,1024]{1,0:T(8,128)(2,1)S(1)}, bf16[128,1024]{1,0:T(8,128)(2,1)}, u32[]{:S(2)}) copy-start(bf16[128,1024]{1,0:T(8,128)(2,1)} %refs_2_.1) | copy-start | bytes 786436
  36.2 5.1 %copy-start = (bf16[1024,512]{1,0:T(8,128)(2,1)S(1)}, bf16[1024,512]{1,0:T(8,128)(2,1)}, u32[]{:S(2)}) copy-start(bf16[1024,512]{1,0:T(8,128)(2,1)} %constant.12.clone.table_ref.refs_0_) | copy-start | bytes 3145732
  37.5 10.1 %collective-permute-start.12 = (bf16[2,128,1024]{2,1,0:T(8,128)(2,1)S(1)}, bf16[2,128,1024]{2,1,0:T(8,128)(2,1)S(1)}, u32[]{:S(2)}, u32[]{:S(2)}) collective-permute-start(bf16[2,128,1024]{2,1,0:T(8,128)(2,1)S(1)} %get-tuple-element.63.refs_4_), channel_id=1, source_target_pairs={{0,16},{8,24},{16,0},{24,8},{1,17},{9,25},{17,1},{25,9},{2,18},{10... | collective-permute-start | bytes 1572872 | tf_op jit(solution)/shard_map/ppermute | solution.py:338
  38.7 1.5 %collective-permute-start.10 = (bf16[2,128,512]{2,1,0:T(8,128)(2,1)S(1)}, bf16[2,128,512]{2,1,0:T(8,128)(2,1)S(1)}, u32[]{:S(2)}, u32[]{:S(2)}) collective-permute-start(bf16[2,128,512]{2,1,0:T(8,128)(2,1)S(1)} %get-tuple-element.64), channel_id=1, source_target_pairs={{0,8},{8,0},{16,24},{24,16},{1,9},{9,1},{17,25},{25,17},{2,10},{10... | collective-permute-start | bytes 786440 | tf_op jit(solution)/shard_map/ppermute | solution.py:333
  38.7 1.9 %collective-permute-start.11 = (bf16[2,128,512]{2,1,0:T(8,128)(2,1)S(1)}, bf16[2,128,512]{2,1,0:T(8,128)(2,1)S(1)}, u32[]{:S(2)}, u32[]{:S(2)}) collective-permute-start(bf16[2,128,512]{2,1,0:T(8,128)(2,1)S(1)} %get-tuple-element.65), channel_id=1, source_target_pairs={{0,8},{8,0},{16,24},{24,16},{1,9},{9,1},{17,25},{25,17},{2,10},{10... | collective-permute-start | bytes 786440 | tf_op jit(solution)/shard_map/ppermute | solution.py:333
  39.2 1.8 %collective-permute-start.8 = (bf16[128,1024]{1,0:T(8,128)(2,1)S(1)}, bf16[128,1024]{1,0:T(8,128)(2,1)S(1)}, u32[]{:S(2)}, u32[]{:S(2)}) collective-permute-start(bf16[128,1024]{1,0:T(8,128)(2,1)S(1)} %convert_element_type.3.refs_0_), channel_id=1, source_target_pairs={{0,8},{8,0},{16,24},{24,16},{1,9},{9,1},{17,25},{25,17},{2,10},{10... | collective-permute-start | bytes 786440 | tf_op jit(solution)/shard_map/ppermute | solution.py:333
  39.2 2.1 %collective-permute-start.9 = (bf16[128,1024]{1,0:T(8,128)(2,1)S(1)}, bf16[128,1024]{1,0:T(8,128)(2,1)S(1)}, u32[]{:S(2)}, u32[]{:S(2)}) collective-permute-start(bf16[128,1024]{1,0:T(8,128)(2,1)S(1)} %collective-permute-done.7.refs_1_), channel_id=1, source_target_pairs={{0,8},{8,0},{16,24},{24,16},{1,9},{9,1},{17,25},{25,17},{2,10},{10... | collective-permute-start | bytes 786440 | tf_op jit(solution)/shard_map/ppermute | solution.py:333
  47.5 1.9 %collective-permute-start.13 = (bf16[2,128,1024]{2,1,0:T(8,128)(2,1)S(1)}, bf16[2,128,1024]{2,1,0:T(8,128)(2,1)S(1)}, u32[]{:S(2)}, u32[]{:S(2)}) collective-permute-start(bf16[2,128,1024]{2,1,0:T(8,128)(2,1)S(1)} %collective-permute-done.12.refs_6_), channel_id=1, source_target_pairs={{0,8},{8,0},{16,24},{24,16},{1,9},{9,1},{17,25},{25,17},{2,10},{10... | collective-permute-start | bytes 1572872 | tf_op jit(solution)/shard_map/ppermute | solution.py:333

commit v4 on v3

--- a/solution.py
+++ b/solution.py
@@ -184,14 +184,14 @@
 def spectra_kernel(chans, groups, device_ref, table_ref, *refs):
     tap_refs, (own_ref, *other_refs) = refs[:groups], refs[groups:-4]
     filt_ref, near_ref, back_ref, taps = refs[-4:]
-    rows, width = tap_refs[0].shape
+    rows, width = own_ref.shape[1:]
     tile = divisor(width, 256)
     chips = groups // 2
     for number, ref in enumerate(tap_refs):
         owner = sequence_owner(device_ref[0], chans, groups, number % chips)
         if number >= chips:
             owner = owner + 1 - 2 * lax.rem(owner, 2)
-        taps[pl.ds(pl.multiple_of(owner * rows, 128), rows)] = ref[...]
+        taps[pl.ds(pl.multiple_of(owner * rows, 128), rows)] = ref[:rows]
     for start in range(0, width, tile):
         columns = slice(start, start + tile)
         filt_ref[:, columns] = dot(table_ref[...], taps[:, columns])
@@ -211,7 +211,7 @@
 
 
 def spectra(device, chans, table, taps, pair, other_pieces):
-    rows, width = taps[0].shape
+    rows, width = pair.shape[1:]
     bins, length = table.shape
     size = 2 * table.size + 4 * length * width + 40 * rows * width + 2**21
     return pl.pallas_call(
@@ -361,18 +361,24 @@
         next_up = lax.ppermute(up, "chan", forward)
         if step < steps:
             next_down = lax.ppermute(down, "chan", reverse)
-        if step == 1:
-            filt = long_filter.astype(BF16)
-        if step == steps:
-            taps = [filt] + from_other_chips(filt, groups)
         total, weights = add_blocks(
             device, chans, (step - 1, -step), total, first, x, weight
         )
+        taps = []
+        if step == 1:
+            total, filt = lax.optimization_barrier(
+                (total, jnp.concatenate([long_filter, long_filter[:16]], axis=0).astype(BF16))
+            )
+            filters = [filt] + from_other_chips(filt, groups)
+        if step == 2:
+            taps = filters
         if step < steps:
-            up, down, total, filt = lax.optimization_barrier((next_up, next_down, total, filt))
+            up, down, total, *taps = lax.optimization_barrier((next_up, next_down, total, *taps))
+            filters = taps or filters
             first, x = (up, in_vmem(weights)), down
         else:
-            last, total, *taps = lax.optimization_barrier((next_up, total, *taps))
+            last, total = lax.optimization_barrier((next_up, total))
+    taps = filters
 
     table = transform_table(length)
     edge = width // 2

time: 55.2 us -> 54.4 us (0.986)
  waiting for transfers between devices: 10.7 us -> 9.26 us
  starting transfers between devices: 12.4 us -> 13 us
    ppermute x3, waiting for transfers between devices: 2.69 us -> 1.56 us  [per_device(): next_down = lax.ppermute(down, 'chan', reverse)]
    another operation x0 -> x1, other arithmetic: none -> 1.07 us
    convert_element_type x1 -> x0, other arithmetic: 1.07 us -> none  [per_device(): filt = long_filter.astype(BF16)]
    ppermute x4, waiting for transfers between devices: 0.65 us -> 0.01 us  [per_device(): next_up = lax.ppermute(up, 'chan', forward)]
  transfers between devices with their start and end apart: 14 -> 14, of which waited for: 10 -> 9; matrix products, arithmetic and copies ran while one was open for 2% -> 2% of each run, Pallas kernels for 43% -> 43%
where the time goes in v4:
time: 54.4 us; the launch traced here: 54.2 us
  Pallas kernels  29.9 us (55%)
  starting transfers between devices  13 us (24%)
  waiting for transfers between devices  9.26 us (17%)
  other arithmetic  1.09 us (2%)
  between operations  0.92 us (2%)
    pallas_call x4, Pallas kernels, add_blocks(): pl.pallas_call(functools.partial(blocks_kernel, chans, offsets, not own,...  20.9 us
    ppermute x4, starting transfers between devices, per_device(): next_up = lax.ppermute(up, 'chan', forward)  7.81 us
    pallas_call x1, Pallas kernels, convolve(): pl.pallas_call(functools.partial(conv_kernel, chans, groups, pieces, cut....  5.37 us
    ppermute x2, waiting for transfers between devices, from_other_chips(): lax.ppermute(value, 'seq', [(i, (i + 2 * d) % groups) for i in range(grou...  4.05 us
    ppermute x5, waiting for transfers between devices, to_other_core(): return lax.ppermute(value, 'seq', [(i, i ^ 1) for i in range(groups)])  3.64 us
    ppermute x2, starting transfers between devices, from_other_chips(): lax.ppermute(value, 'seq', [(i, (i + 2 * d) % groups) for i in range(grou...  3.25 us
    pallas_call x1, Pallas kernels, spectra(): pl.pallas_call(functools.partial(spectra_kernel, chans, len(taps)), in_sp...  2.43 us
    ppermute x3, waiting for transfers between devices, per_device(): next_down = lax.ppermute(down, 'chan', reverse)  1.56 us
  transfers between devices with their start and end apart: 14, of which 9 were waited for; matrix products, arithmetic and copies ran while one was open for 2% of the time, Pallas kernels for 43%

profile of v4, /device:TPU:0, one launch (start us, length us, event | category | flops | bytes accessed | tf_op | source)
XLA Modules:
  0.0 54.2 jit_solution(5969480272589960757)
XLA Ops:
  0.6 3.1 %collective-permute-start = (bf16[128,1024]{1,0:T(8,128)(2,1)}, bf16[128,1024]{1,0:T(8,128)(2,1)S(1)}, u32[]{:S(2)}, u32[]{:S(2)}) collective-permute-start(bf16[128,1024]{1,0:T(8,128)(2,1)} %refs_0_.2), channel_id=1, source_target_pairs={{0,2},{2,4},{4,6},{6,7},{7,5},{5,3},{3,1},{1,0},{8,10},{10,12},{12... | collective-permute-start | bytes 786440 | tf_op jit(solution)/shard_map/ppermute | solution.py:361
  3.7 0.0 collective-permute-start.1
  3.7 1.1 %convert.5 = bf16[128,1024]{1,0:T(8,128)(2,1)S(1)} convert(f32[128,1024]{1,0:T(8,128)} %param.7) | non-fusion elementwise | flops 131072 | bytes 786432 | tf_op jit(solution)/shard_map/convert
  4.8 4.7 %add_blocks.4 = (f32[3,128,1024]{2,1,0:T(8,128)S(1)}, bf16[3,1024,1024]{2,1,0:T(8,128)(2,1)S(1)}) custom-call(s32[1]{0:T(128)} %bitcast.device_ref, bf16[128,1024]{1,0:T(8,128)(2,1)} %refs_0_.2, bf16[3,8192,1024]{2,1,0:T(8,128)(2,1)} %bitcast.3), custom_call_target="tpu_custom_call" | custom-call | flops 1610612736 | bytes 12582912 | tf_op jit(solution)/shard_map/add_blocks/pallas_call | solution.py:113
  9.6 2.0 %collective-permute-start.4 = (bf16[144,1024]{1,0:T(8,128)(2,1)S(1)}, bf16[144,1024]{1,0:T(8,128)(2,1)S(1)}, u32[]{:S(2)}, u32[]{:S(2)}) collective-permute-start(bf16[144,1024]{1,0:T(8,128)(2,1)S(1)} %pad_maximum_fusion.refs_0_), channel_id=1, source_target_pairs={{0,16},{8,24},{16,0},{24,8},{1,17},{9,25},{17,1},{25,9},{2,18},{10... | collective-permute-start | bytes 884744 | tf_op jit(solution)/shard_map/ppermute | solution.py:338
  11.6 0.0 collective-permute-done.refs_0_
  11.6 0.1 collective-permute-done.1.refs_3_
  11.7 1.6 %collective-permute-start.2 = (bf16[128,1024]{1,0:T(8,128)(2,1)S(1)}, bf16[128,1024]{1,0:T(8,128)(2,1)S(1)}, u32[]{:S(2)}, u32[]{:S(2)}) collective-permute-start(bf16[128,1024]{1,0:T(8,128)(2,1)S(1)} %collective-permute-done.refs_0_), channel_id=1, source_target_pairs={{0,2},{2,4},{4,6},{6,7},{7,5},{5,3},{3,1},{1,0},{8,10},{10,12},{12... | collective-permute-start | bytes 786440 | tf_op jit(solution)/shard_map/ppermute | solution.py:361
  13.3 0.4 collective-permute-start.3
  13.7 5.4 %add_blocks.5 = (f32[3,128,1024]{2,1,0:T(8,128)S(1)}, bf16[3,1024,1024]{2,1,0:T(8,128)(2,1)S(1)}) custom-call(s32[1]{0:T(128)} %bitcast.device_ref, bf16[128,1024]{1,0:T(8,128)(2,1)S(1)} %collective-permute-done.refs_0_, bf16[3,1024,1024]{2,1,0:T(8,128)(2,1)S(1)} %get-tuple-element.42.refs_1_, ...), custom_call_target="tpu_custom_call", output_to_operand_aliasing={{0}: (3, {})} | custom-call | flops 1610612736 | bytes 12582912 | tf_op jit(solution)/shard_map/add_blocks/pallas_call | solution.py:113
  19.1 0.0 collective-permute-done.4.refs_1_
  19.1 0.0 collective-permute-done.2.refs_0_
  19.2 0.9 %collective-permute-done.3.refs_3_ = bf16[128,1024]{1,0:T(8,128)(2,1)S(1)} collective-permute-done((bf16[128,1024]{1,0:T(8,128)(2,1)S(1)}, bf16[128,1024]{1,0:T(8,128)(2,1)S(1)}, u32[]{:S(2)}, u32[]{:S(2)}) %collective-permute-start.3) | collective-permute-done | bytes 262176 | tf_op jit(solution)/shard_map/ppermute | solution.py:363
  20.1 1.6 %collective-permute-start.7 = (bf16[128,1024]{1,0:T(8,128)(2,1)S(1)}, bf16[128,1024]{1,0:T(8,128)(2,1)S(1)}, u32[]{:S(2)}, u32[]{:S(2)}) collective-permute-start(bf16[128,1024]{1,0:T(8,128)(2,1)S(1)} %collective-permute-done.2.refs_0_), channel_id=1, source_target_pairs={{0,2},{2,4},{4,6},{6,7},{7,5},{5,3},{3,1},{1,0},{8,10},{10,12},{12... | collective-permute-start | bytes 786440 | tf_op jit(solution)/shard_map/ppermute | solution.py:361
  21.7 0.4 collective-permute-start.8
  22.1 5.4 %add_blocks.6 = (f32[3,128,1024]{2,1,0:T(8,128)S(1)}, bf16[3,1024,1024]{2,1,0:T(8,128)(2,1)S(1)}) custom-call(s32[1]{0:T(128)} %bitcast.device_ref, bf16[128,1024]{1,0:T(8,128)(2,1)S(1)} %collective-permute-done.2.refs_0_, bf16[3,1024,1024]{2,1,0:T(8,128)(2,1)S(1)} %get-tuple-element.50.refs_1_, ...), custom_call_target="tpu_custom_call", output_to_operand_aliasing={{0}: (3, {})} | custom-call | flops 1610612736 | bytes 12582912 | tf_op jit(solution)/shard_map/add_blocks/pallas_call | solution.py:113
  27.5 0.0 collective-permute-done.7.refs_0_
  27.5 0.5 collective-permute-done.8.refs_3_
  28.0 1.6 %collective-permute-start.9 = (bf16[128,1024]{1,0:T(8,128)(2,1)S(1)}, bf16[128,1024]{1,0:T(8,128)(2,1)S(1)}, u32[]{:S(2)}, u32[]{:S(2)}) collective-permute-start(bf16[128,1024]{1,0:T(8,128)(2,1)S(1)} %collective-permute-done.7.refs_0_), channel_id=1, source_target_pairs={{0,2},{2,4},{4,6},{6,7},{7,5},{5,3},{3,1},{1,0},{8,10},{10,12},{12... | collective-permute-start | bytes 786440 | tf_op jit(solution)/shard_map/ppermute | solution.py:361
  29.6 0.0 copy-start.1
  29.6 5.4 %add_blocks.7 = (f32[3,128,1024]{2,1,0:T(8,128)S(1)}, bf16[3,1024,1024]{2,1,0:T(8,128)(2,1)S(1)}) custom-call(s32[1]{0:T(128)} %bitcast.device_ref, bf16[128,1024]{1,0:T(8,128)(2,1)S(1)} %collective-permute-done.7.refs_0_, bf16[3,1024,1024]{2,1,0:T(8,128)(2,1)S(1)} %get-tuple-element.54.refs_1_, ...), custom_call_target="tpu_custom_call", output_to_operand_aliasing={{0}: (3, {})} | custom-call | flops 1610612736 | bytes 12582912 | tf_op jit(solution)/shard_map/add_blocks/pallas_call | solution.py:113
  35.0 0.0 copy-start
  35.1 0.0 collective-permute-done.9.x_ref
  35.1 0.0 copy-done.1
  35.1 1.2 %last_block.1 = (bf16[3,128,1024]{2,1,0:T(8,128)(2,1)S(1)}, bf16[2,128,1024]{2,1,0:T(8,128)(2,1)S(1)}, bf16[2,128,512]{2,1,0:T(8,128)(2,1)S(1)}, bf16[2,128,512]{2,1,0:T(8,128)(2,1)S(1)}) custom-call(f32[3,128,1024]{2,1,0:T(8,128)S(1)} %get-tuple-element.58.total_ref, bf16[128,1024]{1,0:T(8,128)(2,1)S(1)} %copy-done.1, ...), custom_call_target="tpu_custom_call" | custom-call | flops 805306368 | bytes 1048576 | tf_op jit(solution)/shard_map/last_block/pallas_call | solution.py:147
  36.3 1.3 %collective-permute-start.12 = (bf16[2,128,1024]{2,1,0:T(8,128)(2,1)S(1)}, bf16[2,128,1024]{2,1,0:T(8,128)(2,1)S(1)}, u32[]{:S(2)}, u32[]{:S(2)}) collective-permute-start(bf16[2,128,1024]{2,1,0:T(8,128)(2,1)S(1)} %get-tuple-element.61.refs_4_), channel_id=1, source_target_pairs={{0,16},{8,24},{16,0},{24,8},{1,17},{9,25},{17,1},{25,9},{2,18},{10... | collective-permute-start | bytes 1572872 | tf_op jit(solution)/shard_map/ppermute | solution.py:338
  37.5 0.0 collective-permute-start.5
  37.5 0.5 collective-permute-start.6
  38.0 0.0 collective-permute-start.10
  38.0 0.5 collective-permute-start.11
  38.5 0.6 %collective-permute-done.5.refs_2_ = bf16[144,1024]{1,0:T(8,128)(2,1)S(1)} collective-permute-done((bf16[144,1024]{1,0:T(8,128)(2,1)S(1)}, bf16[144,1024]{1,0:T(8,128)(2,1)S(1)}, u32[]{:S(2)}, u32[]{:S(2)}) %collective-permute-start.5) | collective-permute-done | bytes 294944 | tf_op jit(solution)/shard_map/ppermute | solution.py:333
  39.1 0.4 collective-permute-done.6.refs_3_
  39.5 0.4 collective-permute-done.10.refs_5_
  39.9 0.4 collective-permute-done.11.refs_6_
  40.3 0.0 copy-done
  40.3 2.4 %spectra.1 = (f32[1024,1024]{1,0:T(8,128)S(1)}, f32[1024,2048]{1,0:T(8,128)S(1)}, bf16[128,1024]{1,0:T(8,128)(2,1)S(1)}) custom-call(s32[1]{0:T(128)} %bitcast.device_ref, bf16[1024,512]{1,0:T(8,128)(2,1)S(1)} %copy-done, bf16[144,1024]{1,0:T(8,128)(2,1)S(1)} %pad_maximum_fusion.refs_0_, bf16[144,1024]{1,0:T(8,128)(2,1)S(1)} %collective-permute-done.4.refs_1_, ...), custom_call_target="tpu_custom_call" | custom-call | flops 1048576 | bytes 65536 | tf_op jit(solution)/shard_map/spectra/pallas_call | solution.py:217
  42.7 4.0 %collective-permute-done.12.refs_6_ = bf16[2,128,1024]{2,1,0:T(8,128)(2,1)S(1)} collective-permute-done((bf16[2,128,1024]{2,1,0:T(8,128)(2,1)S(1)}, bf16[2,128,1024]{2,1,0:T(8,128)(2,1)S(1)}, u32[]{:S(2)}, u32[]{:S(2)}) %collective-permute-start.12) | collective-permute-done | bytes 524320 | tf_op jit(solution)/shard_map/ppermute | solution.py:338
  46.7 0.0 collective-permute-start.13
  46.7 1.9 %collective-permute-done.13.refs_7_ = bf16[2,128,1024]{2,1,0:T(8,128)(2,1)S(1)} collective-permute-done((bf16[2,128,1024]{2,1,0:T(8,128)(2,1)S(1)}, bf16[2,128,1024]{2,1,0:T(8,128)(2,1)S(1)}, u32[]{:S(2)}, u32[]{:S(2)}) %collective-permute-start.13) | collective-permute-done | bytes 524320 | tf_op jit(solution)/shard_map/ppermute | solution.py:333
  48.7 5.4 %convolve.1 = (bf16[128,1024]{1,0:T(8,128)(2,1)}, bf16[3,128,1024]{2,1,0:T(8,128)(2,1)}, f32[128,1024]{1,0:T(8,128)}) custom-call(s32[1]{0:T(128)} %bitcast.device_ref, bf16[1024,512]{1,0:T(8,128)(2,1)S(1)} %copy-done, bf16[128,1024]{1,0:T(8,128)(2,1)S(1)} %get-tuple-element.64.refs_1_, bf16[128,1024]{1,0:T(8,128)(2,1)S(1)} %copy-done.1, ...), custom_call_target="tpu_custom_call" | custom-call | flops 1048576 | bytes 65536 | tf_op jit(solution)/shard_map/convolve/pallas_call | solution.py:310
  (2 shorter events, 0.0 us)
Async XLA Ops:
  0.6 10.9 %collective-permute-start = (bf16[128,1024]{1,0:T(8,128)(2,1)}, bf16[128,1024]{1,0:T(8,128)(2,1)S(1)}, u32[]{:S(2)}, u32[]{:S(2)}) collective-permute-start(bf16[128,1024]{1,0:T(8,128)(2,1)} %refs_0_.2), channel_id=1, source_target_pairs={{0,2},{2,4},{4,6},{6,7},{7,5},{5,3},{3,1},{1,0},{8,10},{10,12},{12... | collective-permute-start | bytes 786440 | tf_op jit(solution)/shard_map/ppermute | solution.py:361
  3.7 8.0 %collective-permute-start.1 = (bf16[128,1024]{1,0:T(8,128)(2,1)}, bf16[128,1024]{1,0:T(8,128)(2,1)S(1)}, u32[]{:S(2)}, u32[]{:S(2)}) collective-permute-start(bf16[128,1024]{1,0:T(8,128)(2,1)} %refs_0_.2), channel_id=1, source_target_pairs={{2,0},{4,2},{6,4},{7,6},{5,7},{3,5},{1,3},{0,1},{10,8},{12,10},{14... | collective-permute-start | bytes 786440 | tf_op jit(solution)/shard_map/ppermute | solution.py:363
  9.6 9.6 %collective-permute-start.4 = (bf16[144,1024]{1,0:T(8,128)(2,1)S(1)}, bf16[144,1024]{1,0:T(8,128)(2,1)S(1)}, u32[]{:S(2)}, u32[]{:S(2)}) collective-permute-start(bf16[144,1024]{1,0:T(8,128)(2,1)S(1)} %pad_maximum_fusion.refs_0_), channel_id=1, source_target_pairs={{0,16},{8,24},{16,0},{24,8},{1,17},{9,25},{17,1},{25,9},{2,18},{10... | collective-permute-start | bytes 884744 | tf_op jit(solution)/shard_map/ppermute | solution.py:338
  11.7 7.5 %collective-permute-start.2 = (bf16[128,1024]{1,0:T(8,128)(2,1)S(1)}, bf16[128,1024]{1,0:T(8,128)(2,1)S(1)}, u32[]{:S(2)}, u32[]{:S(2)}) collective-permute-start(bf16[128,1024]{1,0:T(8,128)(2,1)S(1)} %collective-permute-done.refs_0_), channel_id=1, source_target_pairs={{0,2},{2,4},{4,6},{6,7},{7,5},{5,3},{3,1},{1,0},{8,10},{10,12},{12... | collective-permute-start | bytes 786440 | tf_op jit(solution)/shard_map/ppermute | solution.py:361
  13.3 6.8 %collective-permute-start.3 = (bf16[128,1024]{1,0:T(8,128)(2,1)S(1)}, bf16[128,1024]{1,0:T(8,128)(2,1)S(1)}, u32[]{:S(2)}, u32[]{:S(2)}) collective-permute-start(bf16[128,1024]{1,0:T(8,128)(2,1)S(1)} %collective-permute-done.1.refs_3_), channel_id=1, source_target_pairs={{2,0},{4,2},{6,4},{7,6},{5,7},{3,5},{1,3},{0,1},{10,8},{12,10},{14... | collective-permute-start | bytes 786440 | tf_op jit(solution)/shard_map/ppermute | solution.py:363
  20.1 7.4 %collective-permute-start.7 = (bf16[128,1024]{1,0:T(8,128)(2,1)S(1)}, bf16[128,1024]{1,0:T(8,128)(2,1)S(1)}, u32[]{:S(2)}, u32[]{:S(2)}) collective-permute-start(bf16[128,1024]{1,0:T(8,128)(2,1)S(1)} %collective-permute-done.2.refs_0_), channel_id=1, source_target_pairs={{0,2},{2,4},{4,6},{6,7},{7,5},{5,3},{3,1},{1,0},{8,10},{10,12},{12... | collective-permute-start | bytes 786440 | tf_op jit(solution)/shard_map/ppermute | solution.py:361
  21.7 6.4 %collective-permute-start.8 = (bf16[128,1024]{1,0:T(8,128)(2,1)S(1)}, bf16[128,1024]{1,0:T(8,128)(2,1)S(1)}, u32[]{:S(2)}, u32[]{:S(2)}) collective-permute-start(bf16[128,1024]{1,0:T(8,128)(2,1)S(1)} %collective-permute-done.3.refs_3_), channel_id=1, source_target_pairs={{2,0},{4,2},{6,4},{7,6},{5,7},{3,5},{1,3},{0,1},{10,8},{12,10},{14... | collective-permute-start | bytes 786440 | tf_op jit(solution)/shard_map/ppermute | solution.py:363
  28.0 7.0 %collective-permute-start.9 = (bf16[128,1024]{1,0:T(8,128)(2,1)S(1)}, bf16[128,1024]{1,0:T(8,128)(2,1)S(1)}, u32[]{:S(2)}, u32[]{:S(2)}) collective-permute-start(bf16[128,1024]{1,0:T(8,128)(2,1)S(1)} %collective-permute-done.7.refs_0_), channel_id=1, source_target_pairs={{0,2},{2,4},{4,6},{6,7},{7,5},{5,3},{3,1},{1,0},{8,10},{10,12},{12... | collective-permute-start | bytes 786440 | tf_op jit(solution)/shard_map/ppermute | solution.py:361
  29.6 5.5 %copy-start.1 = (bf16[128,1024]{1,0:T(8,128)(2,1)S(1)}, bf16[128,1024]{1,0:T(8,128)(2,1)}, u32[]{:S(2)}) copy-start(bf16[128,1024]{1,0:T(8,128)(2,1)} %refs_2_.1) | copy-start | bytes 786436
  35.0 5.2 %copy-start = (bf16[1024,512]{1,0:T(8,128)(2,1)S(1)}, bf16[1024,512]{1,0:T(8,128)(2,1)}, u32[]{:S(2)}) copy-start(bf16[1024,512]{1,0:T(8,128)(2,1)} %constant.12.clone.table_ref.refs_0_) | copy-start | bytes 3145732
  36.3 10.5 %collective-permute-start.12 = (bf16[2,128,1024]{2,1,0:T(8,128)(2,1)S(1)}, bf16[2,128,1024]{2,1,0:T(8,128)(2,1)S(1)}, u32[]{:S(2)}, u32[]{:S(2)}) collective-permute-start(bf16[2,128,1024]{2,1,0:T(8,128)(2,1)S(1)} %get-tuple-element.61.refs_4_), channel_id=1, source_target_pairs={{0,16},{8,24},{16,0},{24,8},{1,17},{9,25},{17,1},{25,9},{2,18},{10... | collective-permute-start | bytes 1572872 | tf_op jit(solution)/shard_map/ppermute | solution.py:338
  37.5 1.6 %collective-permute-start.5 = (bf16[144,1024]{1,0:T(8,128)(2,1)S(1)}, bf16[144,1024]{1,0:T(8,128)(2,1)S(1)}, u32[]{:S(2)}, u32[]{:S(2)}) collective-permute-start(bf16[144,1024]{1,0:T(8,128)(2,1)S(1)} %pad_maximum_fusion.refs_0_), channel_id=1, source_target_pairs={{0,8},{8,0},{16,24},{24,16},{1,9},{9,1},{17,25},{25,17},{2,10},{10... | collective-permute-start | bytes 884744 | tf_op jit(solution)/shard_map/ppermute | solution.py:333
  37.5 2.0 %collective-permute-start.6 = (bf16[144,1024]{1,0:T(8,128)(2,1)S(1)}, bf16[144,1024]{1,0:T(8,128)(2,1)S(1)}, u32[]{:S(2)}, u32[]{:S(2)}) collective-permute-start(bf16[144,1024]{1,0:T(8,128)(2,1)S(1)} %collective-permute-done.4.refs_1_), channel_id=1, source_target_pairs={{0,8},{8,0},{16,24},{24,16},{1,9},{9,1},{17,25},{25,17},{2,10},{10... | collective-permute-start | bytes 884744 | tf_op jit(solution)/shard_map/ppermute | solution.py:333
  38.0 1.9 %collective-permute-start.10 = (bf16[2,128,512]{2,1,0:T(8,128)(2,1)S(1)}, bf16[2,128,512]{2,1,0:T(8,128)(2,1)S(1)}, u32[]{:S(2)}, u32[]{:S(2)}) collective-permute-start(bf16[2,128,512]{2,1,0:T(8,128)(2,1)S(1)} %get-tuple-element.62), channel_id=1, source_target_pairs={{0,8},{8,0},{16,24},{24,16},{1,9},{9,1},{17,25},{25,17},{2,10},{10... | collective-permute-start | bytes 786440 | tf_op jit(solution)/shard_map/ppermute | solution.py:333
  38.0 2.2 %collective-permute-start.11 = (bf16[2,128,512]{2,1,0:T(8,128)(2,1)S(1)}, bf16[2,128,512]{2,1,0:T(8,128)(2,1)S(1)}, u32[]{:S(2)}, u32[]{:S(2)}) collective-permute-start(bf16[2,128,512]{2,1,0:T(8,128)(2,1)S(1)} %get-tuple-element.63), channel_id=1, source_target_pairs={{0,8},{8,0},{16,24},{24,16},{1,9},{9,1},{17,25},{25,17},{2,10},{10... | collective-permute-start | bytes 786440 | tf_op jit(solution)/shard_map/ppermute | solution.py:333
  46.7 1.9 %collective-permute-start.13 = (bf16[2,128,1024]{2,1,0:T(8,128)(2,1)S(1)}, bf16[2,128,1024]{2,1,0:T(8,128)(2,1)S(1)}, u32[]{:S(2)}, u32[]{:S(2)}) collective-permute-start(bf16[2,128,1024]{2,1,0:T(8,128)(2,1)S(1)} %collective-permute-done.12.refs_6_), channel_id=1, source_target_pairs={{0,8},{8,0},{16,24},{24,16},{1,9},{9,1},{17,25},{25,17},{2,10},{10... | collective-permute-start | bytes 1572872 | tf_op jit(solution)/shard_map/ppermute | solution.py:333

commit v5 on v4

--- a/solution.py
+++ b/solution.py
@@ -57,6 +57,7 @@
     return pltpu.with_memory_space_constraint(array, pltpu.VMEM)
 
 
+SPARE = 16
 VMEM = pl.BlockSpec(memory_space=pltpu.VMEM)
 SMEM = pl.BlockSpec(memory_space=pltpu.SMEM)
 ANY = pl.BlockSpec(memory_space=pl.ANY)
@@ -66,13 +67,18 @@
 def blocks_kernel(chans, offsets, first, fresh, own, device_ref, *refs):
     first_refs, refs = (refs[:2], refs[2:]) if first else ((), refs)
     total_ref, refs = (None, refs) if fresh else (refs[0], refs[1:])
-    x_ref, source, out_ref, next_ref, held, sems, *own_refs = refs
+    if own:
+        x_ref, source, filter_ref, out_ref, next_ref, filt_ref, held, sems, *own_refs = refs
+        own_x, own_filter, own_sems = own_refs
+        own_copies = [
+            pltpu.make_async_copy(x_ref, own_x, own_sems.at[0]),
+            pltpu.make_async_copy(filter_ref, own_filter, own_sems.at[1]),
+        ]
+        own_copies[0].start()
+        x_ref = own_x
+    else:
+        x_ref, source, out_ref, next_ref, held, sems = refs
     depth = x_ref.shape[1]
-    if own:
-        own_x, own_sem = own_refs
-        own_copy = pltpu.make_async_copy(x_ref, own_x, own_sem)
-        own_copy.start()
-        x_ref = own_x
     copies = []
     for slot, target in enumerate((held, next_ref)):
         start = pl.multiple_of(ring_owner(device_ref[0], chans, offsets[slot]) * depth, depth)
@@ -80,6 +86,8 @@
             pltpu.make_async_copy(source.at[:, pl.ds(start, depth)], target, sems.at[slot])
         )
         copies[slot].start()
+    if own:
+        own_copies[1].start()
     values = [None if fresh else total_ref[j] for j in range(3)]
     if first:
         for j in range(3):
@@ -87,15 +95,20 @@
             values[j] = part if fresh else values[j] + part
             out_ref[j] = values[j]
     if own:
-        own_copy.wait()
+        own_copies[0].wait()
     copies[0].wait()
     for j in range(3):
         part = dot(x_ref[...], held[j])
         out_ref[j] = out_ref[j] + part if first else (part if fresh else values[j] + part)
+    if own:
+        own_copies[1].wait()
+        rows = own_filter.shape[0]
+        filt_ref[:rows] = own_filter[...].astype(BF16)
+        filt_ref[rows:] = own_filter[: filt_ref.shape[0] - rows].astype(BF16)
     copies[1].wait()
 
 
-def add_blocks(device, chans, offsets, total, first, x, weight):
+def add_blocks(device, chans, offsets, total, first, x, weight, long_filter=None):
     rows, depth = x.shape
     width = weight.shape[2]
     own = first is None
@@ -104,17 +117,23 @@
     if total is not None:
         aliases = {len(operands): 0}
         operands.append(total)
-    operands += [x, weight]
+    operands += [x, weight] + [long_filter] * own
     block = (3, depth, width)
     size = 2 * int(np.prod(block)) + 16 * rows * width + 8 * rows * depth
     scratch = [pltpu.VMEM(block, BF16), pltpu.SemaphoreType.DMA((2,))]
     if own:
-        scratch += [pltpu.VMEM((rows, depth), BF16), pltpu.SemaphoreType.DMA]
+        size += 16 * rows * width
+        scratch += [
+            pltpu.VMEM((rows, depth), BF16),
+            pltpu.VMEM((rows, width), F32),
+            pltpu.SemaphoreType.DMA((2,)),
+        ]
     return pl.pallas_call(
         functools.partial(blocks_kernel, chans, offsets, not own, total is None, own),
-        in_specs=[SMEM] + [VMEM] * (len(operands) - 3) + [ANY if own else VMEM, ANY],
-        out_specs=[VMEM] * 2,
-        out_shape=[jax.ShapeDtypeStruct((3, rows, width), F32), pltpu.VMEM(block, BF16)],
+        in_specs=[SMEM] + ([ANY] * 3 if own else [VMEM] * (len(operands) - 2) + [ANY]),
+        out_specs=[VMEM] * (2 + own),
+        out_shape=[jax.ShapeDtypeStruct((3, rows, width), F32), pltpu.VMEM(block, BF16)]
+        + [jax.ShapeDtypeStruct((rows + SPARE, width), BF16)] * own,
         scratch_shapes=scratch,
         input_output_aliases=aliases,
         compiler_params=params(mebibytes_for(size)),
@@ -361,14 +380,13 @@
         next_up = lax.ppermute(up, "chan", forward)
         if step < steps:
             next_down = lax.ppermute(down, "chan", reverse)
-        total, weights = add_blocks(
-            device, chans, (step - 1, -step), total, first, x, weight
-        )
+        offsets = (step - 1, -step)
         taps = []
-        if step == 1:
-            total, filt = lax.optimization_barrier(
-                (total, jnp.concatenate([long_filter, long_filter[:16]], axis=0).astype(BF16))
-            )
+        if step > 1:
+            total, weights = add_blocks(device, chans, offsets, total, first, x, weight)
+        else:
+            filt = pltpu.with_memory_space_constraint(long_filter, pltpu.HBM)
+            total, weights, filt = add_blocks(device, chans, offsets, None, None, x, weight, filt)
             filters = [filt] + from_other_chips(filt, groups)
         if step == 2:
             taps = filters

time: 54.4 us -> 53.8 us (0.989)
  other arithmetic: 1.09 us -> 0 us
    another operation x1 -> x0, other arithmetic: 1.07 us -> none
    ppermute x3, waiting for transfers between devices: 1.56 us -> 2.29 us  [per_device(): next_down = lax.ppermute(down, 'chan', reverse)]
  transfers between devices with their start and end apart: 14 -> 14, of which waited for: 9 -> 9; matrix products, arithmetic and copies ran while one was open for 2% -> 0% of each run, Pallas kernels for 43% -> 44%
where the time goes in v5:
time: 53.8 us; the launch traced here: 53.7 us
  Pallas kernels  30 us (56%)
  starting transfers between devices  13.2 us (25%)
  waiting for transfers between devices  9.55 us (18%)
  between operations  0.89 us (2%)
    pallas_call x4, Pallas kernels, add_blocks(): pl.pallas_call(functools.partial(blocks_kernel, chans, offsets, not own,...  21.1 us
    ppermute x4, starting transfers between devices, per_device(): next_up = lax.ppermute(up, 'chan', forward)  7.75 us
    pallas_call x1, Pallas kernels, convolve(): pl.pallas_call(functools.partial(conv_kernel, chans, groups, pieces, cut....  5.38 us
    ppermute x5, waiting for transfers between devices, to_other_core(): return lax.ppermute(value, 'seq', [(i, i ^ 1) for i in range(groups)])  3.64 us
    ppermute x2, waiting for transfers between devices, from_other_chips(): lax.ppermute(value, 'seq', [(i, (i + 2 * d) % groups) for i in range(grou...  3.61 us
    ppermute x2, starting transfers between devices, from_other_chips(): lax.ppermute(value, 'seq', [(i, (i + 2 * d) % groups) for i in range(grou...  3.56 us
    pallas_call x1, Pallas kernels, spectra(): pl.pallas_call(functools.partial(spectra_kernel, chans, len(taps)), in_sp...  2.43 us
    ppermute x3, waiting for transfers between devices, per_device(): next_down = lax.ppermute(down, 'chan', reverse)  2.29 us
  transfers between devices with their start and end apart: 14, of which 9 were waited for; matrix products, arithmetic and copies ran while one was open for 0% of the time, Pallas kernels for 44%

profile of v5, /device:TPU:0, one launch (start us, length us, event | category | flops | bytes accessed | tf_op | source)
XLA Modules:
  0.0 53.7 jit_solution(862099220504107200)
XLA Ops:
  0.6 3.1 %collective-permute-start = (bf16[128,1024]{1,0:T(8,128)(2,1)}, bf16[128,1024]{1,0:T(8,128)(2,1)S(1)}, u32[]{:S(2)}, u32[]{:S(2)}) collective-permute-start(bf16[128,1024]{1,0:T(8,128)(2,1)} %refs_0_.2), channel_id=1, source_target_pairs={{0,2},{2,4},{4,6},{6,7},{7,5},{5,3},{3,1},{1,0},{8,10},{10,12},{12... | collective-permute-start | bytes 786440 | tf_op jit(solution)/shard_map/ppermute | solution.py:380
  3.7 0.0 collective-permute-start.1
  3.7 4.9 %add_blocks.4 = (f32[3,128,1024]{2,1,0:T(8,128)S(1)}, bf16[3,1024,1024]{2,1,0:T(8,128)(2,1)S(1)}, bf16[144,1024]{1,0:T(8,128)(2,1)S(1)}) custom-call(s32[1]{0:T(128)} %bitcast.device_ref, bf16[128,1024]{1,0:T(8,128)(2,1)} %refs_0_.2, bf16[3,8192,1024]{2,1,0:T(8,128)(2,1)} %bitcast.3, f32[128,1024]{1,0:T(8,128)} %refs_2_.2), custom_call_target="tpu_custom_call" | custom-call | flops 1610612736 | bytes 12582912 | tf_op jit(solution)/shard_map/add_blocks/pallas_call | solution.py:131
  8.6 2.0 %collective-permute-start.4 = (bf16[144,1024]{1,0:T(8,128)(2,1)S(1)}, bf16[144,1024]{1,0:T(8,128)(2,1)S(1)}, u32[]{:S(2)}, u32[]{:S(2)}) collective-permute-start(bf16[144,1024]{1,0:T(8,128)(2,1)S(1)} %get-tuple-element.44.refs_0_), channel_id=1, source_target_pairs={{0,16},{8,24},{16,0},{24,8},{1,17},{9,25},{17,1},{25,9},{2,18},{10... | collective-permute-start | bytes 884744 | tf_op jit(solution)/shard_map/ppermute | solution.py:357
  10.6 0.0 collective-permute-done.refs_0_
  10.6 1.1 %collective-permute-done.1.refs_3_ = bf16[128,1024]{1,0:T(8,128)(2,1)S(1)} collective-permute-done((bf16[128,1024]{1,0:T(8,128)(2,1)}, bf16[128,1024]{1,0:T(8,128)(2,1)S(1)}, u32[]{:S(2)}, u32[]{:S(2)}) %collective-permute-start.1) | collective-permute-done | bytes 262176 | tf_op jit(solution)/shard_map/ppermute | solution.py:382
  11.7 1.6 %collective-permute-start.2 = (bf16[128,1024]{1,0:T(8,128)(2,1)S(1)}, bf16[128,1024]{1,0:T(8,128)(2,1)S(1)}, u32[]{:S(2)}, u32[]{:S(2)}) collective-permute-start(bf16[128,1024]{1,0:T(8,128)(2,1)S(1)} %collective-permute-done.refs_0_), channel_id=1, source_target_pairs={{0,2},{2,4},{4,6},{6,7},{7,5},{5,3},{3,1},{1,0},{8,10},{10,12},{12... | collective-permute-start | bytes 786440 | tf_op jit(solution)/shard_map/ppermute | solution.py:380
  13.3 0.4 collective-permute-start.3
  13.7 5.4 %add_blocks.5 = (f32[3,128,1024]{2,1,0:T(8,128)S(1)}, bf16[3,1024,1024]{2,1,0:T(8,128)(2,1)S(1)}) custom-call(s32[1]{0:T(128)} %bitcast.device_ref, bf16[128,1024]{1,0:T(8,128)(2,1)S(1)} %collective-permute-done.refs_0_, bf16[3,1024,1024]{2,1,0:T(8,128)(2,1)S(1)} %get-tuple-element.40.refs_1_, ...), custom_call_target="tpu_custom_call", output_to_operand_aliasing={{0}: (3, {})} | custom-call | flops 1610612736 | bytes 12582912 | tf_op jit(solution)/shard_map/add_blocks/pallas_call | solution.py:131
  19.1 0.0 collective-permute-done.4.refs_1_
  19.1 0.0 collective-permute-done.2.refs_0_
  19.2 0.7 %collective-permute-done.3.refs_3_ = bf16[128,1024]{1,0:T(8,128)(2,1)S(1)} collective-permute-done((bf16[128,1024]{1,0:T(8,128)(2,1)S(1)}, bf16[128,1024]{1,0:T(8,128)(2,1)S(1)}, u32[]{:S(2)}, u32[]{:S(2)}) %collective-permute-start.3) | collective-permute-done | bytes 262176 | tf_op jit(solution)/shard_map/ppermute | solution.py:382
  19.8 1.6 %collective-permute-start.7 = (bf16[128,1024]{1,0:T(8,128)(2,1)S(1)}, bf16[128,1024]{1,0:T(8,128)(2,1)S(1)}, u32[]{:S(2)}, u32[]{:S(2)}) collective-permute-start(bf16[128,1024]{1,0:T(8,128)(2,1)S(1)} %collective-permute-done.2.refs_0_), channel_id=1, source_target_pairs={{0,2},{2,4},{4,6},{6,7},{7,5},{5,3},{3,1},{1,0},{8,10},{10,12},{12... | collective-permute-start | bytes 786440 | tf_op jit(solution)/shard_map/ppermute | solution.py:380
  21.4 0.4 collective-permute-start.8
  21.9 5.4 %add_blocks.6 = (f32[3,128,1024]{2,1,0:T(8,128)S(1)}, bf16[3,1024,1024]{2,1,0:T(8,128)(2,1)S(1)}) custom-call(s32[1]{0:T(128)} %bitcast.device_ref, bf16[128,1024]{1,0:T(8,128)(2,1)S(1)} %collective-permute-done.2.refs_0_, bf16[3,1024,1024]{2,1,0:T(8,128)(2,1)S(1)} %get-tuple-element.48.refs_1_, ...), custom_call_target="tpu_custom_call", output_to_operand_aliasing={{0}: (3, {})} | custom-call | flops 1610612736 | bytes 12582912 | tf_op jit(solution)/shard_map/add_blocks/pallas_call | solution.py:131
  27.2 0.0 collective-permute-done.7.refs_0_
  27.3 0.5 collective-permute-done.8.refs_3_
  27.8 1.5 %collective-permute-start.9 = (bf16[128,1024]{1,0:T(8,128)(2,1)S(1)}, bf16[128,1024]{1,0:T(8,128)(2,1)S(1)}, u32[]{:S(2)}, u32[]{:S(2)}) collective-permute-start(bf16[128,1024]{1,0:T(8,128)(2,1)S(1)} %collective-permute-done.7.refs_0_), channel_id=1, source_target_pairs={{0,2},{2,4},{4,6},{6,7},{7,5},{5,3},{3,1},{1,0},{8,10},{10,12},{12... | collective-permute-start | bytes 786440 | tf_op jit(solution)/shard_map/ppermute | solution.py:380
  29.3 0.0 copy-start.1
  29.3 5.4 %add_blocks.7 = (f32[3,128,1024]{2,1,0:T(8,128)S(1)}, bf16[3,1024,1024]{2,1,0:T(8,128)(2,1)S(1)}) custom-call(s32[1]{0:T(128)} %bitcast.device_ref, bf16[128,1024]{1,0:T(8,128)(2,1)S(1)} %collective-permute-done.7.refs_0_, bf16[3,1024,1024]{2,1,0:T(8,128)(2,1)S(1)} %get-tuple-element.52.refs_1_, ...), custom_call_target="tpu_custom_call", output_to_operand_aliasing={{0}: (3, {})} | custom-call | flops 1610612736 | bytes 12582912 | tf_op jit(solution)/shard_map/add_blocks/pallas_call | solution.py:131
  34.7 0.0 copy-start
  34.7 0.0 collective-permute-done.9.x_ref
  34.7 0.0 copy-done.1
  34.7 1.1 %last_block.1 = (bf16[3,128,1024]{2,1,0:T(8,128)(2,1)S(1)}, bf16[2,128,1024]{2,1,0:T(8,128)(2,1)S(1)}, bf16[2,128,512]{2,1,0:T(8,128)(2,1)S(1)}, bf16[2,128,512]{2,1,0:T(8,128)(2,1)S(1)}) custom-call(f32[3,128,1024]{2,1,0:T(8,128)S(1)} %get-tuple-element.56.total_ref, bf16[128,1024]{1,0:T(8,128)(2,1)S(1)} %copy-done.1, ...), custom_call_target="tpu_custom_call" | custom-call | flops 805306368 | bytes 1048576 | tf_op jit(solution)/shard_map/last_block/pallas_call | solution.py:166
  35.9 1.6 %collective-permute-start.12 = (bf16[2,128,1024]{2,1,0:T(8,128)(2,1)S(1)}, bf16[2,128,1024]{2,1,0:T(8,128)(2,1)S(1)}, u32[]{:S(2)}, u32[]{:S(2)}) collective-permute-start(bf16[2,128,1024]{2,1,0:T(8,128)(2,1)S(1)} %get-tuple-element.59.refs_4_), channel_id=1, source_target_pairs={{0,16},{8,24},{16,0},{24,8},{1,17},{9,25},{17,1},{25,9},{2,18},{10... | collective-permute-start | bytes 1572872 | tf_op jit(solution)/shard_map/ppermute | solution.py:357
  37.4 0.0 collective-permute-start.5
  37.4 0.5 collective-permute-start.6
  37.9 0.0 collective-permute-start.10
  37.9 0.5 collective-permute-start.11
  38.5 0.6 %collective-permute-done.5.refs_2_ = bf16[144,1024]{1,0:T(8,128)(2,1)S(1)} collective-permute-done((bf16[144,1024]{1,0:T(8,128)(2,1)S(1)}, bf16[144,1024]{1,0:T(8,128)(2,1)S(1)}, u32[]{:S(2)}, u32[]{:S(2)}) %collective-permute-start.5) | collective-permute-done | bytes 294944 | tf_op jit(solution)/shard_map/ppermute | solution.py:352
  39.0 0.4 collective-permute-done.6.refs_3_
  39.4 0.4 collective-permute-done.10.refs_5_
  39.8 0.4 collective-permute-done.11.refs_6_
  40.2 0.0 copy-done
  40.2 2.4 %spectra.1 = (f32[1024,1024]{1,0:T(8,128)S(1)}, f32[1024,2048]{1,0:T(8,128)S(1)}, bf16[128,1024]{1,0:T(8,128)(2,1)S(1)}) custom-call(s32[1]{0:T(128)} %bitcast.device_ref, bf16[1024,512]{1,0:T(8,128)(2,1)S(1)} %copy-done, bf16[144,1024]{1,0:T(8,128)(2,1)S(1)} %get-tuple-element.44.refs_0_, bf16[144,1024]{1,0:T(8,128)(2,1)S(1)} %collective-permute-done.4.refs_1_, ...), custom_call_target="tpu_custom_call" | custom-call | flops 1048576 | bytes 65536 | tf_op jit(solution)/shard_map/spectra/pallas_call | solution.py:236
  42.6 3.6 %collective-permute-done.12.refs_6_ = bf16[2,128,1024]{2,1,0:T(8,128)(2,1)S(1)} collective-permute-done((bf16[2,128,1024]{2,1,0:T(8,128)(2,1)S(1)}, bf16[2,128,1024]{2,1,0:T(8,128)(2,1)S(1)}, u32[]{:S(2)}, u32[]{:S(2)}) %collective-permute-start.12) | collective-permute-done | bytes 524320 | tf_op jit(solution)/shard_map/ppermute | solution.py:357
  46.2 0.0 collective-permute-start.13
  46.2 1.9 %collective-permute-done.13.refs_7_ = bf16[2,128,1024]{2,1,0:T(8,128)(2,1)S(1)} collective-permute-done((bf16[2,128,1024]{2,1,0:T(8,128)(2,1)S(1)}, bf16[2,128,1024]{2,1,0:T(8,128)(2,1)S(1)}, u32[]{:S(2)}, u32[]{:S(2)}) %collective-permute-start.13) | collective-permute-done | bytes 524320 | tf_op jit(solution)/shard_map/ppermute | solution.py:352
  48.1 5.4 %convolve.1 = (bf16[128,1024]{1,0:T(8,128)(2,1)}, bf16[3,128,1024]{2,1,0:T(8,128)(2,1)}, f32[128,1024]{1,0:T(8,128)}) custom-call(s32[1]{0:T(128)} %bitcast.device_ref, bf16[1024,512]{1,0:T(8,128)(2,1)S(1)} %copy-done, bf16[128,1024]{1,0:T(8,128)(2,1)S(1)} %get-tuple-element.62.refs_1_, bf16[128,1024]{1,0:T(8,128)(2,1)S(1)} %copy-done.1, ...), custom_call_target="tpu_custom_call" | custom-call | flops 1048576 | bytes 65536 | tf_op jit(solution)/shard_map/convolve/pallas_call | solution.py:329
Async XLA Ops:
  0.6 10.0 %collective-permute-start = (bf16[128,1024]{1,0:T(8,128)(2,1)}, bf16[128,1024]{1,0:T(8,128)(2,1)S(1)}, u32[]{:S(2)}, u32[]{:S(2)}) collective-permute-start(bf16[128,1024]{1,0:T(8,128)(2,1)} %refs_0_.2), channel_id=1, source_target_pairs={{0,2},{2,4},{4,6},{6,7},{7,5},{5,3},{3,1},{1,0},{8,10},{10,12},{12... | collective-permute-start | bytes 786440 | tf_op jit(solution)/shard_map/ppermute | solution.py:380
  3.7 8.0 %collective-permute-start.1 = (bf16[128,1024]{1,0:T(8,128)(2,1)}, bf16[128,1024]{1,0:T(8,128)(2,1)S(1)}, u32[]{:S(2)}, u32[]{:S(2)}) collective-permute-start(bf16[128,1024]{1,0:T(8,128)(2,1)} %refs_0_.2), channel_id=1, source_target_pairs={{2,0},{4,2},{6,4},{7,6},{5,7},{3,5},{1,3},{0,1},{10,8},{12,10},{14... | collective-permute-start | bytes 786440 | tf_op jit(solution)/shard_map/ppermute | solution.py:382
  8.6 10.5 %collective-permute-start.4 = (bf16[144,1024]{1,0:T(8,128)(2,1)S(1)}, bf16[144,1024]{1,0:T(8,128)(2,1)S(1)}, u32[]{:S(2)}, u32[]{:S(2)}) collective-permute-start(bf16[144,1024]{1,0:T(8,128)(2,1)S(1)} %get-tuple-element.44.refs_0_), channel_id=1, source_target_pairs={{0,16},{8,24},{16,0},{24,8},{1,17},{9,25},{17,1},{25,9},{2,18},{10... | collective-permute-start | bytes 884744 | tf_op jit(solution)/shard_map/ppermute | solution.py:357
  11.7 7.5 %collective-permute-start.2 = (bf16[128,1024]{1,0:T(8,128)(2,1)S(1)}, bf16[128,1024]{1,0:T(8,128)(2,1)S(1)}, u32[]{:S(2)}, u32[]{:S(2)}) collective-permute-start(bf16[128,1024]{1,0:T(8,128)(2,1)S(1)} %collective-permute-done.refs_0_), channel_id=1, source_target_pairs={{0,2},{2,4},{4,6},{6,7},{7,5},{5,3},{3,1},{1,0},{8,10},{10,12},{12... | collective-permute-start | bytes 786440 | tf_op jit(solution)/shard_map/ppermute | solution.py:380
  13.3 6.6 %collective-permute-start.3 = (bf16[128,1024]{1,0:T(8,128)(2,1)S(1)}, bf16[128,1024]{1,0:T(8,128)(2,1)S(1)}, u32[]{:S(2)}, u32[]{:S(2)}) collective-permute-start(bf16[128,1024]{1,0:T(8,128)(2,1)S(1)} %collective-permute-done.1.refs_3_), channel_id=1, source_target_pairs={{2,0},{4,2},{6,4},{7,6},{5,7},{3,5},{1,3},{0,1},{10,8},{12,10},{14... | collective-permute-start | bytes 786440 | tf_op jit(solution)/shard_map/ppermute | solution.py:382
  19.8 7.4 %collective-permute-start.7 = (bf16[128,1024]{1,0:T(8,128)(2,1)S(1)}, bf16[128,1024]{1,0:T(8,128)(2,1)S(1)}, u32[]{:S(2)}, u32[]{:S(2)}) collective-permute-start(bf16[128,1024]{1,0:T(8,128)(2,1)S(1)} %collective-permute-done.2.refs_0_), channel_id=1, source_target_pairs={{0,2},{2,4},{4,6},{6,7},{7,5},{5,3},{3,1},{1,0},{8,10},{10,12},{12... | collective-permute-start | bytes 786440 | tf_op jit(solution)/shard_map/ppermute | solution.py:380
  21.4 6.4 %collective-permute-start.8 = (bf16[128,1024]{1,0:T(8,128)(2,1)S(1)}, bf16[128,1024]{1,0:T(8,128)(2,1)S(1)}, u32[]{:S(2)}, u32[]{:S(2)}) collective-permute-start(bf16[128,1024]{1,0:T(8,128)(2,1)S(1)} %collective-permute-done.3.refs_3_), channel_id=1, source_target_pairs={{2,0},{4,2},{6,4},{7,6},{5,7},{3,5},{1,3},{0,1},{10,8},{12,10},{14... | collective-permute-start | bytes 786440 | tf_op jit(solution)/shard_map/ppermute | solution.py:382
  27.8 6.9 %collective-permute-start.9 = (bf16[128,1024]{1,0:T(8,128)(2,1)S(1)}, bf16[128,1024]{1,0:T(8,128)(2,1)S(1)}, u32[]{:S(2)}, u32[]{:S(2)}) collective-permute-start(bf16[128,1024]{1,0:T(8,128)(2,1)S(1)} %collective-permute-done.7.refs_0_), channel_id=1, source_target_pairs={{0,2},{2,4},{4,6},{6,7},{7,5},{5,3},{3,1},{1,0},{8,10},{10,12},{12... | collective-permute-start | bytes 786440 | tf_op jit(solution)/shard_map/ppermute | solution.py:380
  29.3 5.4 %copy-start.1 = (bf16[128,1024]{1,0:T(8,128)(2,1)S(1)}, bf16[128,1024]{1,0:T(8,128)(2,1)}, u32[]{:S(2)}) copy-start(bf16[128,1024]{1,0:T(8,128)(2,1)} %refs_2_.3) | copy-start | bytes 786436
  34.7 5.5 %copy-start = (bf16[1024,512]{1,0:T(8,128)(2,1)S(1)}, bf16[1024,512]{1,0:T(8,128)(2,1)}, u32[]{:S(2)}) copy-start(bf16[1024,512]{1,0:T(8,128)(2,1)} %constant.12.clone.table_ref.refs_0_) | copy-start | bytes 3145732
  35.9 10.3 %collective-permute-start.12 = (bf16[2,128,1024]{2,1,0:T(8,128)(2,1)S(1)}, bf16[2,128,1024]{2,1,0:T(8,128)(2,1)S(1)}, u32[]{:S(2)}, u32[]{:S(2)}) collective-permute-start(bf16[2,128,1024]{2,1,0:T(8,128)(2,1)S(1)} %get-tuple-element.59.refs_4_), channel_id=1, source_target_pairs={{0,16},{8,24},{16,0},{24,8},{1,17},{9,25},{17,1},{25,9},{2,18},{10... | collective-permute-start | bytes 1572872 | tf_op jit(solution)/shard_map/ppermute | solution.py:357
  37.4 1.6 %collective-permute-start.5 = (bf16[144,1024]{1,0:T(8,128)(2,1)S(1)}, bf16[144,1024]{1,0:T(8,128)(2,1)S(1)}, u32[]{:S(2)}, u32[]{:S(2)}) collective-permute-start(bf16[144,1024]{1,0:T(8,128)(2,1)S(1)} %get-tuple-element.44.refs_0_), channel_id=1, source_target_pairs={{0,8},{8,0},{16,24},{24,16},{1,9},{9,1},{17,25},{25,17},{2,10},{10... | collective-permute-start | bytes 884744 | tf_op jit(solution)/shard_map/ppermute | solution.py:352
  37.4 2.0 %collective-permute-start.6 = (bf16[144,1024]{1,0:T(8,128)(2,1)S(1)}, bf16[144,1024]{1,0:T(8,128)(2,1)S(1)}, u32[]{:S(2)}, u32[]{:S(2)}) collective-permute-start(bf16[144,1024]{1,0:T(8,128)(2,1)S(1)} %collective-permute-done.4.refs_1_), channel_id=1, source_target_pairs={{0,8},{8,0},{16,24},{24,16},{1,9},{9,1},{17,25},{25,17},{2,10},{10... | collective-permute-start | bytes 884744 | tf_op jit(solution)/shard_map/ppermute | solution.py:352
  37.9 1.9 %collective-permute-start.10 = (bf16[2,128,512]{2,1,0:T(8,128)(2,1)S(1)}, bf16[2,128,512]{2,1,0:T(8,128)(2,1)S(1)}, u32[]{:S(2)}, u32[]{:S(2)}) collective-permute-start(bf16[2,128,512]{2,1,0:T(8,128)(2,1)S(1)} %get-tuple-element.60), channel_id=1, source_target_pairs={{0,8},{8,0},{16,24},{24,16},{1,9},{9,1},{17,25},{25,17},{2,10},{10... | collective-permute-start | bytes 786440 | tf_op jit(solution)/shard_map/ppermute | solution.py:352
  37.9 2.2 %collective-permute-start.11 = (bf16[2,128,512]{2,1,0:T(8,128)(2,1)S(1)}, bf16[2,128,512]{2,1,0:T(8,128)(2,1)S(1)}, u32[]{:S(2)}, u32[]{:S(2)}) collective-permute-start(bf16[2,128,512]{2,1,0:T(8,128)(2,1)S(1)} %get-tuple-element.61), channel_id=1, source_target_pairs={{0,8},{8,0},{16,24},{24,16},{1,9},{9,1},{17,25},{25,17},{2,10},{10... | collective-permute-start | bytes 786440 | tf_op jit(solution)/shard_map/ppermute | solution.py:352
  46.2 1.9 %collective-permute-start.13 = (bf16[2,128,1024]{2,1,0:T(8,128)(2,1)S(1)}, bf16[2,128,1024]{2,1,0:T(8,128)(2,1)S(1)}, u32[]{:S(2)}, u32[]{:S(2)}) collective-permute-start(bf16[2,128,1024]{2,1,0:T(8,128)(2,1)S(1)} %collective-permute-done.12.refs_6_), channel_id=1, source_target_pairs={{0,8},{8,0},{16,24},{24,16},{1,9},{9,1},{17,25},{25,17},{2,10},{10... | collective-permute-start | bytes 1572872 | tf_op jit(solution)/shard_map/ppermute | solution.py:352

commit v6 on v5

--- a/solution.py
+++ b/solution.py
@@ -41,16 +41,24 @@
     return [(order[i], order[(i + 1) % size]) for i in range(size)]
 
 
+def remainder(number, size):
+    return number & (size - 1) if size & (size - 1) == 0 else lax.rem(number, size)
+
+
+def quotient(number, size):
+    return number >> (size.bit_length() - 1) if size & (size - 1) == 0 else lax.div(number, size)
+
+
 def ring_owner(device, chans, offset):
-    index = lax.rem(device, chans)
-    half = lax.div(index, 2)
-    position = jnp.where(lax.rem(index, 2) == 0, half, chans - 1 - half)
-    position = lax.rem(position + (offset + chans), chans)
+    index = remainder(device, chans)
+    half = index >> 1
+    position = jnp.where(index & 1 == 0, half, chans - 1 - half)
+    position = remainder(position + (offset + chans), chans)
     return jnp.where(position < chans // 2, 2 * position, 2 * (chans - 1 - position) + 1)
 
 
 def sequence_owner(device, chans, groups, distance):
-    return lax.rem(lax.div(device, chans) + (groups - 2 * distance), groups)
+    return remainder(quotient(device, chans) + (groups - 2 * distance), groups)
 
 
 def in_vmem(array):
@@ -186,7 +194,7 @@
 
 
 def chip_rows(owner, ref, other_ref):
-    first = lax.rem(owner, 2) == 0
+    first = owner & 1 == 0
     signals = []
     for signal in range(2):
         mine, others = ref[signal], other_ref[signal]
@@ -197,7 +205,7 @@
 
 
 def chip_table(table_ref, owner, rows):
-    return table_ref[:, pl.ds(pl.multiple_of(owner // 2 * 2 * rows, 256), 2 * rows)]
+    return table_ref[:, pl.ds(pl.multiple_of((owner >> 1) * (2 * rows), 256), 2 * rows)]
 
 
 def spectra_kernel(chans, groups, device_ref, table_ref, *refs):
@@ -209,7 +217,7 @@
     for number, ref in enumerate(tap_refs):
         owner = sequence_owner(device_ref[0], chans, groups, number % chips)
         if number >= chips:
-            owner = owner + 1 - 2 * lax.rem(owner, 2)
+            owner = owner ^ 1
         taps[pl.ds(pl.multiple_of(owner * rows, 128), rows)] = ref[:rows]
     for start in range(0, width, tile):
         columns = slice(start, start + tile)

time: 53.8 us -> 52.9 us (0.983)
  Pallas kernels: 30 us -> 28.3 us
  waiting for transfers between devices: 9.55 us -> 10.3 us
    pallas_call x4, Pallas kernels: 21.1 us -> 19.3 us  [add_blocks(): pl.pallas_call(functools.partial(blocks_kernel, chans, offsets, not own,...]
    ppermute x3, waiting for transfers between devices: 2.29 us -> 3.48 us  [per_device(): next_down = lax.ppermute(down, 'chan', reverse)]
  transfers between devices with their start and end apart: 14 -> 14, of which waited for: 9 -> 9; matrix products, arithmetic and copies ran while one was open for 0% -> 0% of each run, Pallas kernels for 44% -> 41%
where the time goes in v6:
time: 52.9 us; the launch traced here: 52.7 us
  Pallas kernels  28.3 us (53%)
  starting transfers between devices  13.2 us (25%)
  waiting for transfers between devices  10.3 us (19%)
  between operations  0.89 us (2%)
    pallas_call x4, Pallas kernels, add_blocks(): pl.pallas_call(functools.partial(blocks_kernel, chans, offsets, not own,...  19.3 us
    ppermute x4, starting transfers between devices, per_device(): next_up = lax.ppermute(up, 'chan', forward)  7.75 us
    pallas_call x1, Pallas kernels, convolve(): pl.pallas_call(functools.partial(conv_kernel, chans, groups, pieces, cut....  5.37 us
    ppermute x5, waiting for transfers between devices, to_other_core(): return lax.ppermute(value, 'seq', [(i, i ^ 1) for i in range(groups)])  3.64 us
    ppermute x2, starting transfers between devices, from_other_chips(): lax.ppermute(value, 'seq', [(i, (i + 2 * d) % groups) for i in range(grou...  3.54 us
    ppermute x3, waiting for transfers between devices, per_device(): next_down = lax.ppermute(down, 'chan', reverse)  3.48 us
    ppermute x2, waiting for transfers between devices, from_other_chips(): lax.ppermute(value, 'seq', [(i, (i + 2 * d) % groups) for i in range(grou...  3.18 us
    pallas_call x1, Pallas kernels, spectra(): pl.pallas_call(functools.partial(spectra_kernel, chans, len(taps)), in_sp...  2.42 us
  transfers between devices with their start and end apart: 14, of which 9 were waited for; matrix products, arithmetic and copies ran while one was open for 0% of the time, Pallas kernels for 41%

profile of v6, /device:TPU:0, one launch (start us, length us, event | category | flops | bytes accessed | tf_op | source)
XLA Modules:
  0.0 52.7 jit_solution(903056085515289032)
XLA Ops:
  0.6 3.1 %collective-permute-start = (bf16[128,1024]{1,0:T(8,128)(2,1)}, bf16[128,1024]{1,0:T(8,128)(2,1)S(1)}, u32[]{:S(2)}, u32[]{:S(2)}) collective-permute-start(bf16[128,1024]{1,0:T(8,128)(2,1)} %refs_0_.2), channel_id=1, source_target_pairs={{0,2},{2,4},{4,6},{6,7},{7,5},{5,3},{3,1},{1,0},{8,10},{10,12},{12... | collective-permute-start | bytes 786440 | tf_op jit(solution)/shard_map/ppermute | solution.py:388
  3.7 0.0 collective-permute-start.1
  3.7 4.8 %add_blocks.4 = (f32[3,128,1024]{2,1,0:T(8,128)S(1)}, bf16[3,1024,1024]{2,1,0:T(8,128)(2,1)S(1)}, bf16[144,1024]{1,0:T(8,128)(2,1)S(1)}) custom-call(s32[1]{0:T(128)} %bitcast.device_ref, bf16[128,1024]{1,0:T(8,128)(2,1)} %refs_0_.2, bf16[3,8192,1024]{2,1,0:T(8,128)(2,1)} %bitcast.3, f32[128,1024]{1,0:T(8,128)} %refs_2_.2), custom_call_target="tpu_custom_call" | custom-call | flops 1610612736 | bytes 12582912 | tf_op jit(solution)/shard_map/add_blocks/pallas_call | solution.py:139
  8.5 2.0 %collective-permute-start.4 = (bf16[144,1024]{1,0:T(8,128)(2,1)S(1)}, bf16[144,1024]{1,0:T(8,128)(2,1)S(1)}, u32[]{:S(2)}, u32[]{:S(2)}) collective-permute-start(bf16[144,1024]{1,0:T(8,128)(2,1)S(1)} %get-tuple-element.44.refs_0_), channel_id=1, source_target_pairs={{0,16},{8,24},{16,0},{24,8},{1,17},{9,25},{17,1},{25,9},{2,18},{10... | collective-permute-start | bytes 884744 | tf_op jit(solution)/shard_map/ppermute | solution.py:365
  10.5 0.0 collective-permute-done.refs_0_
  10.5 1.2 %collective-permute-done.1.refs_3_ = bf16[128,1024]{1,0:T(8,128)(2,1)S(1)} collective-permute-done((bf16[128,1024]{1,0:T(8,128)(2,1)}, bf16[128,1024]{1,0:T(8,128)(2,1)S(1)}, u32[]{:S(2)}, u32[]{:S(2)}) %collective-permute-start.1) | collective-permute-done | bytes 262176 | tf_op jit(solution)/shard_map/ppermute | solution.py:390
  11.7 1.6 %collective-permute-start.2 = (bf16[128,1024]{1,0:T(8,128)(2,1)S(1)}, bf16[128,1024]{1,0:T(8,128)(2,1)S(1)}, u32[]{:S(2)}, u32[]{:S(2)}) collective-permute-start(bf16[128,1024]{1,0:T(8,128)(2,1)S(1)} %collective-permute-done.refs_0_), channel_id=1, source_target_pairs={{0,2},{2,4},{4,6},{6,7},{7,5},{5,3},{3,1},{1,0},{8,10},{10,12},{12... | collective-permute-start | bytes 786440 | tf_op jit(solution)/shard_map/ppermute | solution.py:388
  13.3 0.4 collective-permute-start.3
  13.7 4.8 %add_blocks.5 = (f32[3,128,1024]{2,1,0:T(8,128)S(1)}, bf16[3,1024,1024]{2,1,0:T(8,128)(2,1)S(1)}) custom-call(s32[1]{0:T(128)} %bitcast.device_ref, bf16[128,1024]{1,0:T(8,128)(2,1)S(1)} %collective-permute-done.refs_0_, bf16[3,1024,1024]{2,1,0:T(8,128)(2,1)S(1)} %get-tuple-element.40.refs_1_, ...), custom_call_target="tpu_custom_call", output_to_operand_aliasing={{0}: (3, {})} | custom-call | flops 1610612736 | bytes 12582912 | tf_op jit(solution)/shard_map/add_blocks/pallas_call | solution.py:139
  18.6 0.0 collective-permute-done.4.refs_1_
  18.6 0.0 collective-permute-done.2.refs_0_
  18.6 1.3 %collective-permute-done.3.refs_3_ = bf16[128,1024]{1,0:T(8,128)(2,1)S(1)} collective-permute-done((bf16[128,1024]{1,0:T(8,128)(2,1)S(1)}, bf16[128,1024]{1,0:T(8,128)(2,1)S(1)}, u32[]{:S(2)}, u32[]{:S(2)}) %collective-permute-start.3) | collective-permute-done | bytes 262176 | tf_op jit(solution)/shard_map/ppermute | solution.py:390
  19.8 1.6 %collective-permute-start.7 = (bf16[128,1024]{1,0:T(8,128)(2,1)S(1)}, bf16[128,1024]{1,0:T(8,128)(2,1)S(1)}, u32[]{:S(2)}, u32[]{:S(2)}) collective-permute-start(bf16[128,1024]{1,0:T(8,128)(2,1)S(1)} %collective-permute-done.2.refs_0_), channel_id=1, source_target_pairs={{0,2},{2,4},{4,6},{6,7},{7,5},{5,3},{3,1},{1,0},{8,10},{10,12},{12... | collective-permute-start | bytes 786440 | tf_op jit(solution)/shard_map/ppermute | solution.py:388
  21.4 0.4 collective-permute-start.8
  21.9 4.8 %add_blocks.6 = (f32[3,128,1024]{2,1,0:T(8,128)S(1)}, bf16[3,1024,1024]{2,1,0:T(8,128)(2,1)S(1)}) custom-call(s32[1]{0:T(128)} %bitcast.device_ref, bf16[128,1024]{1,0:T(8,128)(2,1)S(1)} %collective-permute-done.2.refs_0_, bf16[3,1024,1024]{2,1,0:T(8,128)(2,1)S(1)} %get-tuple-element.48.refs_1_, ...), custom_call_target="tpu_custom_call", output_to_operand_aliasing={{0}: (3, {})} | custom-call | flops 1610612736 | bytes 12582912 | tf_op jit(solution)/shard_map/add_blocks/pallas_call | solution.py:139
  26.7 0.0 collective-permute-done.7.refs_0_
  26.7 1.1 %collective-permute-done.8.refs_3_ = bf16[128,1024]{1,0:T(8,128)(2,1)S(1)} collective-permute-done((bf16[128,1024]{1,0:T(8,128)(2,1)S(1)}, bf16[128,1024]{1,0:T(8,128)(2,1)S(1)}, u32[]{:S(2)}, u32[]{:S(2)}) %collective-permute-start.8) | collective-permute-done | bytes 262176 | tf_op jit(solution)/shard_map/ppermute | solution.py:390
  27.8 1.5 %collective-permute-start.9 = (bf16[128,1024]{1,0:T(8,128)(2,1)S(1)}, bf16[128,1024]{1,0:T(8,128)(2,1)S(1)}, u32[]{:S(2)}, u32[]{:S(2)}) collective-permute-start(bf16[128,1024]{1,0:T(8,128)(2,1)S(1)} %collective-permute-done.7.refs_0_), channel_id=1, source_target_pairs={{0,2},{2,4},{4,6},{6,7},{7,5},{5,3},{3,1},{1,0},{8,10},{10,12},{12... | collective-permute-start | bytes 786440 | tf_op jit(solution)/shard_map/ppermute | solution.py:388
  29.3 0.0 copy-start.1
  29.3 4.9 %add_blocks.7 = (f32[3,128,1024]{2,1,0:T(8,128)S(1)}, bf16[3,1024,1024]{2,1,0:T(8,128)(2,1)S(1)}) custom-call(s32[1]{0:T(128)} %bitcast.device_ref, bf16[128,1024]{1,0:T(8,128)(2,1)S(1)} %collective-permute-done.7.refs_0_, bf16[3,1024,1024]{2,1,0:T(8,128)(2,1)S(1)} %get-tuple-element.52.refs_1_, ...), custom_call_target="tpu_custom_call", output_to_operand_aliasing={{0}: (3, {})} | custom-call | flops 1610612736 | bytes 12582912 | tf_op jit(solution)/shard_map/add_blocks/pallas_call | solution.py:139
  34.2 0.0 copy-start
  34.2 0.0 collective-permute-done.9.x_ref
  34.2 0.0 copy-done.1
  34.2 1.1 %last_block.1 = (bf16[3,128,1024]{2,1,0:T(8,128)(2,1)S(1)}, bf16[2,128,1024]{2,1,0:T(8,128)(2,1)S(1)}, bf16[2,128,512]{2,1,0:T(8,128)(2,1)S(1)}, bf16[2,128,512]{2,1,0:T(8,128)(2,1)S(1)}) custom-call(f32[3,128,1024]{2,1,0:T(8,128)S(1)} %get-tuple-element.56.total_ref, bf16[128,1024]{1,0:T(8,128)(2,1)S(1)} %copy-done.1, ...), custom_call_target="tpu_custom_call" | custom-call | flops 805306368 | bytes 1048576 | tf_op jit(solution)/shard_map/last_block/pallas_call | solution.py:174
  35.4 1.5 %collective-permute-start.12 = (bf16[2,128,1024]{2,1,0:T(8,128)(2,1)S(1)}, bf16[2,128,1024]{2,1,0:T(8,128)(2,1)S(1)}, u32[]{:S(2)}, u32[]{:S(2)}) collective-permute-start(bf16[2,128,1024]{2,1,0:T(8,128)(2,1)S(1)} %get-tuple-element.59.refs_4_), channel_id=1, source_target_pairs={{0,16},{8,24},{16,0},{24,8},{1,17},{9,25},{17,1},{25,9},{2,18},{10... | collective-permute-start | bytes 1572872 | tf_op jit(solution)/shard_map/ppermute | solution.py:365
  36.9 0.0 collective-permute-start.5
  36.9 0.5 collective-permute-start.6
  37.4 0.0 collective-permute-start.10
  37.4 0.5 collective-permute-start.11
  37.9 0.6 %collective-permute-done.5.refs_2_ = bf16[144,1024]{1,0:T(8,128)(2,1)S(1)} collective-permute-done((bf16[144,1024]{1,0:T(8,128)(2,1)S(1)}, bf16[144,1024]{1,0:T(8,128)(2,1)S(1)}, u32[]{:S(2)}, u32[]{:S(2)}) %collective-permute-start.5) | collective-permute-done | bytes 294944 | tf_op jit(solution)/shard_map/ppermute | solution.py:360
  38.5 0.4 collective-permute-done.6.refs_3_
  38.9 0.4 collective-permute-done.10.refs_5_
  39.3 0.4 collective-permute-done.11.refs_6_
  39.7 0.0 copy-done
  39.7 2.4 %spectra.1 = (f32[1024,1024]{1,0:T(8,128)S(1)}, f32[1024,2048]{1,0:T(8,128)S(1)}, bf16[128,1024]{1,0:T(8,128)(2,1)S(1)}) custom-call(s32[1]{0:T(128)} %bitcast.device_ref, bf16[1024,512]{1,0:T(8,128)(2,1)S(1)} %copy-done, bf16[144,1024]{1,0:T(8,128)(2,1)S(1)} %get-tuple-element.44.refs_0_, bf16[144,1024]{1,0:T(8,128)(2,1)S(1)} %collective-permute-done.4.refs_1_, ...), custom_call_target="tpu_custom_call" | custom-call | flops 1048576 | bytes 65536 | tf_op jit(solution)/shard_map/spectra/pallas_call | solution.py:244
  42.1 3.2 %collective-permute-done.12.refs_6_ = bf16[2,128,1024]{2,1,0:T(8,128)(2,1)S(1)} collective-permute-done((bf16[2,128,1024]{2,1,0:T(8,128)(2,1)S(1)}, bf16[2,128,1024]{2,1,0:T(8,128)(2,1)S(1)}, u32[]{:S(2)}, u32[]{:S(2)}) %collective-permute-start.12) | collective-permute-done | bytes 524320 | tf_op jit(solution)/shard_map/ppermute | solution.py:365
  45.3 0.0 collective-permute-start.13
  45.3 1.9 %collective-permute-done.13.refs_7_ = bf16[2,128,1024]{2,1,0:T(8,128)(2,1)S(1)} collective-permute-done((bf16[2,128,1024]{2,1,0:T(8,128)(2,1)S(1)}, bf16[2,128,1024]{2,1,0:T(8,128)(2,1)S(1)}, u32[]{:S(2)}, u32[]{:S(2)}) %collective-permute-start.13) | collective-permute-done | bytes 524320 | tf_op jit(solution)/shard_map/ppermute | solution.py:360
  47.2 5.4 %convolve.1 = (bf16[128,1024]{1,0:T(8,128)(2,1)}, bf16[3,128,1024]{2,1,0:T(8,128)(2,1)}, f32[128,1024]{1,0:T(8,128)}) custom-call(s32[1]{0:T(128)} %bitcast.device_ref, bf16[1024,512]{1,0:T(8,128)(2,1)S(1)} %copy-done, bf16[128,1024]{1,0:T(8,128)(2,1)S(1)} %get-tuple-element.62.refs_1_, bf16[128,1024]{1,0:T(8,128)(2,1)S(1)} %copy-done.1, ...), custom_call_target="tpu_custom_call" | custom-call | flops 1048576 | bytes 65536 | tf_op jit(solution)/shard_map/convolve/pallas_call | solution.py:337
Async XLA Ops:
  0.6 9.9 %collective-permute-start = (bf16[128,1024]{1,0:T(8,128)(2,1)}, bf16[128,1024]{1,0:T(8,128)(2,1)S(1)}, u32[]{:S(2)}, u32[]{:S(2)}) collective-permute-start(bf16[128,1024]{1,0:T(8,128)(2,1)} %refs_0_.2), channel_id=1, source_target_pairs={{0,2},{2,4},{4,6},{6,7},{7,5},{5,3},{3,1},{1,0},{8,10},{10,12},{12... | collective-permute-start | bytes 786440 | tf_op jit(solution)/shard_map/ppermute | solution.py:388
  3.7 8.0 %collective-permute-start.1 = (bf16[128,1024]{1,0:T(8,128)(2,1)}, bf16[128,1024]{1,0:T(8,128)(2,1)S(1)}, u32[]{:S(2)}, u32[]{:S(2)}) collective-permute-start(bf16[128,1024]{1,0:T(8,128)(2,1)} %refs_0_.2), channel_id=1, source_target_pairs={{2,0},{4,2},{6,4},{7,6},{5,7},{3,5},{1,3},{0,1},{10,8},{12,10},{14... | collective-permute-start | bytes 786440 | tf_op jit(solution)/shard_map/ppermute | solution.py:390
  8.5 10.0 %collective-permute-start.4 = (bf16[144,1024]{1,0:T(8,128)(2,1)S(1)}, bf16[144,1024]{1,0:T(8,128)(2,1)S(1)}, u32[]{:S(2)}, u32[]{:S(2)}) collective-permute-start(bf16[144,1024]{1,0:T(8,128)(2,1)S(1)} %get-tuple-element.44.refs_0_), channel_id=1, source_target_pairs={{0,16},{8,24},{16,0},{24,8},{1,17},{9,25},{17,1},{25,9},{2,18},{10... | collective-permute-start | bytes 884744 | tf_op jit(solution)/shard_map/ppermute | solution.py:365
  11.7 6.9 %collective-permute-start.2 = (bf16[128,1024]{1,0:T(8,128)(2,1)S(1)}, bf16[128,1024]{1,0:T(8,128)(2,1)S(1)}, u32[]{:S(2)}, u32[]{:S(2)}) collective-permute-start(bf16[128,1024]{1,0:T(8,128)(2,1)S(1)} %collective-permute-done.refs_0_), channel_id=1, source_target_pairs={{0,2},{2,4},{4,6},{6,7},{7,5},{5,3},{3,1},{1,0},{8,10},{10,12},{12... | collective-permute-start | bytes 786440 | tf_op jit(solution)/shard_map/ppermute | solution.py:388
  13.3 6.6 %collective-permute-start.3 = (bf16[128,1024]{1,0:T(8,128)(2,1)S(1)}, bf16[128,1024]{1,0:T(8,128)(2,1)S(1)}, u32[]{:S(2)}, u32[]{:S(2)}) collective-permute-start(bf16[128,1024]{1,0:T(8,128)(2,1)S(1)} %collective-permute-done.1.refs_3_), channel_id=1, source_target_pairs={{2,0},{4,2},{6,4},{7,6},{5,7},{3,5},{1,3},{0,1},{10,8},{12,10},{14... | collective-permute-start | bytes 786440 | tf_op jit(solution)/shard_map/ppermute | solution.py:390
  19.8 6.9 %collective-permute-start.7 = (bf16[128,1024]{1,0:T(8,128)(2,1)S(1)}, bf16[128,1024]{1,0:T(8,128)(2,1)S(1)}, u32[]{:S(2)}, u32[]{:S(2)}) collective-permute-start(bf16[128,1024]{1,0:T(8,128)(2,1)S(1)} %collective-permute-done.2.refs_0_), channel_id=1, source_target_pairs={{0,2},{2,4},{4,6},{6,7},{7,5},{5,3},{3,1},{1,0},{8,10},{10,12},{12... | collective-permute-start | bytes 786440 | tf_op jit(solution)/shard_map/ppermute | solution.py:388
  21.4 6.4 %collective-permute-start.8 = (bf16[128,1024]{1,0:T(8,128)(2,1)S(1)}, bf16[128,1024]{1,0:T(8,128)(2,1)S(1)}, u32[]{:S(2)}, u32[]{:S(2)}) collective-permute-start(bf16[128,1024]{1,0:T(8,128)(2,1)S(1)} %collective-permute-done.3.refs_3_), channel_id=1, source_target_pairs={{2,0},{4,2},{6,4},{7,6},{5,7},{3,5},{1,3},{0,1},{10,8},{12,10},{14... | collective-permute-start | bytes 786440 | tf_op jit(solution)/shard_map/ppermute | solution.py:390
  27.8 6.4 %collective-permute-start.9 = (bf16[128,1024]{1,0:T(8,128)(2,1)S(1)}, bf16[128,1024]{1,0:T(8,128)(2,1)S(1)}, u32[]{:S(2)}, u32[]{:S(2)}) collective-permute-start(bf16[128,1024]{1,0:T(8,128)(2,1)S(1)} %collective-permute-done.7.refs_0_), channel_id=1, source_target_pairs={{0,2},{2,4},{4,6},{6,7},{7,5},{5,3},{3,1},{1,0},{8,10},{10,12},{12... | collective-permute-start | bytes 786440 | tf_op jit(solution)/shard_map/ppermute | solution.py:388
  29.3 4.9 %copy-start.1 = (bf16[128,1024]{1,0:T(8,128)(2,1)S(1)}, bf16[128,1024]{1,0:T(8,128)(2,1)}, u32[]{:S(2)}) copy-start(bf16[128,1024]{1,0:T(8,128)(2,1)} %refs_2_.3) | copy-start | bytes 786436
  34.2 5.5 %copy-start = (bf16[1024,512]{1,0:T(8,128)(2,1)S(1)}, bf16[1024,512]{1,0:T(8,128)(2,1)}, u32[]{:S(2)}) copy-start(bf16[1024,512]{1,0:T(8,128)(2,1)} %constant.12.clone.table_ref.refs_0_) | copy-start | bytes 3145732
  35.4 9.9 %collective-permute-start.12 = (bf16[2,128,1024]{2,1,0:T(8,128)(2,1)S(1)}, bf16[2,128,1024]{2,1,0:T(8,128)(2,1)S(1)}, u32[]{:S(2)}, u32[]{:S(2)}) collective-permute-start(bf16[2,128,1024]{2,1,0:T(8,128)(2,1)S(1)} %get-tuple-element.59.refs_4_), channel_id=1, source_target_pairs={{0,16},{8,24},{16,0},{24,8},{1,17},{9,25},{17,1},{25,9},{2,18},{10... | collective-permute-start | bytes 1572872 | tf_op jit(solution)/shard_map/ppermute | solution.py:365
  36.9 1.6 %collective-permute-start.5 = (bf16[144,1024]{1,0:T(8,128)(2,1)S(1)}, bf16[144,1024]{1,0:T(8,128)(2,1)S(1)}, u32[]{:S(2)}, u32[]{:S(2)}) collective-permute-start(bf16[144,1024]{1,0:T(8,128)(2,1)S(1)} %get-tuple-element.44.refs_0_), channel_id=1, source_target_pairs={{0,8},{8,0},{16,24},{24,16},{1,9},{9,1},{17,25},{25,17},{2,10},{10... | collective-permute-start | bytes 884744 | tf_op jit(solution)/shard_map/ppermute | solution.py:360
  36.9 2.0 %collective-permute-start.6 = (bf16[144,1024]{1,0:T(8,128)(2,1)S(1)}, bf16[144,1024]{1,0:T(8,128)(2,1)S(1)}, u32[]{:S(2)}, u32[]{:S(2)}) collective-permute-start(bf16[144,1024]{1,0:T(8,128)(2,1)S(1)} %collective-permute-done.4.refs_1_), channel_id=1, source_target_pairs={{0,8},{8,0},{16,24},{24,16},{1,9},{9,1},{17,25},{25,17},{2,10},{10... | collective-permute-start | bytes 884744 | tf_op jit(solution)/shard_map/ppermute | solution.py:360
  37.4 1.9 %collective-permute-start.10 = (bf16[2,128,512]{2,1,0:T(8,128)(2,1)S(1)}, bf16[2,128,512]{2,1,0:T(8,128)(2,1)S(1)}, u32[]{:S(2)}, u32[]{:S(2)}) collective-permute-start(bf16[2,128,512]{2,1,0:T(8,128)(2,1)S(1)} %get-tuple-element.60), channel_id=1, source_target_pairs={{0,8},{8,0},{16,24},{24,16},{1,9},{9,1},{17,25},{25,17},{2,10},{10... | collective-permute-start | bytes 786440 | tf_op jit(solution)/shard_map/ppermute | solution.py:360
  37.4 2.2 %collective-permute-start.11 = (bf16[2,128,512]{2,1,0:T(8,128)(2,1)S(1)}, bf16[2,128,512]{2,1,0:T(8,128)(2,1)S(1)}, u32[]{:S(2)}, u32[]{:S(2)}) collective-permute-start(bf16[2,128,512]{2,1,0:T(8,128)(2,1)S(1)} %get-tuple-element.61), channel_id=1, source_target_pairs={{0,8},{8,0},{16,24},{24,16},{1,9},{9,1},{17,25},{25,17},{2,10},{10... | collective-permute-start | bytes 786440 | tf_op jit(solution)/shard_map/ppermute | solution.py:360
  45.3 1.9 %collective-permute-start.13 = (bf16[2,128,1024]{2,1,0:T(8,128)(2,1)S(1)}, bf16[2,128,1024]{2,1,0:T(8,128)(2,1)S(1)}, u32[]{:S(2)}, u32[]{:S(2)}) collective-permute-start(bf16[2,128,1024]{2,1,0:T(8,128)(2,1)S(1)} %collective-permute-done.12.refs_6_), channel_id=1, source_target_pairs={{0,8},{8,0},{16,24},{24,16},{1,9},{9,1},{17,25},{25,17},{2,10},{10... | collective-permute-start | bytes 1572872 | tf_op jit(solution)/shard_map/ppermute | solution.py:360

commit v7 on v6

--- a/solution.py
+++ b/solution.py
@@ -284,38 +284,30 @@
         src_re, src_im = both[:bins, :tile], both[bins:, :tile]
         grad_re, grad_im = both[:bins, tile:], both[bins:, tile:]
         filt_re, filt_im = filt_ref[:bins, there], filt_ref[bins:, there]
-        real = [
-            src_re * filt_re - src_im * filt_im,
-            filt_re * grad_re + filt_im * grad_im,
-            src_re * grad_re + src_im * grad_im,
-        ]
-        imag = [
-            src_re * filt_im + src_im * filt_re,
-            filt_re * grad_im - filt_im * grad_re,
-            src_re * grad_im - src_im * grad_re,
-        ]
-        products = jnp.concatenate(
-            [
-                jnp.concatenate([re.astype(BF16), im.astype(BF16)], axis=0)
-                for re, im in zip(real, imag)
-            ],
-            axis=1,
+        number = start // tile
+
+        def back(real, imag):
+            products = jnp.concatenate([real.astype(BF16), imag.astype(BF16)], axis=0)
+            return dot(back_ref[...], products)
+
+        def send(source, target, output):
+            copies.append(pltpu.make_async_copy(source, target, sems.at[number, output]))
+            copies[-1].start()
+
+        conv_out = back(src_re * filt_re - src_im * filt_im, src_re * filt_im + src_im * filt_re)
+        gated[:, here] = (proj_ref[1, :, there].astype(F32) * conv_out).astype(BF16)
+        gproj[1, :, here] = (grad_ref[:, there].astype(F32) * conv_out).astype(BF16)
+        grad_source = back(
+            filt_re * grad_re + filt_im * grad_im, filt_re * grad_im - filt_im * grad_re
         )
-        result = dot(back_ref[...], products)
-        conv_out, grad_source = result[:, :tile], result[:, tile : 2 * tile]
-        gfilt[:, here] = result[:, 2 * tile :]
-        gated[:, here] = (proj_ref[1, :, there].astype(F32) * conv_out).astype(BF16)
         gproj[0, :, here] = (grad_source * proj_ref[2, :, there].astype(F32)).astype(BF16)
-        gproj[1, :, here] = (grad_ref[:, there].astype(F32) * conv_out).astype(BF16)
         gproj[2, :, here] = (grad_source * proj_ref[0, :, there].astype(F32)).astype(BF16)
-        number = start // tile
-        copies += [
-            pltpu.make_async_copy(gated.at[:, here], gated_out.at[:, there], sems.at[number, 0]),
-            pltpu.make_async_copy(gproj.at[:, :, here], gproj_out.at[:, :, there], sems.at[number, 1]),
-            pltpu.make_async_copy(gfilt.at[:, here], gfilt_out.at[:, there], sems.at[number, 2]),
-        ]
-        for copy in copies[-3:]:
-            copy.start()
+        send(gated.at[:, here], gated_out.at[:, there], 0)
+        send(gproj.at[:, :, here], gproj_out.at[:, :, there], 1)
+        gfilt[:, here] = back(
+            src_re * grad_re + src_im * grad_im, src_re * grad_im - src_im * grad_re
+        )
+        send(gfilt.at[:, here], gfilt_out.at[:, there], 2)
     for copy in copies:
         copy.wait()
 

time: 52.9 us -> 52.9 us (level)
  no operation moved by 1% of the time
where the time goes in v7:
time: 52.9 us; the launch traced here: 52.8 us
  Pallas kernels  28.3 us (53%)
  starting transfers between devices  13.2 us (25%)
  waiting for transfers between devices  10.3 us (19%)
  between operations  0.89 us (2%)
    pallas_call x4, Pallas kernels, add_blocks(): pl.pallas_call(functools.partial(blocks_kernel, chans, offsets, not own,...  19.3 us
    ppermute x4, starting transfers between devices, per_device(): next_up = lax.ppermute(up, 'chan', forward)  7.75 us
    pallas_call x1, Pallas kernels, convolve(): pl.pallas_call(functools.partial(conv_kernel, chans, groups, pieces, cut....  5.42 us
    ppermute x5, waiting for transfers between devices, to_other_core(): return lax.ppermute(value, 'seq', [(i, i ^ 1) for i in range(groups)])  3.64 us
    ppermute x2, starting transfers between devices, from_other_chips(): lax.ppermute(value, 'seq', [(i, (i + 2 * d) % groups) for i in range(grou...  3.54 us
    ppermute x3, waiting for transfers between devices, per_device(): next_down = lax.ppermute(down, 'chan', reverse)  3.48 us
    ppermute x2, waiting for transfers between devices, from_other_chips(): lax.ppermute(value, 'seq', [(i, (i + 2 * d) % groups) for i in range(grou...  3.18 us
    pallas_call x1, Pallas kernels, spectra(): pl.pallas_call(functools.partial(spectra_kernel, chans, len(taps)), in_sp...  2.42 us
  transfers between devices with their start and end apart: 14, of which 9 were waited for; matrix products, arithmetic and copies ran while one was open for 0% of the time, Pallas kernels for 41%

profile of v7, /device:TPU:0, one launch (start us, length us, event | category | flops | bytes accessed | tf_op | source)
XLA Modules:
  0.0 52.8 jit_solution(14678465170464430098)
XLA Ops:
  0.6 3.1 %collective-permute-start = (bf16[128,1024]{1,0:T(8,128)(2,1)}, bf16[128,1024]{1,0:T(8,128)(2,1)S(1)}, u32[]{:S(2)}, u32[]{:S(2)}) collective-permute-start(bf16[128,1024]{1,0:T(8,128)(2,1)} %refs_0_.2), channel_id=1, source_target_pairs={{0,2},{2,4},{4,6},{6,7},{7,5},{5,3},{3,1},{1,0},{8,10},{10,12},{12... | collective-permute-start | bytes 786440 | tf_op jit(solution)/shard_map/ppermute | solution.py:380
  3.7 0.0 collective-permute-start.1
  3.7 4.8 %add_blocks.4 = (f32[3,128,1024]{2,1,0:T(8,128)S(1)}, bf16[3,1024,1024]{2,1,0:T(8,128)(2,1)S(1)}, bf16[144,1024]{1,0:T(8,128)(2,1)S(1)}) custom-call(s32[1]{0:T(128)} %bitcast.device_ref, bf16[128,1024]{1,0:T(8,128)(2,1)} %refs_0_.2, bf16[3,8192,1024]{2,1,0:T(8,128)(2,1)} %bitcast.3, f32[128,1024]{1,0:T(8,128)} %refs_2_.2), custom_call_target="tpu_custom_call" | custom-call | flops 1610612736 | bytes 12582912 | tf_op jit(solution)/shard_map/add_blocks/pallas_call | solution.py:139
  8.5 2.0 %collective-permute-start.4 = (bf16[144,1024]{1,0:T(8,128)(2,1)S(1)}, bf16[144,1024]{1,0:T(8,128)(2,1)S(1)}, u32[]{:S(2)}, u32[]{:S(2)}) collective-permute-start(bf16[144,1024]{1,0:T(8,128)(2,1)S(1)} %get-tuple-element.44.refs_0_), channel_id=1, source_target_pairs={{0,16},{8,24},{16,0},{24,8},{1,17},{9,25},{17,1},{25,9},{2,18},{10... | collective-permute-start | bytes 884744 | tf_op jit(solution)/shard_map/ppermute | solution.py:357
  10.5 0.0 collective-permute-done.refs_0_
  10.5 1.2 %collective-permute-done.1.refs_3_ = bf16[128,1024]{1,0:T(8,128)(2,1)S(1)} collective-permute-done((bf16[128,1024]{1,0:T(8,128)(2,1)}, bf16[128,1024]{1,0:T(8,128)(2,1)S(1)}, u32[]{:S(2)}, u32[]{:S(2)}) %collective-permute-start.1) | collective-permute-done | bytes 262176 | tf_op jit(solution)/shard_map/ppermute | solution.py:382
  11.7 1.6 %collective-permute-start.2 = (bf16[128,1024]{1,0:T(8,128)(2,1)S(1)}, bf16[128,1024]{1,0:T(8,128)(2,1)S(1)}, u32[]{:S(2)}, u32[]{:S(2)}) collective-permute-start(bf16[128,1024]{1,0:T(8,128)(2,1)S(1)} %collective-permute-done.refs_0_), channel_id=1, source_target_pairs={{0,2},{2,4},{4,6},{6,7},{7,5},{5,3},{3,1},{1,0},{8,10},{10,12},{12... | collective-permute-start | bytes 786440 | tf_op jit(solution)/shard_map/ppermute | solution.py:380
  13.3 0.4 collective-permute-start.3
  13.7 4.8 %add_blocks.5 = (f32[3,128,1024]{2,1,0:T(8,128)S(1)}, bf16[3,1024,1024]{2,1,0:T(8,128)(2,1)S(1)}) custom-call(s32[1]{0:T(128)} %bitcast.device_ref, bf16[128,1024]{1,0:T(8,128)(2,1)S(1)} %collective-permute-done.refs_0_, bf16[3,1024,1024]{2,1,0:T(8,128)(2,1)S(1)} %get-tuple-element.40.refs_1_, ...), custom_call_target="tpu_custom_call", output_to_operand_aliasing={{0}: (3, {})} | custom-call | flops 1610612736 | bytes 12582912 | tf_op jit(solution)/shard_map/add_blocks/pallas_call | solution.py:139
  18.6 0.0 collective-permute-done.4.refs_1_
  18.6 0.0 collective-permute-done.2.refs_0_
  18.6 1.3 %collective-permute-done.3.refs_3_ = bf16[128,1024]{1,0:T(8,128)(2,1)S(1)} collective-permute-done((bf16[128,1024]{1,0:T(8,128)(2,1)S(1)}, bf16[128,1024]{1,0:T(8,128)(2,1)S(1)}, u32[]{:S(2)}, u32[]{:S(2)}) %collective-permute-start.3) | collective-permute-done | bytes 262176 | tf_op jit(solution)/shard_map/ppermute | solution.py:382
  19.8 1.6 %collective-permute-start.7 = (bf16[128,1024]{1,0:T(8,128)(2,1)S(1)}, bf16[128,1024]{1,0:T(8,128)(2,1)S(1)}, u32[]{:S(2)}, u32[]{:S(2)}) collective-permute-start(bf16[128,1024]{1,0:T(8,128)(2,1)S(1)} %collective-permute-done.2.refs_0_), channel_id=1, source_target_pairs={{0,2},{2,4},{4,6},{6,7},{7,5},{5,3},{3,1},{1,0},{8,10},{10,12},{12... | collective-permute-start | bytes 786440 | tf_op jit(solution)/shard_map/ppermute | solution.py:380
  21.4 0.4 collective-permute-start.8
  21.9 4.8 %add_blocks.6 = (f32[3,128,1024]{2,1,0:T(8,128)S(1)}, bf16[3,1024,1024]{2,1,0:T(8,128)(2,1)S(1)}) custom-call(s32[1]{0:T(128)} %bitcast.device_ref, bf16[128,1024]{1,0:T(8,128)(2,1)S(1)} %collective-permute-done.2.refs_0_, bf16[3,1024,1024]{2,1,0:T(8,128)(2,1)S(1)} %get-tuple-element.48.refs_1_, ...), custom_call_target="tpu_custom_call", output_to_operand_aliasing={{0}: (3, {})} | custom-call | flops 1610612736 | bytes 12582912 | tf_op jit(solution)/shard_map/add_blocks/pallas_call | solution.py:139
  26.7 0.0 collective-permute-done.7.refs_0_
  26.7 1.1 %collective-permute-done.8.refs_3_ = bf16[128,1024]{1,0:T(8,128)(2,1)S(1)} collective-permute-done((bf16[128,1024]{1,0:T(8,128)(2,1)S(1)}, bf16[128,1024]{1,0:T(8,128)(2,1)S(1)}, u32[]{:S(2)}, u32[]{:S(2)}) %collective-permute-start.8) | collective-permute-done | bytes 262176 | tf_op jit(solution)/shard_map/ppermute | solution.py:382
  27.8 1.5 %collective-permute-start.9 = (bf16[128,1024]{1,0:T(8,128)(2,1)S(1)}, bf16[128,1024]{1,0:T(8,128)(2,1)S(1)}, u32[]{:S(2)}, u32[]{:S(2)}) collective-permute-start(bf16[128,1024]{1,0:T(8,128)(2,1)S(1)} %collective-permute-done.7.refs_0_), channel_id=1, source_target_pairs={{0,2},{2,4},{4,6},{6,7},{7,5},{5,3},{3,1},{1,0},{8,10},{10,12},{12... | collective-permute-start | bytes 786440 | tf_op jit(solution)/shard_map/ppermute | solution.py:380
  29.3 0.0 copy-start.1
  29.3 4.9 %add_blocks.7 = (f32[3,128,1024]{2,1,0:T(8,128)S(1)}, bf16[3,1024,1024]{2,1,0:T(8,128)(2,1)S(1)}) custom-call(s32[1]{0:T(128)} %bitcast.device_ref, bf16[128,1024]{1,0:T(8,128)(2,1)S(1)} %collective-permute-done.7.refs_0_, bf16[3,1024,1024]{2,1,0:T(8,128)(2,1)S(1)} %get-tuple-element.52.refs_1_, ...), custom_call_target="tpu_custom_call", output_to_operand_aliasing={{0}: (3, {})} | custom-call | flops 1610612736 | bytes 12582912 | tf_op jit(solution)/shard_map/add_blocks/pallas_call | solution.py:139
  34.2 0.0 copy-start
  34.2 0.0 collective-permute-done.9.x_ref
  34.2 0.0 copy-done.1
  34.2 1.1 %last_block.1 = (bf16[3,128,1024]{2,1,0:T(8,128)(2,1)S(1)}, bf16[2,128,1024]{2,1,0:T(8,128)(2,1)S(1)}, bf16[2,128,512]{2,1,0:T(8,128)(2,1)S(1)}, bf16[2,128,512]{2,1,0:T(8,128)(2,1)S(1)}) custom-call(f32[3,128,1024]{2,1,0:T(8,128)S(1)} %get-tuple-element.56.total_ref, bf16[128,1024]{1,0:T(8,128)(2,1)S(1)} %copy-done.1, ...), custom_call_target="tpu_custom_call" | custom-call | flops 805306368 | bytes 1048576 | tf_op jit(solution)/shard_map/last_block/pallas_call | solution.py:174
  35.4 1.5 %collective-permute-start.12 = (bf16[2,128,1024]{2,1,0:T(8,128)(2,1)S(1)}, bf16[2,128,1024]{2,1,0:T(8,128)(2,1)S(1)}, u32[]{:S(2)}, u32[]{:S(2)}) collective-permute-start(bf16[2,128,1024]{2,1,0:T(8,128)(2,1)S(1)} %get-tuple-element.59.refs_4_), channel_id=1, source_target_pairs={{0,16},{8,24},{16,0},{24,8},{1,17},{9,25},{17,1},{25,9},{2,18},{10... | collective-permute-start | bytes 1572872 | tf_op jit(solution)/shard_map/ppermute | solution.py:357
  36.9 0.0 collective-permute-start.5
  36.9 0.5 collective-permute-start.6
  37.4 0.0 collective-permute-start.10
  37.4 0.5 collective-permute-start.11
  37.9 0.6 %collective-permute-done.5.refs_2_ = bf16[144,1024]{1,0:T(8,128)(2,1)S(1)} collective-permute-done((bf16[144,1024]{1,0:T(8,128)(2,1)S(1)}, bf16[144,1024]{1,0:T(8,128)(2,1)S(1)}, u32[]{:S(2)}, u32[]{:S(2)}) %collective-permute-start.5) | collective-permute-done | bytes 294944 | tf_op jit(solution)/shard_map/ppermute | solution.py:352
  38.5 0.4 collective-permute-done.6.refs_3_
  38.9 0.4 collective-permute-done.10.refs_5_
  39.3 0.4 collective-permute-done.11.refs_6_
  39.7 0.0 copy-done
  39.7 2.4 %spectra.1 = (f32[1024,1024]{1,0:T(8,128)S(1)}, f32[1024,2048]{1,0:T(8,128)S(1)}, bf16[128,1024]{1,0:T(8,128)(2,1)S(1)}) custom-call(s32[1]{0:T(128)} %bitcast.device_ref, bf16[1024,512]{1,0:T(8,128)(2,1)S(1)} %copy-done, bf16[144,1024]{1,0:T(8,128)(2,1)S(1)} %get-tuple-element.44.refs_0_, bf16[144,1024]{1,0:T(8,128)(2,1)S(1)} %collective-permute-done.4.refs_1_, ...), custom_call_target="tpu_custom_call" | custom-call | flops 1048576 | bytes 65536 | tf_op jit(solution)/shard_map/spectra/pallas_call | solution.py:244
  42.1 3.2 %collective-permute-done.12.refs_6_ = bf16[2,128,1024]{2,1,0:T(8,128)(2,1)S(1)} collective-permute-done((bf16[2,128,1024]{2,1,0:T(8,128)(2,1)S(1)}, bf16[2,128,1024]{2,1,0:T(8,128)(2,1)S(1)}, u32[]{:S(2)}, u32[]{:S(2)}) %collective-permute-start.12) | collective-permute-done | bytes 524320 | tf_op jit(solution)/shard_map/ppermute | solution.py:357
  45.3 0.0 collective-permute-start.13
  45.3 1.9 %collective-permute-done.13.refs_7_ = bf16[2,128,1024]{2,1,0:T(8,128)(2,1)S(1)} collective-permute-done((bf16[2,128,1024]{2,1,0:T(8,128)(2,1)S(1)}, bf16[2,128,1024]{2,1,0:T(8,128)(2,1)S(1)}, u32[]{:S(2)}, u32[]{:S(2)}) %collective-permute-start.13) | collective-permute-done | bytes 524320 | tf_op jit(solution)/shard_map/ppermute | solution.py:352
  47.2 5.4 %convolve.1 = (bf16[128,1024]{1,0:T(8,128)(2,1)}, bf16[3,128,1024]{2,1,0:T(8,128)(2,1)}, f32[128,1024]{1,0:T(8,128)}) custom-call(s32[1]{0:T(128)} %bitcast.device_ref, bf16[1024,512]{1,0:T(8,128)(2,1)S(1)} %copy-done, bf16[128,1024]{1,0:T(8,128)(2,1)S(1)} %get-tuple-element.62.refs_1_, bf16[128,1024]{1,0:T(8,128)(2,1)S(1)} %copy-done.1, ...), custom_call_target="tpu_custom_call" | custom-call | flops 1048576 | bytes 65536 | tf_op jit(solution)/shard_map/convolve/pallas_call | solution.py:329
Async XLA Ops:
  0.6 9.9 %collective-permute-start = (bf16[128,1024]{1,0:T(8,128)(2,1)}, bf16[128,1024]{1,0:T(8,128)(2,1)S(1)}, u32[]{:S(2)}, u32[]{:S(2)}) collective-permute-start(bf16[128,1024]{1,0:T(8,128)(2,1)} %refs_0_.2), channel_id=1, source_target_pairs={{0,2},{2,4},{4,6},{6,7},{7,5},{5,3},{3,1},{1,0},{8,10},{10,12},{12... | collective-permute-start | bytes 786440 | tf_op jit(solution)/shard_map/ppermute | solution.py:380
  3.7 8.0 %collective-permute-start.1 = (bf16[128,1024]{1,0:T(8,128)(2,1)}, bf16[128,1024]{1,0:T(8,128)(2,1)S(1)}, u32[]{:S(2)}, u32[]{:S(2)}) collective-permute-start(bf16[128,1024]{1,0:T(8,128)(2,1)} %refs_0_.2), channel_id=1, source_target_pairs={{2,0},{4,2},{6,4},{7,6},{5,7},{3,5},{1,3},{0,1},{10,8},{12,10},{14... | collective-permute-start | bytes 786440 | tf_op jit(solution)/shard_map/ppermute | solution.py:382
  8.5 10.0 %collective-permute-start.4 = (bf16[144,1024]{1,0:T(8,128)(2,1)S(1)}, bf16[144,1024]{1,0:T(8,128)(2,1)S(1)}, u32[]{:S(2)}, u32[]{:S(2)}) collective-permute-start(bf16[144,1024]{1,0:T(8,128)(2,1)S(1)} %get-tuple-element.44.refs_0_), channel_id=1, source_target_pairs={{0,16},{8,24},{16,0},{24,8},{1,17},{9,25},{17,1},{25,9},{2,18},{10... | collective-permute-start | bytes 884744 | tf_op jit(solution)/shard_map/ppermute | solution.py:357
  11.7 6.9 %collective-permute-start.2 = (bf16[128,1024]{1,0:T(8,128)(2,1)S(1)}, bf16[128,1024]{1,0:T(8,128)(2,1)S(1)}, u32[]{:S(2)}, u32[]{:S(2)}) collective-permute-start(bf16[128,1024]{1,0:T(8,128)(2,1)S(1)} %collective-permute-done.refs_0_), channel_id=1, source_target_pairs={{0,2},{2,4},{4,6},{6,7},{7,5},{5,3},{3,1},{1,0},{8,10},{10,12},{12... | collective-permute-start | bytes 786440 | tf_op jit(solution)/shard_map/ppermute | solution.py:380
  13.3 6.6 %collective-permute-start.3 = (bf16[128,1024]{1,0:T(8,128)(2,1)S(1)}, bf16[128,1024]{1,0:T(8,128)(2,1)S(1)}, u32[]{:S(2)}, u32[]{:S(2)}) collective-permute-start(bf16[128,1024]{1,0:T(8,128)(2,1)S(1)} %collective-permute-done.1.refs_3_), channel_id=1, source_target_pairs={{2,0},{4,2},{6,4},{7,6},{5,7},{3,5},{1,3},{0,1},{10,8},{12,10},{14... | collective-permute-start | bytes 786440 | tf_op jit(solution)/shard_map/ppermute | solution.py:382
  19.8 6.9 %collective-permute-start.7 = (bf16[128,1024]{1,0:T(8,128)(2,1)S(1)}, bf16[128,1024]{1,0:T(8,128)(2,1)S(1)}, u32[]{:S(2)}, u32[]{:S(2)}) collective-permute-start(bf16[128,1024]{1,0:T(8,128)(2,1)S(1)} %collective-permute-done.2.refs_0_), channel_id=1, source_target_pairs={{0,2},{2,4},{4,6},{6,7},{7,5},{5,3},{3,1},{1,0},{8,10},{10,12},{12... | collective-permute-start | bytes 786440 | tf_op jit(solution)/shard_map/ppermute | solution.py:380
  21.4 6.4 %collective-permute-start.8 = (bf16[128,1024]{1,0:T(8,128)(2,1)S(1)}, bf16[128,1024]{1,0:T(8,128)(2,1)S(1)}, u32[]{:S(2)}, u32[]{:S(2)}) collective-permute-start(bf16[128,1024]{1,0:T(8,128)(2,1)S(1)} %collective-permute-done.3.refs_3_), channel_id=1, source_target_pairs={{2,0},{4,2},{6,4},{7,6},{5,7},{3,5},{1,3},{0,1},{10,8},{12,10},{14... | collective-permute-start | bytes 786440 | tf_op jit(solution)/shard_map/ppermute | solution.py:382
  27.8 6.4 %collective-permute-start.9 = (bf16[128,1024]{1,0:T(8,128)(2,1)S(1)}, bf16[128,1024]{1,0:T(8,128)(2,1)S(1)}, u32[]{:S(2)}, u32[]{:S(2)}) collective-permute-start(bf16[128,1024]{1,0:T(8,128)(2,1)S(1)} %collective-permute-done.7.refs_0_), channel_id=1, source_target_pairs={{0,2},{2,4},{4,6},{6,7},{7,5},{5,3},{3,1},{1,0},{8,10},{10,12},{12... | collective-permute-start | bytes 786440 | tf_op jit(solution)/shard_map/ppermute | solution.py:380
  29.3 4.9 %copy-start.1 = (bf16[128,1024]{1,0:T(8,128)(2,1)S(1)}, bf16[128,1024]{1,0:T(8,128)(2,1)}, u32[]{:S(2)}) copy-start(bf16[128,1024]{1,0:T(8,128)(2,1)} %refs_2_.3) | copy-start | bytes 786436
  34.2 5.5 %copy-start = (bf16[1024,512]{1,0:T(8,128)(2,1)S(1)}, bf16[1024,512]{1,0:T(8,128)(2,1)}, u32[]{:S(2)}) copy-start(bf16[1024,512]{1,0:T(8,128)(2,1)} %constant.12.clone.table_ref.refs_0_) | copy-start | bytes 3145732
  35.4 9.9 %collective-permute-start.12 = (bf16[2,128,1024]{2,1,0:T(8,128)(2,1)S(1)}, bf16[2,128,1024]{2,1,0:T(8,128)(2,1)S(1)}, u32[]{:S(2)}, u32[]{:S(2)}) collective-permute-start(bf16[2,128,1024]{2,1,0:T(8,128)(2,1)S(1)} %get-tuple-element.59.refs_4_), channel_id=1, source_target_pairs={{0,16},{8,24},{16,0},{24,8},{1,17},{9,25},{17,1},{25,9},{2,18},{10... | collective-permute-start | bytes 1572872 | tf_op jit(solution)/shard_map/ppermute | solution.py:357
  36.9 1.6 %collective-permute-start.5 = (bf16[144,1024]{1,0:T(8,128)(2,1)S(1)}, bf16[144,1024]{1,0:T(8,128)(2,1)S(1)}, u32[]{:S(2)}, u32[]{:S(2)}) collective-permute-start(bf16[144,1024]{1,0:T(8,128)(2,1)S(1)} %get-tuple-element.44.refs_0_), channel_id=1, source_target_pairs={{0,8},{8,0},{16,24},{24,16},{1,9},{9,1},{17,25},{25,17},{2,10},{10... | collective-permute-start | bytes 884744 | tf_op jit(solution)/shard_map/ppermute | solution.py:352
  36.9 2.0 %collective-permute-start.6 = (bf16[144,1024]{1,0:T(8,128)(2,1)S(1)}, bf16[144,1024]{1,0:T(8,128)(2,1)S(1)}, u32[]{:S(2)}, u32[]{:S(2)}) collective-permute-start(bf16[144,1024]{1,0:T(8,128)(2,1)S(1)} %collective-permute-done.4.refs_1_), channel_id=1, source_target_pairs={{0,8},{8,0},{16,24},{24,16},{1,9},{9,1},{17,25},{25,17},{2,10},{10... | collective-permute-start | bytes 884744 | tf_op jit(solution)/shard_map/ppermute | solution.py:352
  37.4 1.9 %collective-permute-start.10 = (bf16[2,128,512]{2,1,0:T(8,128)(2,1)S(1)}, bf16[2,128,512]{2,1,0:T(8,128)(2,1)S(1)}, u32[]{:S(2)}, u32[]{:S(2)}) collective-permute-start(bf16[2,128,512]{2,1,0:T(8,128)(2,1)S(1)} %get-tuple-element.60), channel_id=1, source_target_pairs={{0,8},{8,0},{16,24},{24,16},{1,9},{9,1},{17,25},{25,17},{2,10},{10... | collective-permute-start | bytes 786440 | tf_op jit(solution)/shard_map/ppermute | solution.py:352
  37.4 2.2 %collective-permute-start.11 = (bf16[2,128,512]{2,1,0:T(8,128)(2,1)S(1)}, bf16[2,128,512]{2,1,0:T(8,128)(2,1)S(1)}, u32[]{:S(2)}, u32[]{:S(2)}) collective-permute-start(bf16[2,128,512]{2,1,0:T(8,128)(2,1)S(1)} %get-tuple-element.61), channel_id=1, source_target_pairs={{0,8},{8,0},{16,24},{24,16},{1,9},{9,1},{17,25},{25,17},{2,10},{10... | collective-permute-start | bytes 786440 | tf_op jit(solution)/shard_map/ppermute | solution.py:352
  45.3 1.9 %collective-permute-start.13 = (bf16[2,128,1024]{2,1,0:T(8,128)(2,1)S(1)}, bf16[2,128,1024]{2,1,0:T(8,128)(2,1)S(1)}, u32[]{:S(2)}, u32[]{:S(2)}) collective-permute-start(bf16[2,128,1024]{2,1,0:T(8,128)(2,1)S(1)} %collective-permute-done.12.refs_6_), channel_id=1, source_target_pairs={{0,8},{8,0},{16,24},{24,16},{1,9},{9,1},{17,25},{25,17},{2,10},{10... | collective-permute-start | bytes 1572872 | tf_op jit(solution)/shard_map/ppermute | solution.py:352
